TPU v7x, 32 devices: a whole 2x2x4 slice. The times are simulated.
32 devices in a mesh: pipe: 4 (over z), expert: 8 (over y, x, core).
Axes of the slice: x: 2, y: 2, z: 4, core: 2. Of those that a mesh axis runs over, the one named last changes fastest.
Arguments:
- enc_states: bfloat16 [32, 512], P('pipe'), may hold values from -6 to 6
- key_weight: bfloat16 [512, 512], P(None, 'expert'), may hold values from -0.25 to 0.25
- value_weight: bfloat16 [512, 512], P(None, 'expert'), may hold values from -0.25 to 0.25
- queries: bfloat16 [4096, 512], P('pipe', 'expert'), may hold values from -240 to 240
- lengths: int32 [4096], P('pipe'), may hold values from 1 to 32
- context_grad: bfloat16 [4096, 512], P('pipe', 'expert'), may hold values from -6 to 6
- residual: bfloat16 [4096, 512], P(('pipe', 'expert')), may hold values from -6 to 6
- norm_gain: bfloat16 [512], replicated, may hold values from 0.5 to 1.5
- routes: int32 [4096, 1], P(('pipe', 'expert')), may hold values from 0 to 7
- w_in: bfloat16 [8, 512, 1280], P('expert', None, 'pipe'), may hold values from -0.25 to 0.25
- w_out: bfloat16 [8, 1280, 512], P('expert', 'pipe'), may hold values from -0.15625 to 0.15625
Outputs:
- layer_out: bfloat16 [4096, 512], P(('pipe', 'expert'))
- enc_grad: bfloat16 [32, 512], P('pipe')
All inputs are finite; a program needn't handle non-finite values.
Results may differ from a plain program's by a relative error of at most 0.013.
The roundings to bfloat16 on the way count: a program that leaves them out, or rounds other values in their place, can miss the bound.
Values may be sent and summed in bfloat16 or wider, within the bound.
No kernel may reach another device: no remote copies, remote signals or barrier semaphores. Data moves between devices by JAX's collectives and lax.ppermute only.
A program may use at most 64 MiB of HBM per device.

v0:
```python
import math

import jax
import jax.numpy as jnp
from jax import lax
from jax.sharding import PartitionSpec as P


def per_device(
    enc_states,
    key_weight,
    value_weight,
    queries,
    lengths,
    context_grad,
    residual,
    norm_gain,
    routes,
    w_in,
    w_out,
):
    head = key_weight.shape[1]
    tok_dev = residual.shape[0]
    model = residual.shape[1]
    experts = lax.axis_size("expert")
    cap = tok_dev // (2 * experts)
    scale = 1.0 / math.sqrt(head)
    keys_local = jnp.dot(enc_states, key_weight, preferred_element_type=jnp.float32).astype(
        jnp.bfloat16
    )
    values_local = jnp.dot(enc_states, value_weight, preferred_element_type=jnp.float32).astype(
        jnp.bfloat16
    )
    keys, values = (
        lax.all_gather(keys_local, "pipe", axis=0, tiled=True),
        lax.all_gather(values_local, "pipe", axis=0, tiled=True),
    )
    scores = (
        lax.dot_general(queries, keys, (((1,), (1,)), ((), ())), preferred_element_type=jnp.float32)
        * scale
    )
    visible = jnp.arange(keys.shape[0], dtype=jnp.int32)[None, :] < lengths[:, None]
    scores = jnp.where(visible, scores, -1e30)
    highest = jnp.max(scores, axis=1, keepdims=True)
    weights = jnp.where(visible, jnp.exp(scores - highest), 0.0)
    probs = weights / jnp.sum(weights, axis=1, keepdims=True)
    probs_low = probs.astype(jnp.bfloat16)
    context = jnp.dot(probs_low, values, preferred_element_type=jnp.float32).astype(jnp.bfloat16)
    gathered_rows = lax.all_to_all(context, "expert", split_axis=0, concat_axis=1, tiled=True)
    hidden_state = residual.astype(jnp.float32) + gathered_rows.astype(jnp.float32)
    power = jnp.mean(hidden_state * hidden_state, axis=1, keepdims=True)
    normed = (hidden_state * lax.rsqrt(power + 1e-06) * norm_gain.astype(jnp.float32)).astype(
        jnp.bfloat16
    )
    expert_ids = routes[:, 0]
    onehot = (expert_ids[:, None] == jnp.arange(experts, dtype=jnp.int32)[None, :]).astype(
        jnp.int32
    )
    slot_rank = jnp.sum((jnp.cumsum(onehot, axis=0) - onehot) * onehot, axis=1)
    target = jnp.where(slot_rank < cap, expert_ids * cap + slot_rank, -1)
    placing = (jnp.arange(experts * cap, dtype=jnp.int32)[:, None] == target[None, :]).astype(
        jnp.bfloat16
    )
    outgoing = jnp.dot(placing, normed, preferred_element_type=jnp.float32).astype(jnp.bfloat16)
    outgoing = outgoing.reshape(experts, cap, model)
    w_first = w_in[0]
    w_second = w_out[0]
    arrived = lax.all_to_all(outgoing, "expert", split_axis=0, concat_axis=0, tiled=True)
    active = jnp.maximum(
        jnp.dot(
            lax.all_gather(arrived.reshape(experts * cap, model), "pipe", axis=0, tiled=True),
            w_first,
            preferred_element_type=jnp.float32,
        ),
        0.0,
    ).astype(jnp.bfloat16)
    partial_value = jnp.dot(active, w_second, preferred_element_type=jnp.float32)
    summed = (
        lax.psum_scatter(
            partial_value.astype(jnp.bfloat16), "pipe", scatter_dimension=0, tiled=True
        )
        .astype(jnp.float32)
        .reshape(experts, cap, model)
    )
    returned = lax.all_to_all(
        summed.astype(jnp.bfloat16), "expert", split_axis=0, concat_axis=0, tiled=True
    )
    expert_out = lax.dot_general(
        placing,
        returned.reshape(experts * cap, model),
        (((0,), (0,)), ((), ())),
        preferred_element_type=jnp.float32,
    )
    layer_out = (hidden_state + expert_out).astype(jnp.bfloat16)
    grad_values = lax.dot_general(
        probs_low, context_grad, (((0,), (0,)), ((), ())), preferred_element_type=jnp.float32
    )
    grad_probs = lax.dot_general(
        context_grad, values, (((1,), (1,)), ((), ())), preferred_element_type=jnp.float32
    )
    row_delta = jnp.sum(probs * grad_probs, axis=1, keepdims=True)
    grad_scores = (probs * (grad_probs - row_delta) * scale).astype(jnp.bfloat16)
    grad_keys = lax.dot_general(
        grad_scores, queries, (((0,), (0,)), ((), ())), preferred_element_type=jnp.float32
    )
    keys_total, values_total = lax.psum((grad_keys, grad_values), "pipe")
    enc_dev = enc_states.shape[0]
    first_row = lax.axis_index("pipe") * enc_dev
    own_keys = lax.dynamic_slice_in_dim(keys_total, first_row, enc_dev, 0)
    own_values = lax.dynamic_slice_in_dim(values_total, first_row, enc_dev, 0)
    enc_part = lax.dot_general(
        own_keys.astype(jnp.bfloat16),
        key_weight,
        (((1,), (1,)), ((), ())),
        preferred_element_type=jnp.float32,
    )
    enc_part = enc_part + lax.dot_general(
        own_values.astype(jnp.bfloat16),
        value_weight,
        (((1,), (1,)), ((), ())),
        preferred_element_type=jnp.float32,
    )
    enc_grad = lax.psum(enc_part, "expert").astype(jnp.bfloat16)
    return (layer_out, enc_grad)


def solution(mesh):
    placed = (
        P("pipe", None),
        P(None, "expert"),
        P(None, "expert"),
        P("pipe", "expert"),
        P("pipe"),
        P("pipe", "expert"),
        P(("pipe", "expert"), None),
        P(),
        P(("pipe", "expert"), None),
        P("expert", None, "pipe"),
        P("expert", "pipe", None),
    )
    return jax.shard_map(
        per_device,
        mesh=mesh,
        in_specs=placed,
        out_specs=(P(("pipe", "expert"), None), P("pipe", None)),
        check_vma=False,
    )
```

profile of v0, /device:TPU:0, one launch (start us, length us, event | category | flops | bytes accessed | tf_op | source)
XLA Modules:
  0.0 125.6 jit_solution(10576054242835351895)
XLA Ops:
  7.2 0.0 copy-start
  7.2 0.0 copy-start.5
  7.2 0.0 copy-start.2
  7.2 1.0 convolution_convert_fusion.3
  8.2 0.0 copy-done.5
  8.2 0.0 copy-done.2
  8.2 0.1 convolution_convert_fusion.4
  8.4 13.6 %all_gather.10 = bf16[32,64]{1,0:T(8,128)(2,1)S(1)} all-gather(bf16[8,64]{1,0:T(8,128)(2,1)S(1)} %convolution_convert_fusion.3), channel_id=1, replica_groups=mesh['pipe'=4,'expert'=8] {'pipe'}, dimensions={0}, use_global_device_ids=true | all-gather | bytes 5120 | tf_op jit(solution)/shard_map/all_gather | solution.py:36
  21.9 12.0 %all_gather.9 = bf16[32,64]{1,0:T(8,128)(2,1)S(1)} all-gather(bf16[8,64]{1,0:T(8,128)(2,1)S(1)} %convolution_convert_fusion.4), channel_id=1, replica_groups=mesh['pipe'=4,'expert'=8] {'pipe'}, dimensions={0}, use_global_device_ids=true | all-gather | bytes 5120 | tf_op jit(solution)/shard_map/all_gather | solution.py:35
  33.9 0.0 copy-done.6
  33.9 1.1 fusion.32
  35.0 0.2 fusion.4
  35.3 0.7 copy.18
  35.9 3.9 %all-to-all-start = ((bf16[8,128,64]{1,2,0:T(8,128)(2,1)}), bf16[8,128,64]{1,2,0:T(8,128)(2,1)S(1)}, u32[]{:S(2)}, u32[]{:S(2)}) async-start(bf16[8,128,64]{1,2,0:T(8,128)(2,1)} %bitcast.43), calls=%async_computation | async-start | bytes 262144 | tf_op jit(solution)/shard_map/all_to_all | solution.py:49
  39.8 0.0 copy-done.8
  39.8 0.0 copy-start.7
  39.8 0.6 copy-done.7
  40.5 0.1 fusion.18
  40.6 0.2 reduce_window_sum.11
  40.7 0.2 select_reduce_fusion
  40.9 4.4 %all-to-all-done = bf16[8,128,64]{1,2,0:T(8,128)(2,1)S(1)} async-done(((bf16[8,128,64]{1,2,0:T(8,128)(2,1)}), bf16[8,128,64]{1,2,0:T(8,128)(2,1)S(1)}, u32[]{:S(2)}, u32[]{:S(2)}) %all-to-all-start) | async-done | bytes 131104 | tf_op jit(solution)/shard_map/all_to_all | solution.py:49
  45.4 0.0 copy-start.1
  45.4 0.1 copy.15
  45.5 0.8 copy-done.1
  46.3 0.1 multiply_reduce_fusion
  46.4 0.9 fusion.5
  47.3 3.5 %all-to-all-start.1 = ((bf16[8,8,512]{2,1,0:T(8,128)(2,1)}), bf16[8,8,512]{2,1,0:T(8,128)(2,1)S(1)}, u32[]{:S(2)}, u32[]{:S(2)}) async-start(bf16[8,8,512]{2,1,0:T(8,128)(2,1)} %fusion.5), calls=%async_computation.1 | async-start | bytes 131072 | tf_op jit(solution)/shard_map/all_to_all | solution.py:68
  50.8 0.0 reduce-scatter.2.cloned.1.call-start
  50.8 0.0 copy-done.10
  50.8 0.2 multiply_reduce_fusion.1
  51.0 0.0 copy-start.9
  51.0 4.7 %all-to-all-done.1 = bf16[8,8,512]{2,1,0:T(8,128)(2,1)S(1)} async-done(((bf16[8,8,512]{2,1,0:T(8,128)(2,1)}), bf16[8,8,512]{2,1,0:T(8,128)(2,1)S(1)}, u32[]{:S(2)}, u32[]{:S(2)}) %all-to-all-start.1) | async-done | bytes 65568 | tf_op jit(solution)/shard_map/all_to_all | solution.py:68
  55.7 14.3 %all_gather.11 = bf16[256,512]{1,0:T(8,128)(2,1)S(1)} all-gather(bf16[64,512]{1,0:T(8,128)(2,1)S(1)} %bitcast.45), channel_id=1, replica_groups=mesh['pipe'=4,'expert'=8] {'pipe'}, dimensions={0}, use_global_device_ids=true | all-gather | bytes 327680 | tf_op jit(solution)/shard_map/all_gather | solution.py:71
  70.0 0.0 copy-done
  70.0 0.0 copy-done.9
  70.0 1.3 convolution_convert_fusion
  71.3 0.0 reduce-scatter.2.cloned.1.call-update
  71.3 0.0 copy-start.4
  71.3 0.2 fusion.19
  71.5 0.7 copy-done.4
  72.2 0.2 fusion.14
  72.4 16.4 %all-reduce = (bf16[32,64]{1,0:T(8,128)(2,1)S(1)}, bf16[32,64]{1,0:T(8,128)(2,1)S(1)}) all-reduce(f32[32,64]{1,0:T(8,128)S(1)} %fusion.14, f32[32,64]{1,0:T(8,128)S(1)} %fusion.19), channel_id=1, replica_groups=mesh['pipe'=4,'expert'=8] {'pipe'}, use_global_device_ids=true, to_apply=%region_7.8 | all-reduce | flops 4096 | bytes 24576 | tf_op jit(solution)/shard_map/psum | solution.py:106
  88.8 0.1 fusion.24
  88.9 3.5 %all-to-all-start.2 = ((bf16[8,8,512]{2,1,0:T(8,128)(2,1)}), bf16[8,8,512]{2,1,0:T(8,128)(2,1)S(1)}, u32[]{:S(2)}, u32[]{:S(2)}) async-start(bf16[8,8,512]{2,1,0:T(8,128)(2,1)} %bitcast.46), calls=%async_computation.3 | async-start | bytes 131072 | tf_op jit(solution)/shard_map/all_to_all | solution.py:85
  92.4 0.1 convolution_add_fusion.1
  92.6 25.3 %psum.23 = bf16[8,512]{1,0:T(8,128)(2,1)} all-reduce(f32[8,512]{1,0:T(8,128)S(1)} %convolution_add_fusion.1), channel_id=1, replica_groups=mesh['pipe'=4,'expert'=8] {'expert'}, use_global_device_ids=true, to_apply=%region_9.10 | all-reduce | flops 4096 | bytes 24576 | tf_op jit(solution)/shard_map/psum | solution.py:123
  117.9 0.0 all-to-all-done.2
  117.9 0.9 fusion.1
  (11 shorter events, 0.1 us)
Async XLA Ops:
  7.2 62.9 %copy-start = (bf16[1,320,512]{2,1,0:T(8,128)(2,1)S(1)}, bf16[1,320,512]{2,1,0:T(8,128)(2,1)}, u32[]{:S(2)}) copy-start(bf16[1,320,512]{2,1,0:T(8,128)(2,1)} %param.21) | copy-start | bytes 983044
  7.2 1.0 copy-start.5
  7.2 1.0 copy-start.2
  21.9 12.0 %copy-start.6 = (s32[1024]{0:T(1024)S(1)}, s32[1024]{0:T(1024)}, u32[]{:S(2)}) copy-start(s32[1024]{0:T(1024)} %param.15) | copy-start | bytes 12292
  35.9 3.9 %copy-start.8 = (bf16[512]{0:T(512)(128)(2,1)S(1)}, bf16[512]{0:T(512)(128)(2,1)}, u32[]{:S(2)}) copy-start(bf16[512]{0:T(512)(128)(2,1)} %param.18) | copy-start | bytes 3076
  35.9 9.4 %all-to-all-start = ((bf16[8,128,64]{1,2,0:T(8,128)(2,1)}), bf16[8,128,64]{1,2,0:T(8,128)(2,1)S(1)}, u32[]{:S(2)}, u32[]{:S(2)}) async-start(bf16[8,128,64]{1,2,0:T(8,128)(2,1)} %bitcast.43), calls=%async_computation | async-start | bytes 262144 | tf_op jit(solution)/shard_map/all_to_all | solution.py:49
  39.8 0.7 copy-start.7
  45.4 0.9 copy-start.1
  47.3 3.5 %copy-start.10 = (bf16[1024,64]{0,1:T(8,128)(2,1)S(1)}, bf16[1024,64]{0,1:T(8,128)(2,1)}, u32[]{:S(2)}) copy-start(bf16[1024,64]{0,1:T(8,128)(2,1)} %param.16) | copy-start | bytes 393220
  47.3 8.4 %all-to-all-start.1 = ((bf16[8,8,512]{2,1,0:T(8,128)(2,1)}), bf16[8,8,512]{2,1,0:T(8,128)(2,1)S(1)}, u32[]{:S(2)}, u32[]{:S(2)}) async-start(bf16[8,8,512]{2,1,0:T(8,128)(2,1)} %fusion.5), calls=%async_computation.1 | async-start | bytes 131072 | tf_op jit(solution)/shard_map/all_to_all | solution.py:68
  50.8 38.2 %reduce-scatter.2.cloned.1.call-start = ((), (), s32[]{:S(2)}) async-start(), calls=%async_computation.4 | async-start | bytes 327680 | tf_op jit(solution)/shard_map/reduce_scatter | solution.py:79
  51.0 19.0 %copy-start.9 = (bf16[1,512,320]{1,2,0:T(8,128)(2,1)S(1)}, bf16[1,512,320]{1,2,0:T(8,128)(2,1)}, u32[]{:S(2)}) copy-start(bf16[1,512,320]{1,2,0:T(8,128)(2,1)} %param.20) | copy-start | bytes 983044
  71.3 0.9 copy-start.4
  88.9 3.5 %copy-start.3 = (bf16[512,64]{0,1:T(8,128)(2,1)S(1)}, bf16[512,64]{0,1:T(8,128)(2,1)}, u32[]{:S(2)}) copy-start(bf16[512,64]{0,1:T(8,128)(2,1)} %param.13) | copy-start | bytes 196612
  88.9 29.0 %all-to-all-start.2 = ((bf16[8,8,512]{2,1,0:T(8,128)(2,1)}), bf16[8,8,512]{2,1,0:T(8,128)(2,1)S(1)}, u32[]{:S(2)}, u32[]{:S(2)}) async-start(bf16[8,8,512]{2,1,0:T(8,128)(2,1)} %bitcast.46), calls=%async_computation.3 | async-start | bytes 131072 | tf_op jit(solution)/shard_map/all_to_all | solution.py:85
Sparse Core Ops, SparseCore 0:
  71.4 16.3 reduce-scatter.1
where the time goes:
time: 126 us
  blocking collectives  81.6 us (65%)
  between operations  14.2 us (11%)
  starting transfers between devices  10.9 us (9%)
  waiting for transfers between devices  9.13 us (7%)
  matrix products  6.19 us (5%)
  local copies, waits for them, and re-layouts  3 us (2%)
    psum x1, blocking collectives, per_device(): enc_grad = lax.psum(enc_part, 'expert').astype(jnp.bfloat16)  25.3 us
    psum x1, blocking collectives, per_device(): keys_total, values_total = lax.psum((grad_keys, grad_values), 'pipe')  16.4 us
    all_gather x1, blocking collectives, per_device(): lax.all_gather(arrived.reshape(experts * cap, model), 'pipe', axis=0, til...  14.3 us
    all_gather x1, blocking collectives, per_device(): lax.all_gather(values_local, 'pipe', axis=0, tiled=True)  13.6 us
    all_gather x1, blocking collectives, per_device(): lax.all_gather(keys_local, 'pipe', axis=0, tiled=True)  12 us
    all_to_all x1, waiting for transfers between devices, per_device(): lax.all_to_all(outgoing, 'expert', split_axis=0, concat_axis=0, tiled=True)  4.71 us
    all_to_all x1, waiting for transfers between devices, per_device(): lax.all_to_all(context, 'expert', split_axis=0, concat_axis=1, tiled=True)  4.41 us
    all_to_all x1, starting transfers between devices, per_device(): lax.all_to_all(context, 'expert', split_axis=0, concat_axis=1, tiled=True)  3.86 us
  transfers between devices with their start and end apart: 4, of which 2 were waited for; matrix products, arithmetic and copies ran while one was open for 1% of the time, Pallas kernels for 0%

commit v1 on v0

v1 whole, which is shorter than its diff:
```python
import math

import jax
import jax.numpy as jnp
from jax import lax
from jax.sharding import PartitionSpec as P


def shifted(value, axis, step):
    size = lax.axis_size(axis)
    return lax.ppermute(value, axis, [(i, (i + step) % size) for i in range(size)])


def per_device(
    enc_states,
    key_weight,
    value_weight,
    queries,
    lengths,
    context_grad,
    residual,
    norm_gain,
    routes,
    w_in,
    w_out,
):
    enc_dev = enc_states.shape[0]
    head = key_weight.shape[1]
    tok_dev = residual.shape[0]
    model = residual.shape[1]
    experts = lax.axis_size("expert")
    pipes = lax.axis_size("pipe")
    everyone = ("pipe", "expert")
    cap = tok_dev // (2 * experts)
    scale = 1.0 / math.sqrt(head)
    f32, bf16 = jnp.float32, jnp.bfloat16
    both_weights = jnp.concatenate([key_weight, value_weight], axis=1)
    own_kv = jnp.dot(enc_states, both_weights, preferred_element_type=f32).astype(bf16)
    blocks = [own_kv] + [shifted(own_kv, "pipe", s) for s in range(1, pipes)]
    kv = jnp.concatenate(blocks, axis=0)
    keys, values = kv[:, :head], kv[:, head:]
    owner = lax.rem(lax.axis_index("pipe") + pipes - jnp.arange(pipes, dtype=jnp.int32), pipes)
    position = (owner[:, None] * enc_dev + jnp.arange(enc_dev, dtype=jnp.int32)[None, :]).reshape(-1)
    scores = (
        lax.dot_general(keys, queries, (((1,), (1,)), ((), ())), preferred_element_type=f32) * scale
    )
    visible = position[:, None] < lengths[None, :]
    scores = jnp.where(visible, scores, -1e30)
    highest = jnp.max(scores, axis=0, keepdims=True)
    weights = jnp.where(visible, jnp.exp(scores - highest), 0.0)
    probs = weights / jnp.sum(weights, axis=0, keepdims=True)
    probs_low = probs.astype(bf16)
    context = lax.dot_general(
        values, probs_low, (((0,), (0,)), ((), ())), preferred_element_type=f32
    ).astype(bf16)
    context_blocks = context.reshape(head, experts, tok_dev).transpose(1, 0, 2)
    gathered = lax.all_to_all(context_blocks, "expert", split_axis=0, concat_axis=0, tiled=True)
    hidden_state = residual.astype(f32) + gathered.reshape(model, tok_dev).T.astype(f32)
    power = jnp.mean(hidden_state * hidden_state, axis=1, keepdims=True)
    normed = (hidden_state * lax.rsqrt(power + 1e-06) * norm_gain.astype(f32)).astype(bf16)
    expert_ids = routes[:, 0]
    onehot = (expert_ids[:, None] == jnp.arange(experts, dtype=jnp.int32)[None, :]).astype(
        jnp.int32
    )
    slot_rank = jnp.sum((jnp.cumsum(onehot, axis=0) - onehot) * onehot, axis=1)
    target = jnp.where(slot_rank < cap, expert_ids * cap + slot_rank, -1)
    placing = (jnp.arange(experts * cap, dtype=jnp.int32)[:, None] == target[None, :]).astype(bf16)
    outgoing = jnp.dot(placing, normed, preferred_element_type=f32).astype(bf16)
    outgoing = jnp.broadcast_to(
        outgoing.reshape(1, experts, cap, model), (pipes, experts, cap, model)
    ).reshape(pipes * experts, cap, model)
    arrived = lax.all_to_all(outgoing, everyone, split_axis=0, concat_axis=0, tiled=True)
    active = jnp.maximum(
        jnp.dot(
            arrived.reshape(pipes * experts * cap, model), w_in[0], preferred_element_type=f32
        ),
        0.0,
    ).astype(bf16)
    part = jnp.dot(active, w_out[0], preferred_element_type=f32).astype(bf16)
    returned = lax.all_to_all(
        part.reshape(pipes * experts, cap, model),
        everyone,
        split_axis=0,
        concat_axis=0,
        tiled=True,
    ).reshape(pipes, experts * cap, model)
    expert_rows = jnp.sum(returned.astype(f32), axis=0).astype(bf16)
    expert_out = lax.dot_general(
        placing, expert_rows, (((0,), (0,)), ((), ())), preferred_element_type=f32
    )
    layer_out = (hidden_state + expert_out).astype(bf16)

    grad_values = jnp.dot(probs_low, context_grad, preferred_element_type=f32)
    grad_probs = lax.dot_general(
        values, context_grad, (((1,), (1,)), ((), ())), preferred_element_type=f32
    )
    row_delta = jnp.sum(probs * grad_probs, axis=0, keepdims=True)
    grad_scores = (probs * (grad_probs - row_delta) * scale).astype(bf16)
    grad_keys = jnp.dot(grad_scores, queries, preferred_element_type=f32)
    grads = jnp.concatenate([grad_keys, grad_values], axis=1)
    total = grads[:enc_dev]
    for s in range(1, pipes):
        total = total + shifted(grads[s * enc_dev : (s + 1) * enc_dev], "pipe", -s)
    enc_part = lax.dot_general(
        total.astype(bf16), both_weights, (((1,), (1,)), ((), ())), preferred_element_type=f32
    )
    parts = lax.all_to_all(
        jnp.broadcast_to(enc_part[None], (experts, enc_dev, model)),
        "expert",
        split_axis=0,
        concat_axis=0,
        tiled=True,
    )
    enc_grad = jnp.sum(parts, axis=0).astype(bf16)
    return (layer_out, enc_grad)


def solution(mesh):
    placed = (
        P("pipe", None),
        P(None, "expert"),
        P(None, "expert"),
        P("pipe", "expert"),
        P("pipe"),
        P("pipe", "expert"),
        P(("pipe", "expert"), None),
        P(),
        P(("pipe", "expert"), None),
        P("expert", None, "pipe"),
        P("expert", "pipe", None),
    )
    return jax.shard_map(
        per_device,
        mesh=mesh,
        in_specs=placed,
        out_specs=(P(("pipe", "expert"), None), P("pipe", None)),
        check_vma=False,
    )
```

time: 126 us -> 63.1 us (0.50)
  blocking collectives: 81.6 us -> 0 us
  waiting for transfers between devices: 9.13 us -> 27.1 us
  between operations: 14.2 us -> 0.81 us
  starting transfers between devices: 10.9 us -> 23.2 us
  local copies, waits for them, and re-layouts: 3 us -> 5.91 us
  matrix products: 6.19 us -> 3.97 us
    psum x2 -> x0, blocking collectives: 41.8 us -> none  [the longest x1 25.3 us: per_device(): enc_grad = lax.psum(enc_part, 'expert').astype(jnp.bfloat16)]
    all_gather x3 -> x0, blocking collectives: 39.9 us -> none  [the longest x1 14.3 us: per_device(): lax.all_gather(arrived.reshape(experts * cap, model), 'pipe', axis=0, til...]
    ppermute x0 -> x6, starting transfers between devices: none -> 10.8 us  [shifted(): lax.ppermute(value, axis, [(i, (i + step) % size) for i in range(size)])]
    all_to_all x3 -> x4, waiting for transfers between devices: 9.12 us -> 19.9 us  [the longest x1 9.99 us: per_device(): lax.all_to_all(part.reshape(pipes * experts, cap, model), everyone, split...]
    ppermute x0 -> x6, waiting for transfers between devices: none -> 7.21 us  [shifted(): lax.ppermute(value, axis, [(i, (i + step) % size) for i in range(size)])]
    dot_general x12 -> x10, matrix products: 6.19 us -> 3.97 us  [the longest x1 1.43 us: per_device(): part = jnp.dot(active, w_out[0], preferred_element_type=f32).astype(bf16)]
    all_to_all x3 -> x4, starting transfers between devices: 10.8 us -> 12.4 us  [the longest x1 3.85 us: per_device(): lax.all_to_all(context_blocks, 'expert', split_axis=0, concat_axis=0, til...]
    unnamed x22 -> x21, local copies, waits for them, and re-layouts: 2.19 us -> 3.63 us
  transfers between devices with their start and end apart: 4 -> 10, of which waited for: 2 -> 9; matrix products, arithmetic and copies ran while one was open for 1% -> 6% of each run, Pallas kernels for 0% -> 0%
where the time goes in v1:
time: 63.1 us; the launch traced here: 62.4 us
  waiting for transfers between devices  27.1 us (43%)
  starting transfers between devices  23.2 us (37%)
  local copies, waits for them, and re-layouts  5.91 us (9%)
  matrix products  3.97 us (6%)
  other arithmetic  1.49 us (2%)
  between operations  0.81 us (1%)
    ppermute x6, starting transfers between devices, shifted(): lax.ppermute(value, axis, [(i, (i + step) % size) for i in range(size)])  10.8 us
    all_to_all x1, waiting for transfers between devices, per_device(): lax.all_to_all(part.reshape(pipes * experts, cap, model), everyone, split...  9.99 us
    ppermute x6, waiting for transfers between devices, shifted(): lax.ppermute(value, axis, [(i, (i + step) % size) for i in range(size)])  7.21 us
    all_to_all x1, waiting for transfers between devices, per_device(): lax.all_to_all(context_blocks, 'expert', split_axis=0, concat_axis=0, til...  5.07 us
    all_to_all x1, waiting for transfers between devices, per_device(): lax.all_to_all(jnp.broadcast_to(enc_part[None], (experts, enc_dev, model)...  4.02 us
    all_to_all x1, starting transfers between devices, per_device(): lax.all_to_all(context_blocks, 'expert', split_axis=0, concat_axis=0, til...  3.85 us
    unnamed x21, local copies, waits for them, and re-layouts  3.63 us
    all_to_all x1, starting transfers between devices, per_device(): lax.all_to_all(jnp.broadcast_to(enc_part[None], (experts, enc_dev, model)...  3.37 us
  transfers between devices with their start and end apart: 10, of which 9 were waited for; matrix products, arithmetic and copies ran while one was open for 6% of the time, Pallas kernels for 0%

profile of v1, /device:TPU:0, one launch (start us, length us, event | category | flops | bytes accessed | tf_op | source)
XLA Modules:
  0.0 62.4 jit_solution(11143915720885311184)
XLA Ops:
  0.6 0.0 copy-start
  0.7 0.9 %constant_dynamic-update-slice_fusion.1 = bf16[512,128]{0,1:T(8,128)(2,1)S(1)} fusion(bf16[512,64]{0,1:T(8,128)(2,1)} %param.12), kind=kLoop, calls=%fused_computation.55 | loop fusion | bytes 131072
  1.6 0.7 %copy-done.5 = bf16[8,512]{1,0:T(8,128)(2,1)S(1)} copy-done((bf16[8,512]{1,0:T(8,128)(2,1)S(1)}, bf16[8,512]{1,0:T(8,128)(2,1)}, u32[]{:S(2)}) %copy-start.5) | copy-done | bytes 8216
  2.3 0.1 fusion.6
  2.4 5.1 %collective-permute-start.2 = (bf16[8,128]{1,0:T(8,128)(2,1)S(1)}, bf16[8,128]{1,0:T(8,128)(2,1)S(1)}, u32[]{:S(2)}, u32[]{:S(2)}) collective-permute-start(bf16[8,128]{1,0:T(8,128)(2,1)S(1)} %fusion.6), channel_id=1, source_target_pairs={{0,24},{8,0},{16,8},{24,16},{1,25},{9,1},{17,9},{25,17},{2,26},{10... | collective-permute-start | bytes 6152 | tf_op jit(solution)/shard_map/ppermute | solution.py:11
  7.5 1.0 %collective-permute-start = (bf16[8,128]{1,0:T(8,128)(2,1)S(1)}, bf16[8,128]{1,0:T(8,128)(2,1)S(1)}, u32[]{:S(2)}, u32[]{:S(2)}) collective-permute-start(bf16[8,128]{1,0:T(8,128)(2,1)S(1)} %fusion.6), channel_id=1, source_target_pairs={{0,8},{8,16},{16,24},{24,0},{1,9},{9,17},{17,25},{25,1},{2,10},{10... | collective-permute-start | bytes 6152 | tf_op jit(solution)/shard_map/ppermute | solution.py:11
  8.5 0.1 iota_add_fusion
  8.6 0.7 %copy-done.6 = s32[128,1]{0,1:T(1,128)S(1)} copy-done((s32[128,1]{0,1:T(1,128)S(1)}, s32[128,1]{0,1:T(1,128)}, u32[]{:S(2)}) %copy-start.6) | copy-done | bytes 536
  9.2 0.1 fusion.19
  9.3 0.2 reduce_window_sum.11
  9.5 0.2 select_reduce_fusion
  9.7 0.0 copy-start.7
  9.7 0.1 add.60
  9.8 0.6 copy-done.7
  10.4 1.6 %collective-permute-done.1 = bf16[8,128]{1,0:T(8,128)(2,1)S(1)} collective-permute-done((bf16[8,128]{1,0:T(8,128)(2,1)S(1)}, bf16[8,128]{1,0:T(8,128)(2,1)S(1)}, u32[]{:S(2)}, u32[]{:S(2)}) %collective-permute-start.1) | collective-permute-done | bytes 2080 | tf_op jit(solution)/shard_map/ppermute | solution.py:11
  12.0 0.9 %collective-permute-done = bf16[8,128]{1,0:T(8,128)(2,1)S(1)} collective-permute-done((bf16[8,128]{1,0:T(8,128)(2,1)S(1)}, bf16[8,128]{1,0:T(8,128)(2,1)S(1)}, u32[]{:S(2)}, u32[]{:S(2)}) %collective-permute-start) | collective-permute-done | bytes 2080 | tf_op jit(solution)/shard_map/ppermute | solution.py:11
  12.9 0.2 fusion.47
  13.0 0.1 fusion.16
  13.1 0.3 fusion.4
  13.4 0.7 %copy.20 = bf16[8,8,8,128]{3,2,0,1:T(8,128)(2,1)} copy(bf16[8,8,8,128]{3,2,1,0:T(8,128)(2,1)S(1)} %fusion.4) | data formatting | bytes 262144 | tf_op jit(solution)/shard_map/reshape | solution.py:56
  14.1 3.9 %all-to-all-start = ((bf16[8,64,128]{2,1,0:T(8,128)(2,1)}), bf16[8,64,128]{2,1,0:T(8,128)(2,1)S(1)}, u32[]{:S(2)}, u32[]{:S(2)}) async-start(bf16[8,64,128]{2,1,0:T(8,128)(2,1)} %bitcast.49), calls=%async_computation | async-start | bytes 262144 | tf_op jit(solution)/shard_map/all_to_all | solution.py:57
  18.0 0.2 multiply_reduce_fusion.1
  18.2 0.2 fusion.17
  18.4 5.1 %all-to-all-done = bf16[8,64,128]{2,1,0:T(8,128)(2,1)S(1)} async-done(((bf16[8,64,128]{2,1,0:T(8,128)(2,1)}), bf16[8,64,128]{2,1,0:T(8,128)(2,1)S(1)}, u32[]{:S(2)}, u32[]{:S(2)}) %all-to-all-start) | async-done | bytes 131104 | tf_op jit(solution)/shard_map/all_to_all | solution.py:57
  23.5 0.0 copy-start.1
  23.5 0.1 copy.17
  23.7 0.8 %copy-done.1 = bf16[128,512]{1,0:T(8,128)(2,1)S(1)} copy-done((bf16[128,512]{1,0:T(8,128)(2,1)S(1)}, bf16[128,512]{1,0:T(8,128)(2,1)}, u32[]{:S(2)}) %copy-start.1) | copy-done | bytes 131096
  24.4 0.1 multiply_reduce_fusion
  24.5 0.2 fusion.5
  24.8 0.7 %broadcast_in_dim.21 = bf16[4,8,8,512]{3,2,1,0:T(8,128)(2,1)} broadcast(bf16[8,8,512]{2,1,0:T(8,128)(2,1)S(1)} %fusion.5), dimensions={1,2,3} | broadcast | bytes 327680 | tf_op jit(solution)/shard_map/broadcast_in_dim | solution.py:69
  25.5 2.6 %all-to-all-start.1 = ((bf16[32,8,512]{2,1,0:T(8,128)(2,1)}), bf16[32,8,512]{2,1,0:T(8,128)(2,1)S(1)}, u32[]{:S(2)}, u32[]{:S(2)}) async-start(bf16[32,8,512]{2,1,0:T(8,128)(2,1)} %bitcast.6), calls=%async_computation.1 | async-start | bytes 524288 | tf_op jit(solution)/shard_map/all_to_all | solution.py:72
  28.1 0.2 fusion.21
  28.3 0.1 fusion.36
  28.4 3.6 %collective-permute-start.3 = (f32[8,128]{1,0:T(8,128)S(1)}, f32[8,128]{1,0:T(8,128)S(1)}, u32[]{:S(2)}, u32[]{:S(2)}) collective-permute-start(f32[8,128]{1,0:T(8,128)S(1)} %get-tuple-element.2), channel_id=1, source_target_pairs={{0,24},{8,0},{16,8},{24,16},{1,25},{9,1},{17,9},{25,17},{2,26},{10... | collective-permute-start | bytes 12296 | tf_op jit(solution)/shard_map/ppermute | solution.py:11
  32.0 1.1 %collective-permute-start.4 = (f32[8,128]{1,0:T(8,128)S(1)}, f32[8,128]{1,0:T(8,128)S(1)}, u32[]{:S(2)}, u32[]{:S(2)}) collective-permute-start(f32[8,128]{1,0:T(8,128)S(1)} %get-tuple-element.4), channel_id=1, source_target_pairs={{0,16},{8,24},{16,0},{24,8},{1,17},{9,25},{17,1},{25,9},{2,18},{10... | collective-permute-start | bytes 12296 | tf_op jit(solution)/shard_map/ppermute | solution.py:11
  33.1 0.3 collective-permute-done.3
  33.4 4.1 %collective-permute-done.5 = f32[8,128]{1,0:T(8,128)S(1)} collective-permute-done((f32[8,128]{1,0:T(8,128)S(1)}, f32[8,128]{1,0:T(8,128)S(1)}, u32[]{:S(2)}, u32[]{:S(2)}) %collective-permute-start.5) | collective-permute-done | bytes 4128 | tf_op jit(solution)/shard_map/ppermute | solution.py:11
  37.4 0.4 collective-permute-done.4
  37.8 0.2 fusion.37
  38.0 0.8 %all-to-all-done.1 = bf16[32,8,512]{2,1,0:T(8,128)(2,1)S(1)} async-done(((bf16[32,8,512]{2,1,0:T(8,128)(2,1)}), bf16[32,8,512]{2,1,0:T(8,128)(2,1)S(1)}, u32[]{:S(2)}, u32[]{:S(2)}) %all-to-all-start.1) | async-done | bytes 262176 | tf_op jit(solution)/shard_map/all_to_all | solution.py:72
  38.8 0.7 %broadcast_in_dim.40 = f32[8,8,512]{2,1,0:T(8,128)} broadcast(f32[8,512]{1,0:T(8,128)S(1)} %fusion.37), dimensions={1,2} | broadcast | bytes 147456 | tf_op jit(solution)/shard_map/broadcast_in_dim | solution.py:108
  39.5 3.4 %all-to-all-start.3 = ((f32[8,8,512]{2,1,0:T(8,128)}), f32[8,8,512]{2,1,0:T(8,128)S(1)}, u32[]{:S(2)}, u32[]{:S(2)}) async-start(f32[8,8,512]{2,1,0:T(8,128)} %broadcast_in_dim.40), calls=%async_computation.3 | async-start | bytes 262144 | tf_op jit(solution)/shard_map/all_to_all | solution.py:107
  42.9 1.4 %fusion = bf16[32,8,512]{2,1,0:T(8,128)(2,1)} fusion(bf16[1,320,512]{2,1,0:T(8,128)(2,1)S(1)} %copy-done, bf16[1,512,320]{1,2,0:T(8,128)(2,1)S(1)} %copy-done.8, bf16[32,8,512]{2,1,0:T(8,128)(2,1)S(1)} %all-to-all-done.1), kind=kOutput, calls=%fused_computation.2 | convolution fusion | flops 168067072 | bytes 1179648 | tf_op jit(solution)/shard_map/dot_general | solution.py:79
  44.3 4.0 %all-to-all-done.3 = f32[8,8,512]{2,1,0:T(8,128)S(1)} async-done(((f32[8,8,512]{2,1,0:T(8,128)}), f32[8,8,512]{2,1,0:T(8,128)S(1)}, u32[]{:S(2)}, u32[]{:S(2)}) %all-to-all-start.3) | async-done | bytes 131104 | tf_op jit(solution)/shard_map/all_to_all | solution.py:107
  48.3 2.6 %all-to-all-start.2 = ((bf16[32,8,512]{2,1,0:T(8,128)(2,1)}), bf16[32,8,512]{2,1,0:T(8,128)(2,1)S(1)}, u32[]{:S(2)}, u32[]{:S(2)}) async-start(bf16[32,8,512]{2,1,0:T(8,128)(2,1)} %fusion), calls=%async_computation.2 | async-start | bytes 524288 | tf_op jit(solution)/shard_map/all_to_all | solution.py:80
  50.9 0.6 reduce_sum.62
  51.5 10.0 %all-to-all-done.2 = bf16[32,8,512]{2,1,0:T(8,128)(2,1)S(1)} async-done(((bf16[32,8,512]{2,1,0:T(8,128)(2,1)}), bf16[32,8,512]{2,1,0:T(8,128)(2,1)S(1)}, u32[]{:S(2)}, u32[]{:S(2)}) %all-to-all-start.2) | async-done | bytes 262176 | tf_op jit(solution)/shard_map/all_to_all | solution.py:80
  61.6 0.9 %fusion.2 = bf16[128,512]{1,0:T(8,128)(2,1)} fusion(bf16[64,512]{1,0:T(8,128)(2,1)S(1)} %bitcast_reduce_fusion, f32[512,128]{0,1:T(8,128)S(1)} %copy.17, bf16[128,512]{1,0:T(8,128)(2,1)S(1)} %copy-done.1, s32[128]{0:T(128)S(1)} %compare_select_fusion.3), kind=kOutput, calls=%fused_computation.5 | convolution fusion | flops 8658944 | bytes 590336 | tf_op jit(solution)/shard_map/dot_general | solution.py:88
  (24 shorter events, 0.1 us)
Async XLA Ops:
  0.6 42.2 %copy-start = (bf16[1,320,512]{2,1,0:T(8,128)(2,1)S(1)}, bf16[1,320,512]{2,1,0:T(8,128)(2,1)}, u32[]{:S(2)}) copy-start(bf16[1,320,512]{2,1,0:T(8,128)(2,1)} %param.21) | copy-start | bytes 983044
  0.6 0.9 %copy-start.3 = (bf16[512,64]{0,1:T(8,128)(2,1)S(1)}, bf16[512,64]{0,1:T(8,128)(2,1)}, u32[]{:S(2)}) copy-start(bf16[512,64]{0,1:T(8,128)(2,1)} %param.13) | copy-start | bytes 196612
  1.6 0.7 %copy-start.5 = (bf16[8,512]{1,0:T(8,128)(2,1)S(1)}, bf16[8,512]{1,0:T(8,128)(2,1)}, u32[]{:S(2)}) copy-start(bf16[8,512]{1,0:T(8,128)(2,1)} %param.11) | copy-start | bytes 24580
  2.4 8.0 %collective-permute-start.2 = (bf16[8,128]{1,0:T(8,128)(2,1)S(1)}, bf16[8,128]{1,0:T(8,128)(2,1)S(1)}, u32[]{:S(2)}, u32[]{:S(2)}) collective-permute-start(bf16[8,128]{1,0:T(8,128)(2,1)S(1)} %fusion.6), channel_id=1, source_target_pairs={{0,24},{8,0},{16,8},{24,16},{1,25},{9,1},{17,9},{25,17},{2,26},{10... | collective-permute-start | bytes 6152 | tf_op jit(solution)/shard_map/ppermute | solution.py:11
  7.5 4.5 %collective-permute-start.1 = (bf16[8,128]{1,0:T(8,128)(2,1)S(1)}, bf16[8,128]{1,0:T(8,128)(2,1)S(1)}, u32[]{:S(2)}, u32[]{:S(2)}) collective-permute-start(bf16[8,128]{1,0:T(8,128)(2,1)S(1)} %fusion.6), channel_id=1, source_target_pairs={{0,16},{8,24},{16,0},{24,8},{1,17},{9,25},{17,1},{25,9},{2,18},{10... | collective-permute-start | bytes 6152 | tf_op jit(solution)/shard_map/ppermute | solution.py:11
  7.5 5.4 %collective-permute-start = (bf16[8,128]{1,0:T(8,128)(2,1)S(1)}, bf16[8,128]{1,0:T(8,128)(2,1)S(1)}, u32[]{:S(2)}, u32[]{:S(2)}) collective-permute-start(bf16[8,128]{1,0:T(8,128)(2,1)S(1)} %fusion.6), channel_id=1, source_target_pairs={{0,8},{8,16},{16,24},{24,0},{1,9},{9,17},{17,25},{25,1},{2,10},{10... | collective-permute-start | bytes 6152 | tf_op jit(solution)/shard_map/ppermute | solution.py:11
  8.6 0.7 %copy-start.6 = (s32[128,1]{0,1:T(1,128)S(1)}, s32[128,1]{0,1:T(1,128)}, u32[]{:S(2)}) copy-start(s32[128,1]{0,1:T(1,128)} %param.19) | copy-start | bytes 1540
  9.2 3.6 %copy-start.2 = (bf16[1024,64]{0,1:T(8,128)(2,1)S(1)}, bf16[1024,64]{0,1:T(8,128)(2,1)}, u32[]{:S(2)}) copy-start(bf16[1024,64]{0,1:T(8,128)(2,1)} %param.14) | copy-start | bytes 393220
  9.7 0.7 %copy-start.7 = (bf16[512]{0:T(512)(128)(2,1)S(1)}, bf16[512]{0:T(512)(128)(2,1)}, u32[]{:S(2)}) copy-start(bf16[512]{0:T(512)(128)(2,1)} %param.18) | copy-start | bytes 3076
  10.4 2.5 %copy-start.4 = (s32[1024]{0:T(1024)S(1)}, s32[1024]{0:T(1024)}, u32[]{:S(2)}) copy-start(s32[1024]{0:T(1024)} %param.15) | copy-start | bytes 12292
  14.1 3.9 %copy-start.9 = (bf16[1024,64]{0,1:T(8,128)(2,1)S(1)}, bf16[1024,64]{0,1:T(8,128)(2,1)}, u32[]{:S(2)}) copy-start(bf16[1024,64]{0,1:T(8,128)(2,1)} %param.16) | copy-start | bytes 393220
  14.1 9.4 %all-to-all-start = ((bf16[8,64,128]{2,1,0:T(8,128)(2,1)}), bf16[8,64,128]{2,1,0:T(8,128)(2,1)S(1)}, u32[]{:S(2)}, u32[]{:S(2)}) async-start(bf16[8,64,128]{2,1,0:T(8,128)(2,1)} %bitcast.49), calls=%async_computation | async-start | bytes 262144 | tf_op jit(solution)/shard_map/all_to_all | solution.py:57
  23.5 0.9 %copy-start.1 = (bf16[128,512]{1,0:T(8,128)(2,1)S(1)}, bf16[128,512]{1,0:T(8,128)(2,1)}, u32[]{:S(2)}) copy-start(bf16[128,512]{1,0:T(8,128)(2,1)} %param.17) | copy-start | bytes 393220
  25.5 13.3 %all-to-all-start.1 = ((bf16[32,8,512]{2,1,0:T(8,128)(2,1)}), bf16[32,8,512]{2,1,0:T(8,128)(2,1)S(1)}, u32[]{:S(2)}, u32[]{:S(2)}) async-start(bf16[32,8,512]{2,1,0:T(8,128)(2,1)} %bitcast.6), calls=%async_computation.1 | async-start | bytes 524288 | tf_op jit(solution)/shard_map/all_to_all | solution.py:72
  28.3 14.6 %copy-start.8 = (bf16[1,512,320]{1,2,0:T(8,128)(2,1)S(1)}, bf16[1,512,320]{1,2,0:T(8,128)(2,1)}, u32[]{:S(2)}) copy-start(bf16[1,512,320]{1,2,0:T(8,128)(2,1)} %param.20) | copy-start | bytes 983044
  28.4 5.0 %collective-permute-start.3 = (f32[8,128]{1,0:T(8,128)S(1)}, f32[8,128]{1,0:T(8,128)S(1)}, u32[]{:S(2)}, u32[]{:S(2)}) collective-permute-start(f32[8,128]{1,0:T(8,128)S(1)} %get-tuple-element.2), channel_id=1, source_target_pairs={{0,24},{8,0},{16,8},{24,16},{1,25},{9,1},{17,9},{25,17},{2,26},{10... | collective-permute-start | bytes 12296 | tf_op jit(solution)/shard_map/ppermute | solution.py:11
  32.0 5.4 %collective-permute-start.5 = (f32[8,128]{1,0:T(8,128)S(1)}, f32[8,128]{1,0:T(8,128)S(1)}, u32[]{:S(2)}, u32[]{:S(2)}) collective-permute-start(f32[8,128]{1,0:T(8,128)S(1)} %get-tuple-element.3), channel_id=1, source_target_pairs={{0,8},{8,16},{16,24},{24,0},{1,9},{9,17},{17,25},{25,1},{2,10},{10... | collective-permute-start | bytes 12296 | tf_op jit(solution)/shard_map/ppermute | solution.py:11
  32.0 5.8 %collective-permute-start.4 = (f32[8,128]{1,0:T(8,128)S(1)}, f32[8,128]{1,0:T(8,128)S(1)}, u32[]{:S(2)}, u32[]{:S(2)}) collective-permute-start(f32[8,128]{1,0:T(8,128)S(1)} %get-tuple-element.4), channel_id=1, source_target_pairs={{0,16},{8,24},{16,0},{24,8},{1,17},{9,25},{17,1},{25,9},{2,18},{10... | collective-permute-start | bytes 12296 | tf_op jit(solution)/shard_map/ppermute | solution.py:11
  39.5 8.8 %all-to-all-start.3 = ((f32[8,8,512]{2,1,0:T(8,128)}), f32[8,8,512]{2,1,0:T(8,128)S(1)}, u32[]{:S(2)}, u32[]{:S(2)}) async-start(f32[8,8,512]{2,1,0:T(8,128)} %broadcast_in_dim.40), calls=%async_computation.3 | async-start | bytes 262144 | tf_op jit(solution)/shard_map/all_to_all | solution.py:107
  48.3 13.2 %all-to-all-start.2 = ((bf16[32,8,512]{2,1,0:T(8,128)(2,1)}), bf16[32,8,512]{2,1,0:T(8,128)(2,1)S(1)}, u32[]{:S(2)}, u32[]{:S(2)}) async-start(bf16[32,8,512]{2,1,0:T(8,128)(2,1)} %fusion), calls=%async_computation.2 | async-start | bytes 524288 | tf_op jit(solution)/shard_map/all_to_all | solution.py:80

commit v2 on v1

v2 whole, which is shorter than its diff:
```python
import functools
import math

import jax
import jax.numpy as jnp
from jax import lax
from jax.experimental import pallas as pl
from jax.experimental.pallas import tpu as pltpu
from jax.sharding import PartitionSpec as P

EVERYONE = ("pipe", "expert")
VMEM = pl.BlockSpec(memory_space=pltpu.VMEM)
HBM = pl.BlockSpec(memory_space=pltpu.HBM)


def shifted(value, axis, step):
    size = lax.axis_size(axis)
    return lax.ppermute(value, axis, [(i, (i + step) % size) for i in range(size)])


def crossed(value, bit):
    size = lax.axis_size("expert")
    return lax.ppermute(value, "expert", [(i, i ^ bit) for i in range(size)])


def pick_half(ref, bit, mine):
    half = ref.shape[1] // 2
    side = lax.rem(lax.axis_index("expert") // bit, 2)
    return ref[:, pl.ds(pl.multiple_of((side if mine else 1 - side) * half, half), half)]


def project_kernel(
    cap, enc_hbm, key_hbm, value_hbm, queries_hbm, lengths_hbm, gain_hbm, routes_hbm, residual_hbm, *refs
):
    spread_hbm, keep_ref, send_ref, lengths_ref, gain_ref, target_ref, residual_ref = refs[:7]
    enc_ref, key_ref, value_ref, queries_ref, routes_ref, spread_ref, arrived, left = refs[7:]
    f32, bf16 = jnp.float32, jnp.bfloat16
    here, experts = lax.axis_index("expert"), lax.axis_size("expert")
    tok_dev = routes_ref.shape[1]
    own_tokens = pl.ds(pl.multiple_of(here * tok_dev, tok_dev), tok_dev)
    fetches = [
        pltpu.make_async_copy(source, target, arrived.at[i])
        for i, (source, target) in enumerate(
            (
                (enc_hbm, enc_ref),
                (key_hbm, key_ref),
                (value_hbm, value_ref),
                (routes_hbm, routes_ref),
                (queries_hbm, queries_ref),
                (lengths_hbm.at[own_tokens], lengths_ref),
                (gain_hbm, gain_ref),
                (residual_hbm, residual_ref),
            )
        )
    ]
    for fetch in fetches:
        fetch.start()
    for fetch in fetches[:3]:
        fetch.wait()
    enc = enc_ref[...]
    own = jnp.concatenate(
        [
            lax.dot_general(enc, ref[...], (((1,), (1,)), ((), ())), preferred_element_type=f32)
            for ref in (key_ref, value_ref)
        ],
        axis=1,
    )
    spread_ref[...] = jnp.broadcast_to(own.astype(bf16)[None], spread_ref.shape)
    leave = pltpu.make_async_copy(spread_ref, spread_hbm, left)
    leave.start()
    for fetch in fetches[3:]:
        fetch.wait()
    keep_ref[...] = pick_half(queries_ref, experts // 2, True)
    send_ref[...] = pick_half(queries_ref, experts // 2, False)
    routes = routes_ref[...]
    onehot = lax.broadcasted_iota(jnp.int32, (experts, tok_dev), 0) == routes
    earlier = lax.broadcasted_iota(jnp.int32, (tok_dev, tok_dev), 0) < lax.broadcasted_iota(
        jnp.int32, (tok_dev, tok_dev), 1
    )
    before = jnp.dot(
        onehot.astype(f32).astype(bf16), earlier.astype(f32).astype(bf16), preferred_element_type=f32
    )
    slot_rank = jnp.sum(jnp.where(onehot, before, 0.0), axis=0, keepdims=True).astype(jnp.int32)
    target_ref[...] = jnp.where(slot_rank < cap, routes * cap + slot_rank, -1)
    leave.wait()


def split_kernel(bit, kept_ref, got_ref, keep_ref, send_ref):
    rows = kept_ref.shape[0]
    for first, ref in ((0, kept_ref), (rows, got_ref)):
        keep_ref[first : first + rows] = pick_half(ref, bit, True)
        send_ref[first : first + rows] = pick_half(ref, bit, False)


def block_kernel(group, kv_ref, keys_ref, values_ref):
    pipes, heads, enc_dev, wide = kv_ref.shape
    head = wide // 2
    rows, cols = pipes * group * enc_dev, group * head
    f32, bf16 = jnp.float32, jnp.bfloat16
    row_head = lax.rem(lax.broadcasted_iota(jnp.int32, (rows, cols), 0) // enc_dev, group)
    same_head = row_head == lax.broadcasted_iota(jnp.int32, (rows, cols), 1) // head
    left = lax.broadcasted_iota(jnp.int32, (rows, wide), 1) < head
    for part in range(heads // group):
        kv = kv_ref[:, part * group : (part + 1) * group].reshape(rows, wide).astype(f32)
        turned = pltpu.roll(kv, head, 1)
        twice_keys = jnp.where(left, kv, turned).astype(bf16)
        twice_values = jnp.where(left, turned, kv).astype(bf16)
        for twice, ref in ((twice_keys, keys_ref), (twice_values, values_ref)):
            block = jnp.concatenate([twice] * (group // 2), axis=1)
            ref[part] = jnp.where(same_head, block, jnp.zeros_like(block))


def attend_kernel(
    scale,
    enc_dev,
    head,
    keys_ref,
    values_ref,
    lengths_ref,
    residual_ref,
    gain_ref,
    target_ref,
    kept_ref,
    got_ref,
    hidden_ref,
    out_ref,
    q_ref,
):
    parts, rows, cols = keys_ref.shape
    group, heads = cols // head, parts * cols // head
    pipes, tok_dev = rows // (group * enc_dev), q_ref.shape[1]
    f32, bf16 = jnp.float32, jnp.bfloat16
    here = lax.axis_index("expert")
    levels = heads.bit_length() - 1
    for r in range(heads):
        flips = sum(1 << (levels - 1 - i) for i in range(levels) if r >> i & 1)
        which = pl.multiple_of(lax.bitwise_xor(here, flips) * head, head)
        ref, first = (kept_ref, r) if r < heads // 2 else (got_ref, r - heads // 2)
        q_ref[pl.ds(which, head)] = ref[first * head : (first + 1) * head]
    shape = (pipes, group, enc_dev, tok_dev)
    position = lax.broadcasted_iota(jnp.int32, shape, 0) * enc_dev + lax.broadcasted_iota(
        jnp.int32, shape, 2
    )
    visible = position < lengths_ref[...].reshape(1, 1, 1, tok_dev)
    pieces = []
    for part in range(parts):
        scores = scale * jnp.dot(
            keys_ref[part], q_ref[part * cols : (part + 1) * cols], preferred_element_type=f32
        )
        scores = jnp.where(visible, scores.reshape(shape), -1e30)
        highest = jnp.max(jnp.max(scores, axis=0, keepdims=True), axis=2, keepdims=True)
        weights = jnp.where(visible, jnp.exp(scores - highest), 0.0)
        total = jnp.sum(jnp.sum(weights, axis=0, keepdims=True), axis=2, keepdims=True)
        probs_low = (weights / total).reshape(rows, tok_dev).astype(bf16)
        pieces.append(
            lax.dot_general(
                probs_low, values_ref[part], (((0,), (0,)), ((), ())), preferred_element_type=f32
            ).astype(bf16)
        )
    context = pieces[0] if len(pieces) == 1 else jnp.concatenate(pieces, axis=1)
    hidden = residual_ref[...].astype(f32) + context.astype(f32)
    hidden_ref[...] = hidden
    power = jnp.mean(hidden * hidden, axis=1, keepdims=True)
    normed = (hidden * lax.rsqrt(power + 1e-06) * gain_ref[...].astype(f32).reshape(1, -1)).astype(
        bf16
    )
    slots = out_ref.shape[1]
    placing = lax.broadcasted_iota(jnp.int32, (slots, tok_dev), 0) == target_ref[...]
    outgoing = jnp.dot(
        placing.astype(f32).astype(bf16), normed, preferred_element_type=f32
    ).astype(bf16)
    for pipe in range(pipes):
        out_ref[pipe] = outgoing


def backward_kernel(scale, kv_ref, queries_ref, grad_ref, lengths_ref, *refs):
    out_refs, sums_ref = refs[:-1], refs[-1]
    pipes, _, enc_dev, wide = kv_ref.shape
    head, rows = wide // 2, pipes * enc_dev
    f32, bf16 = jnp.float32, jnp.bfloat16
    kv = kv_ref[:, lax.axis_index("expert")].reshape(rows, wide)
    queries, grads = queries_ref[...], grad_ref[...]
    tokens = queries.shape[1]
    keys, values = kv[:, :head], kv[:, head:]
    scores = jnp.dot(keys, queries, preferred_element_type=f32) * scale
    visible = lax.broadcasted_iota(jnp.int32, (rows, tokens), 0) < lengths_ref[...].reshape(1, tokens)
    scores = jnp.where(visible, scores, -1e30)
    highest = jnp.max(scores, axis=0, keepdims=True)
    weights = jnp.where(visible, jnp.exp(scores - highest), 0.0)
    probs = weights / jnp.sum(weights, axis=0, keepdims=True)
    probs_low = probs.astype(bf16)
    grad_probs = jnp.dot(values, grads, preferred_element_type=f32)
    row_delta = jnp.sum(probs * grad_probs, axis=0, keepdims=True)
    grad_scores = (probs * (grad_probs - row_delta) * scale).astype(bf16)
    over_tokens = (((1,), (1,)), ((), ()))
    grad_keys = lax.dot_general(grad_scores, queries, over_tokens, preferred_element_type=f32)
    grad_values = lax.dot_general(probs_low, grads, over_tokens, preferred_element_type=f32)
    sums_ref[...] = jnp.concatenate([grad_keys, grad_values], axis=1).reshape(sums_ref.shape)
    own = lax.axis_index("pipe")
    for s, out_ref in enumerate(out_refs):
        out_ref[...] = sums_ref[lax.rem(own + s, pipes)]


def combine_kernel(returned_ref, target_ref, hidden_ref, out_ref):
    slots, tok_dev = returned_ref.shape[1], hidden_ref.shape[0]
    f32, bf16 = jnp.float32, jnp.bfloat16
    rows = jnp.sum(returned_ref[...].astype(f32), axis=0).astype(bf16)
    placing = lax.broadcasted_iota(jnp.int32, (slots, tok_dev), 0) == target_ref[...]
    expert_out = lax.dot_general(
        placing.astype(f32).astype(bf16), rows, (((0,), (0,)), ((), ())), preferred_element_type=f32
    )
    out_ref[...] = (hidden_ref[...] + expert_out).astype(bf16)


def per_device(
    enc_states,
    key_weight,
    value_weight,
    queries,
    lengths,
    context_grad,
    residual,
    norm_gain,
    routes,
    w_in,
    w_out,
):
    enc_dev = enc_states.shape[0]
    head = key_weight.shape[1]
    tok_dev = residual.shape[0]
    model = residual.shape[1]
    experts = lax.axis_size("expert")
    pipes = lax.axis_size("pipe")
    cap = tok_dev // (2 * experts)
    scale = 1.0 / math.sqrt(head)
    f32, bf16 = jnp.float32, jnp.bfloat16
    here, own_pipe = lax.axis_index("expert"), lax.axis_index("pipe")
    params = pltpu.CompilerParams(vmem_limit_bytes=(8 << 20) if model <= 1024 else (40 << 20))
    queries_turned = queries.T
    half = (head, experts * tok_dev // 2)
    spread_kv, keep, send, own_lengths, gain, target, near_residual = pl.pallas_call(
        functools.partial(project_kernel, cap),
        out_shape=[
            jax.ShapeDtypeStruct((pipes * experts, enc_dev, 2 * head), bf16),
            jax.ShapeDtypeStruct(half, bf16),
            jax.ShapeDtypeStruct(half, bf16),
            jax.ShapeDtypeStruct((tok_dev,), jnp.int32),
            jax.ShapeDtypeStruct((model,), bf16),
            jax.ShapeDtypeStruct((1, tok_dev), jnp.int32),
            jax.ShapeDtypeStruct((tok_dev, model), bf16),
        ],
        in_specs=[HBM] * 8,
        out_specs=[HBM] + [VMEM] * 6,
        scratch_shapes=[
            pltpu.VMEM((enc_dev, model), bf16),
            pltpu.VMEM((head, model), bf16),
            pltpu.VMEM((head, model), bf16),
            pltpu.VMEM((head, experts * tok_dev), bf16),
            pltpu.VMEM((1, tok_dev), jnp.int32),
            pltpu.VMEM((pipes * experts, enc_dev, 2 * head), bf16),
            pltpu.SemaphoreType.DMA((8,)),
            pltpu.SemaphoreType.DMA,
        ],
        compiler_params=params,
    )(
        *(
            pltpu.with_memory_space_constraint(value, pltpu.HBM)
            for value in (
                enc_states,
                key_weight.T,
                value_weight.T,
                queries_turned,
                lengths,
                norm_gain,
                routes.T,
                residual,
            )
        )
    )
    kv = lax.all_to_all(
        spread_kv, EVERYONE, split_axis=0, concat_axis=0, tiled=True
    ).reshape(pipes, experts, enc_dev, 2 * head)
    bit = experts // 2
    got = crossed(send, bit)
    while bit > 1:
        bit //= 2
        keep, send = pl.pallas_call(
            functools.partial(split_kernel, bit),
            out_shape=[jax.ShapeDtypeStruct((2 * keep.shape[0], keep.shape[1] // 2), bf16)] * 2,
            in_specs=[VMEM] * 2,
            out_specs=[VMEM] * 2,
            compiler_params=params,
            cost_estimate=pl.CostEstimate(flops=0, bytes_accessed=0, transcendentals=0),
        )(keep, got)
        got = crossed(send, bit)
    group = max(g for g in range(2, experts + 1, 2) if experts % g == 0 and g * head <= 512)
    blocks = (experts // group, pipes * group * enc_dev, group * head)
    key_blocks, value_blocks = pl.pallas_call(
        functools.partial(block_kernel, group),
        out_shape=[jax.ShapeDtypeStruct(blocks, bf16)] * 2,
        in_specs=[VMEM],
        out_specs=[VMEM] * 2,
        compiler_params=params,
        cost_estimate=pl.CostEstimate(flops=1 << 34, bytes_accessed=1 << 26, transcendentals=0),
    )(kv)
    hidden_state, outgoing = pl.pallas_call(
        functools.partial(attend_kernel, scale, enc_dev, head),
        out_shape=(
            jax.ShapeDtypeStruct((tok_dev, model), f32),
            jax.ShapeDtypeStruct((pipes, experts * cap, model), bf16),
        ),
        in_specs=[VMEM] * 8,
        out_specs=[VMEM] * 2,
        scratch_shapes=[pltpu.VMEM((model, tok_dev), bf16)],
        compiler_params=params,
    )(key_blocks, value_blocks, own_lengths, near_residual, gain, target, keep, got)
    outgoing = outgoing.reshape(pipes * experts, cap, model)
    kv, outgoing = lax.optimization_barrier((kv, outgoing))
    total, *others = pl.pallas_call(
        functools.partial(backward_kernel, scale),
        out_shape=[jax.ShapeDtypeStruct((enc_dev, 2 * head), f32)] * pipes,
        in_specs=[VMEM] * 4,
        out_specs=[VMEM] * pipes,
        scratch_shapes=[pltpu.VMEM((pipes, enc_dev, 2 * head), f32)],
        compiler_params=params,
        cost_estimate=pl.CostEstimate(flops=0, bytes_accessed=0, transcendentals=0),
    )(kv, queries_turned, context_grad.T, lengths)
    for s, other in enumerate(others):
        total = total + shifted(other, "pipe", s + 1)
    total = total.astype(bf16)
    arrived = lax.all_to_all(outgoing, EVERYONE, split_axis=0, concat_axis=0, tiled=True)
    active = jnp.maximum(
        jnp.dot(
            arrived.reshape(pipes * experts * cap, model), w_in[0], preferred_element_type=f32
        ),
        0.0,
    ).astype(bf16)
    part = jnp.dot(active, w_out[0], preferred_element_type=f32).astype(bf16)
    enc_part = lax.dot_general(
        total[:, :head], key_weight, (((1,), (1,)), ((), ())), preferred_element_type=f32
    ) + lax.dot_general(
        total[:, head:], value_weight, (((1,), (1,)), ((), ())), preferred_element_type=f32
    )
    returned = lax.all_to_all(
        part.reshape(pipes * experts, cap, model),
        EVERYONE,
        split_axis=0,
        concat_axis=0,
        tiled=True,
    ).reshape(pipes, experts * cap, model)
    layer_out = pl.pallas_call(
        combine_kernel,
        out_shape=jax.ShapeDtypeStruct((tok_dev, model), bf16),
        in_specs=[VMEM] * 3,
        out_specs=VMEM,
        compiler_params=params,
    )(returned, target, hidden_state)
    for level in range(experts.bit_length() - 1):
        enc_part = enc_part + crossed(enc_part, 1 << level)
    enc_grad = enc_part.astype(bf16)
    return (layer_out, enc_grad)


def solution(mesh):
    placed = (
        P("pipe", None),
        P(None, "expert"),
        P(None, "expert"),
        P("pipe", "expert"),
        P("pipe"),
        P("pipe", "expert"),
        P(("pipe", "expert"), None),
        P(),
        P(("pipe", "expert"), None),
        P("expert", None, "pipe"),
        P("expert", "pipe", None),
    )
    return jax.shard_map(
        per_device,
        mesh=mesh,
        in_specs=placed,
        out_specs=(P(("pipe", "expert"), None), P("pipe", None)),
        check_vma=False,
    )
```

time: 63.1 us -> 50.3 us (0.80)
  waiting for transfers between devices: 27.1 us -> 15.3 us
  local copies, waits for them, and re-layouts: 5.91 us -> 0.68 us
  Pallas kernels: 0 us -> 4.75 us
  starting transfers between devices: 23.2 us -> 26.2 us
  matrix products: 3.97 us -> 1.57 us
  other arithmetic: 1.49 us -> 0.62 us
    all_to_all x4 -> x3, waiting for transfers between devices: 19.9 us -> 3.94 us  [the longest x1 2.68 us: per_device(): lax.all_to_all(spread_kv, EVERYONE, split_axis=0, concat_axis=0, tiled=True)]
    ppermute x0 -> x6, starting transfers between devices: none -> 8.7 us  [crossed(): return lax.ppermute(value, 'expert', [(i, i ^ bit) for i in range(size)])]
    ppermute x0 -> x6, waiting for transfers between devices: none -> 7.74 us  [crossed(): return lax.ppermute(value, 'expert', [(i, i ^ bit) for i in range(size)])]
    ppermute x6 -> x3, starting transfers between devices: 10.8 us -> 5.66 us  [shifted(): lax.ppermute(value, axis, [(i, (i + step) % size) for i in range(size)])]
    pallas_call x0 -> x7, Pallas kernels: none -> 4.75 us  [the longest x1 1.86 us: per_device(): pl.pallas_call(functools.partial(project_kernel, cap), out_shape=[jax.Sha...]
    ppermute x6 -> x3, waiting for transfers between devices: 7.21 us -> 3.59 us  [shifted(): lax.ppermute(value, axis, [(i, (i + step) % size) for i in range(size)])]
    unnamed x21 -> x14, local copies, waits for them, and re-layouts: 3.63 us -> 0.68 us
    dot_general x9 -> x2, matrix products: 2.54 us -> 0.3 us  [the longest x1 0.18 us: per_device(): lax.dot_general(total[:, head:], value_weight, (((1,), (1,)), ((), ())),...]
  transfers between devices with their start and end apart: 10 -> 12, of which waited for: 9 -> 9; matrix products, arithmetic and copies ran while one was open for 6% -> 2% of each run, Pallas kernels for 0% -> 1%
where the time goes in v2:
time: 50.3 us; the launch traced here: 49.9 us
  starting transfers between devices  26.2 us (52%)
  waiting for transfers between devices  15.3 us (30%)
  Pallas kernels  4.75 us (9%)
  matrix products  1.57 us (3%)
  between operations  0.78 us (2%)
  local copies, waits for them, and re-layouts  0.68 us (1%)
  other arithmetic  0.62 us (1%)
    ppermute x6, starting transfers between devices, crossed(): return lax.ppermute(value, 'expert', [(i, i ^ bit) for i in range(size)])  8.7 us
    ppermute x6, waiting for transfers between devices, crossed(): return lax.ppermute(value, 'expert', [(i, i ^ bit) for i in range(size)])  7.74 us
    ppermute x3, starting transfers between devices, shifted(): lax.ppermute(value, axis, [(i, (i + step) % size) for i in range(size)])  5.66 us
    all_to_all x1, starting transfers between devices, per_device(): lax.all_to_all(spread_kv, EVERYONE, split_axis=0, concat_axis=0, tiled=True)  4.89 us
    all_to_all x1, starting transfers between devices, per_device(): lax.all_to_all(outgoing, EVERYONE, split_axis=0, concat_axis=0, tiled=True)  3.98 us
    ppermute x3, waiting for transfers between devices, shifted(): lax.ppermute(value, axis, [(i, (i + step) % size) for i in range(size)])  3.59 us
    all_to_all x1, starting transfers between devices, per_device(): lax.all_to_all(part.reshape(pipes * experts, cap, model), EVERYONE, split...  3 us
    all_to_all x1, waiting for transfers between devices, per_device(): lax.all_to_all(spread_kv, EVERYONE, split_axis=0, concat_axis=0, tiled=True)  2.68 us
  transfers between devices with their start and end apart: 12, of which 9 were waited for; matrix products, arithmetic and copies ran while one was open for 2% of the time, Pallas kernels for 1%

profile of v2, /device:TPU:0, one launch (start us, length us, event | category | flops | bytes accessed | tf_op | source)
XLA Modules:
  0.0 49.9 jit_solution(9061523578528852362)
XLA Ops:
  0.6 0.0 copy-start
  0.6 1.9 %shard_map.122 = (bf16[32,8,128]{2,1,0:T(8,128)(2,1)}, bf16[64,512]{1,0:T(8,128)(2,1)S(1)}, bf16[64,512]{1,0:T(8,128)(2,1)S(1)}, s32[128]{0:T(128)S(1)}, bf16[51...) custom-call(bf16[8,512]{1,0:T(8,128)(2,1)} %enc_hbm.1, bf16[64,512]{1,0:T(8,128)(2,1)} %bitcast.30, ...), custom_call_target="tpu_custom_call" | custom-call | tf_op jit(solution)/shard_map/pallas_call | solution.py:241
  2.5 3.0 %collective-permute-start = (bf16[64,512]{1,0:T(8,128)(2,1)S(1)}, bf16[64,512]{1,0:T(8,128)(2,1)S(1)}, u32[]{:S(2)}, u32[]{:S(2)}) collective-permute-start(bf16[64,512]{1,0:T(8,128)(2,1)S(1)} %get-tuple-element.31), channel_id=1, source_target_pairs={{0,4},{1,5},{2,6},{3,7},{4,0},{5,1},{6,2},{7,3},{8,12},{9,13},{10,... | collective-permute-start | bytes 196616 | tf_op jit(solution)/shard_map/ppermute | solution.py:23
  5.5 4.9 %all-to-all-start = ((bf16[32,8,128]{2,1,0:T(8,128)(2,1)}), bf16[32,8,128]{2,1,0:T(8,128)(2,1)S(1)}, u32[]{:S(2)}, u32[]{:S(2)}) async-start(bf16[32,8,128]{2,1,0:T(8,128)(2,1)} %get-tuple-element.23), calls=%async_computation | async-start | bytes 131072 | tf_op jit(solution)/shard_map/all_to_all | solution.py:280
  10.5 0.0 collective-permute-done.got_ref
  10.5 1.8 %collective-permute-start.1 = (bf16[128,256]{1,0:T(8,128)(2,1)S(1)}, bf16[128,256]{1,0:T(8,128)(2,1)S(1)}, u32[]{:S(2)}, u32[]{:S(2)}) collective-permute-start(bf16[128,256]{1,0:T(8,128)(2,1)S(1)} %get-tuple-element.33), channel_id=1, source_target_pairs={{0,2},{1,3},{2,0},{3,1},{4,6},{5,7},{6,4},{7,5},{8,10},{9,11},{10,... | collective-permute-start | bytes 196616 | tf_op jit(solution)/shard_map/ppermute | solution.py:23
  12.3 2.7 %collective-permute-done.1.got_ref = bf16[128,256]{1,0:T(8,128)(2,1)S(1)} collective-permute-done((bf16[128,256]{1,0:T(8,128)(2,1)S(1)}, bf16[128,256]{1,0:T(8,128)(2,1)S(1)}, u32[]{:S(2)}, u32[]{:S(2)}) %collective-permute-start.1) | collective-permute-done | bytes 65568 | tf_op jit(solution)/shard_map/ppermute | solution.py:23
  15.1 0.1 collective-permute-start.2
  15.2 2.7 %all-to-all-done = bf16[32,8,128]{2,1,0:T(8,128)(2,1)S(1)} async-done(((bf16[32,8,128]{2,1,0:T(8,128)(2,1)}), bf16[32,8,128]{2,1,0:T(8,128)(2,1)S(1)}, u32[]{:S(2)}, u32[]{:S(2)}) %all-to-all-start) | async-done | bytes 65568 | tf_op jit(solution)/shard_map/all_to_all | solution.py:280
  17.9 0.1 shard_map.123
  18.0 0.0 collective-permute-done.2.got_ref
  18.0 0.0 copy-start.3
  18.0 1.4 %shard_map.126 = (f32[128,512]{1,0:T(8,128)S(1)}, bf16[4,64,512]{2,1,0:T(8,128)(2,1)}) custom-call(bf16[1,256,512]{2,1,0:T(8,128)(2,1)S(1)} %get-tuple-element.24.keys_ref, bf16[1,256,512]{2,1,0:T(8,128)(2,1)S(1)} %get-tuple-element.25.values_ref, s32[128]{0:T(128)S(1)} %get-tuple-element.26.lengths_ref, ...), custom_call_target="tpu_custom_call" | custom-call | tf_op jit(solution)/shard_map/pallas_call | solution.py:306
  19.5 0.0 copy-start.1
  19.5 0.0 copy-start.2
  19.5 0.0 copy-start.4
  19.5 4.0 %all-to-all-start.1 = ((bf16[32,8,512]{2,1,0:T(8,128)(2,1)}), bf16[32,8,512]{2,1,0:T(8,128)(2,1)S(1)}, u32[]{:S(2)}, u32[]{:S(2)}) async-start(bf16[32,8,512]{2,1,0:T(8,128)(2,1)} %bitcast.5), calls=%async_computation.1 | async-start | bytes 524288 | tf_op jit(solution)/shard_map/all_to_all | solution.py:331
  23.4 0.0 copy-done.3
  23.5 0.0 copy-done.1
  23.5 0.0 copy-done.2
  23.5 0.4 shard_map.128
  23.9 1.8 %collective-permute-start.3 = (f32[8,128]{1,0:T(8,128)S(1)}, f32[8,128]{1,0:T(8,128)S(1)}, u32[]{:S(2)}, u32[]{:S(2)}) collective-permute-start(f32[8,128]{1,0:T(8,128)S(1)} %get-tuple-element.41), channel_id=1, source_target_pairs={{0,8},{8,16},{16,24},{24,0},{1,9},{9,17},{17,25},{25,1},{2,10},{10... | collective-permute-start | bytes 12296 | tf_op jit(solution)/shard_map/ppermute | solution.py:18
  25.7 2.4 %collective-permute-start.4 = (f32[8,128]{1,0:T(8,128)S(1)}, f32[8,128]{1,0:T(8,128)S(1)}, u32[]{:S(2)}, u32[]{:S(2)}) collective-permute-start(f32[8,128]{1,0:T(8,128)S(1)} %get-tuple-element.42), channel_id=1, source_target_pairs={{0,16},{8,24},{16,0},{24,8},{1,17},{9,25},{17,1},{25,9},{2,18},{10... | collective-permute-start | bytes 12296 | tf_op jit(solution)/shard_map/ppermute | solution.py:18
  28.1 1.4 %collective-permute-start.5 = (f32[8,128]{1,0:T(8,128)S(1)}, f32[8,128]{1,0:T(8,128)S(1)}, u32[]{:S(2)}, u32[]{:S(2)}) collective-permute-start(f32[8,128]{1,0:T(8,128)S(1)} %get-tuple-element.43), channel_id=1, source_target_pairs={{0,24},{8,0},{16,8},{24,16},{1,25},{9,1},{17,9},{25,17},{2,26},{10... | collective-permute-start | bytes 12296 | tf_op jit(solution)/shard_map/ppermute | solution.py:18
  29.5 3.0 %collective-permute-done.3 = f32[8,128]{1,0:T(8,128)S(1)} collective-permute-done((f32[8,128]{1,0:T(8,128)S(1)}, f32[8,128]{1,0:T(8,128)S(1)}, u32[]{:S(2)}, u32[]{:S(2)}) %collective-permute-start.3) | collective-permute-done | bytes 4128 | tf_op jit(solution)/shard_map/ppermute | solution.py:18
  32.6 0.6 %collective-permute-done.4 = f32[8,128]{1,0:T(8,128)S(1)} collective-permute-done((f32[8,128]{1,0:T(8,128)S(1)}, f32[8,128]{1,0:T(8,128)S(1)}, u32[]{:S(2)}, u32[]{:S(2)}) %collective-permute-start.4) | collective-permute-done | bytes 4128 | tf_op jit(solution)/shard_map/ppermute | solution.py:18
  33.1 0.0 collective-permute-done.5
  33.1 1.0 %all-to-all-done.1 = bf16[32,8,512]{2,1,0:T(8,128)(2,1)S(1)} async-done(((bf16[32,8,512]{2,1,0:T(8,128)(2,1)}), bf16[32,8,512]{2,1,0:T(8,128)(2,1)S(1)}, u32[]{:S(2)}, u32[]{:S(2)}) %all-to-all-start.1) | async-done | bytes 262176 | tf_op jit(solution)/shard_map/all_to_all | solution.py:331
  34.2 0.0 copy-done
  34.2 0.0 copy-done.4
  34.2 1.3 %fusion.1 = bf16[32,8,512]{2,1,0:T(8,128)(2,1)} fusion(bf16[1,320,512]{2,1,0:T(8,128)(2,1)S(1)} %copy-done, bf16[1,512,320]{1,2,0:T(8,128)(2,1)S(1)} %copy-done.4, bf16[32,8,512]{2,1,0:T(8,128)(2,1)S(1)} %all-to-all-done.1), kind=kOutput, calls=%fused_computation.3 | convolution fusion | flops 168067072 | bytes 1179648 | tf_op jit(solution)/shard_map/dot_general | solution.py:338
  35.4 0.0 copy-start.5
  35.4 3.0 %all-to-all-start.2 = ((bf16[32,8,512]{2,1,0:T(8,128)(2,1)}), bf16[32,8,512]{2,1,0:T(8,128)(2,1)S(1)}, u32[]{:S(2)}, u32[]{:S(2)}) async-start(bf16[32,8,512]{2,1,0:T(8,128)(2,1)} %fusion.1), calls=%async_computation.2 | async-start | bytes 524288 | tf_op jit(solution)/shard_map/all_to_all | solution.py:344
  38.4 0.0 copy-done.5
  38.5 0.0 copy-start.6
  38.5 0.2 fusion.8
  38.6 0.6 %copy-done.6 = bf16[512,64]{0,1:T(8,128)(2,1)S(1)} copy-done((bf16[512,64]{0,1:T(8,128)(2,1)S(1)}, bf16[512,64]{0,1:T(8,128)(2,1)}, u32[]{:S(2)}) %copy-start.6) | copy-done | bytes 65560
  39.3 0.1 convolution_add_fusion
  39.4 0.3 collective-permute-start.6
  39.7 0.9 %collective-permute-done.6 = f32[8,512]{1,0:T(8,128)S(1)} collective-permute-done((f32[8,512]{1,0:T(8,128)S(1)}, f32[8,512]{1,0:T(8,128)S(1)}, u32[]{:S(2)}, u32[]{:S(2)}) %collective-permute-start.6) | collective-permute-done | bytes 16416 | tf_op jit(solution)/shard_map/ppermute | solution.py:23
  40.6 1.8 %collective-permute-start.7 = (f32[8,512]{1,0:T(8,128)S(1)}, f32[8,512]{1,0:T(8,128)S(1)}, u32[]{:S(2)}, u32[]{:S(2)}) collective-permute-start(f32[8,512]{1,0:T(8,128)S(1)} %add.25), channel_id=1, source_target_pairs={{0,2},{1,3},{2,0},{3,1},{4,6},{5,7},{6,4},{7,5},{8,10},{9,11},{10,... | collective-permute-start | bytes 49160 | tf_op jit(solution)/shard_map/ppermute | solution.py:23
  42.4 2.1 %collective-permute-done.7 = f32[8,512]{1,0:T(8,128)S(1)} collective-permute-done((f32[8,512]{1,0:T(8,128)S(1)}, f32[8,512]{1,0:T(8,128)S(1)}, u32[]{:S(2)}, u32[]{:S(2)}) %collective-permute-start.7) | collective-permute-done | bytes 16416 | tf_op jit(solution)/shard_map/ppermute | solution.py:23
  44.4 1.7 %collective-permute-start.8 = (f32[8,512]{1,0:T(8,128)S(1)}, f32[8,512]{1,0:T(8,128)S(1)}, u32[]{:S(2)}, u32[]{:S(2)}) collective-permute-start(f32[8,512]{1,0:T(8,128)S(1)} %add.26), channel_id=1, source_target_pairs={{0,4},{1,5},{2,6},{3,7},{4,0},{5,1},{6,2},{7,3},{8,12},{9,13},{10,... | collective-permute-start | bytes 49160 | tf_op jit(solution)/shard_map/ppermute | solution.py:23
  46.2 2.0 %collective-permute-done.8 = f32[8,512]{1,0:T(8,128)S(1)} collective-permute-done((f32[8,512]{1,0:T(8,128)S(1)}, f32[8,512]{1,0:T(8,128)S(1)}, u32[]{:S(2)}, u32[]{:S(2)}) %collective-permute-start.8) | collective-permute-done | bytes 16416 | tf_op jit(solution)/shard_map/ppermute | solution.py:23
  48.2 0.6 %add_convert_fusion = bf16[8,512]{1,0:T(8,128)(2,1)} fusion(f32[8,512]{1,0:T(8,128)S(1)} %add.26, f32[8,512]{1,0:T(8,128)S(1)} %collective-permute-done.8), kind=kLoop, calls=%fused_computation.9 | loop fusion | flops 8192 | bytes 40960 | tf_op jit(solution)/shard_map/convert_element_type | solution.py:360
  48.8 0.2 all-to-all-done.2
  49.0 0.9 %shard_map.127 = bf16[128,512]{1,0:T(8,128)(2,1)} custom-call(bf16[4,64,512]{2,1,0:T(8,128)(2,1)S(1)} %bitcast.23, s32[1,128]{1,0:T(1,128)S(1)} %get-tuple-element.29.target_ref, f32[128,512]{1,0:T(8,128)S(1)} %get-tuple-element.38.hidden_ref), custom_call_target="tpu_custom_call" | custom-call | tf_op jit(solution)/shard_map/pallas_call | solution.py:351
  (5 shorter events, 0.1 us)
Async XLA Ops:
  0.6 33.5 %copy-start = (bf16[1,320,512]{2,1,0:T(8,128)(2,1)S(1)}, bf16[1,320,512]{2,1,0:T(8,128)(2,1)}, u32[]{:S(2)}) copy-start(bf16[1,320,512]{2,1,0:T(8,128)(2,1)} %param.21) | copy-start | bytes 983044
  2.5 7.9 %collective-permute-start = (bf16[64,512]{1,0:T(8,128)(2,1)S(1)}, bf16[64,512]{1,0:T(8,128)(2,1)S(1)}, u32[]{:S(2)}, u32[]{:S(2)}) collective-permute-start(bf16[64,512]{1,0:T(8,128)(2,1)S(1)} %get-tuple-element.31), channel_id=1, source_target_pairs={{0,4},{1,5},{2,6},{3,7},{4,0},{5,1},{6,2},{7,3},{8,12},{9,13},{10,... | collective-permute-start | bytes 196616 | tf_op jit(solution)/shard_map/ppermute | solution.py:23
  5.5 12.3 %all-to-all-start = ((bf16[32,8,128]{2,1,0:T(8,128)(2,1)}), bf16[32,8,128]{2,1,0:T(8,128)(2,1)S(1)}, u32[]{:S(2)}, u32[]{:S(2)}) async-start(bf16[32,8,128]{2,1,0:T(8,128)(2,1)} %get-tuple-element.23), calls=%async_computation | async-start | bytes 131072 | tf_op jit(solution)/shard_map/all_to_all | solution.py:280
  10.5 4.6 %collective-permute-start.1 = (bf16[128,256]{1,0:T(8,128)(2,1)S(1)}, bf16[128,256]{1,0:T(8,128)(2,1)S(1)}, u32[]{:S(2)}, u32[]{:S(2)}) collective-permute-start(bf16[128,256]{1,0:T(8,128)(2,1)S(1)} %get-tuple-element.33), channel_id=1, source_target_pairs={{0,2},{1,3},{2,0},{3,1},{4,6},{5,7},{6,4},{7,5},{8,10},{9,11},{10,... | collective-permute-start | bytes 196616 | tf_op jit(solution)/shard_map/ppermute | solution.py:23
  15.1 2.9 %collective-permute-start.2 = (bf16[256,128]{1,0:T(8,128)(2,1)S(1)}, bf16[256,128]{1,0:T(8,128)(2,1)S(1)}, u32[]{:S(2)}, u32[]{:S(2)}) collective-permute-start(bf16[256,128]{1,0:T(8,128)(2,1)S(1)} %get-tuple-element.35), channel_id=1, source_target_pairs={{0,1},{1,0},{2,3},{3,2},{4,5},{5,4},{6,7},{7,6},{8,9},{9,8},{10,11... | collective-permute-start | bytes 196616 | tf_op jit(solution)/shard_map/ppermute | solution.py:23
  18.0 5.4 %copy-start.3 = (s32[1024]{0:T(1024)S(1)}, s32[1024]{0:T(1024)}, u32[]{:S(2)}) copy-start(s32[1024]{0:T(1024)} %lengths_ref.1) | copy-start | bytes 12292
  19.5 4.0 %copy-start.1 = (bf16[1024,64]{0,1:T(8,128)(2,1)S(1)}, bf16[1024,64]{0,1:T(8,128)(2,1)}, u32[]{:S(2)}) copy-start(bf16[1024,64]{0,1:T(8,128)(2,1)} %param.14) | copy-start | bytes 393220
  19.5 4.0 %copy-start.2 = (bf16[1024,64]{0,1:T(8,128)(2,1)S(1)}, bf16[1024,64]{0,1:T(8,128)(2,1)}, u32[]{:S(2)}) copy-start(bf16[1024,64]{0,1:T(8,128)(2,1)} %param.16) | copy-start | bytes 393220
  19.5 14.7 %copy-start.4 = (bf16[1,512,320]{1,2,0:T(8,128)(2,1)S(1)}, bf16[1,512,320]{1,2,0:T(8,128)(2,1)}, u32[]{:S(2)}) copy-start(bf16[1,512,320]{1,2,0:T(8,128)(2,1)} %param.20) | copy-start | bytes 983044
  19.5 14.7 %all-to-all-start.1 = ((bf16[32,8,512]{2,1,0:T(8,128)(2,1)}), bf16[32,8,512]{2,1,0:T(8,128)(2,1)S(1)}, u32[]{:S(2)}, u32[]{:S(2)}) async-start(bf16[32,8,512]{2,1,0:T(8,128)(2,1)} %bitcast.5), calls=%async_computation.1 | async-start | bytes 524288 | tf_op jit(solution)/shard_map/all_to_all | solution.py:331
  23.9 8.7 %collective-permute-start.3 = (f32[8,128]{1,0:T(8,128)S(1)}, f32[8,128]{1,0:T(8,128)S(1)}, u32[]{:S(2)}, u32[]{:S(2)}) collective-permute-start(f32[8,128]{1,0:T(8,128)S(1)} %get-tuple-element.41), channel_id=1, source_target_pairs={{0,8},{8,16},{16,24},{24,0},{1,9},{9,17},{17,25},{25,1},{2,10},{10... | collective-permute-start | bytes 12296 | tf_op jit(solution)/shard_map/ppermute | solution.py:18
  25.7 7.4 %collective-permute-start.4 = (f32[8,128]{1,0:T(8,128)S(1)}, f32[8,128]{1,0:T(8,128)S(1)}, u32[]{:S(2)}, u32[]{:S(2)}) collective-permute-start(f32[8,128]{1,0:T(8,128)S(1)} %get-tuple-element.42), channel_id=1, source_target_pairs={{0,16},{8,24},{16,0},{24,8},{1,17},{9,25},{17,1},{25,9},{2,18},{10... | collective-permute-start | bytes 12296 | tf_op jit(solution)/shard_map/ppermute | solution.py:18
  28.1 5.0 %collective-permute-start.5 = (f32[8,128]{1,0:T(8,128)S(1)}, f32[8,128]{1,0:T(8,128)S(1)}, u32[]{:S(2)}, u32[]{:S(2)}) collective-permute-start(f32[8,128]{1,0:T(8,128)S(1)} %get-tuple-element.43), channel_id=1, source_target_pairs={{0,24},{8,0},{16,8},{24,16},{1,25},{9,1},{17,9},{25,17},{2,26},{10... | collective-permute-start | bytes 12296 | tf_op jit(solution)/shard_map/ppermute | solution.py:18
  35.4 3.0 %copy-start.5 = (bf16[512,64]{0,1:T(8,128)(2,1)S(1)}, bf16[512,64]{0,1:T(8,128)(2,1)}, u32[]{:S(2)}) copy-start(bf16[512,64]{0,1:T(8,128)(2,1)} %param.13) | copy-start | bytes 196612
  35.4 13.6 %all-to-all-start.2 = ((bf16[32,8,512]{2,1,0:T(8,128)(2,1)}), bf16[32,8,512]{2,1,0:T(8,128)(2,1)S(1)}, u32[]{:S(2)}, u32[]{:S(2)}) async-start(bf16[32,8,512]{2,1,0:T(8,128)(2,1)} %fusion.1), calls=%async_computation.2 | async-start | bytes 524288 | tf_op jit(solution)/shard_map/all_to_all | solution.py:344
  38.5 0.8 %copy-start.6 = (bf16[512,64]{0,1:T(8,128)(2,1)S(1)}, bf16[512,64]{0,1:T(8,128)(2,1)}, u32[]{:S(2)}) copy-start(bf16[512,64]{0,1:T(8,128)(2,1)} %param.12) | copy-start | bytes 196612
  39.4 1.2 %collective-permute-start.6 = (f32[8,512]{1,0:T(8,128)S(1)}, f32[8,512]{1,0:T(8,128)S(1)}, u32[]{:S(2)}, u32[]{:S(2)}) collective-permute-start(f32[8,512]{1,0:T(8,128)S(1)} %convolution_add_fusion), channel_id=1, source_target_pairs={{0,1},{1,0},{2,3},{3,2},{4,5},{5,4},{6,7},{7,6},{8,9},{9,8},{10,11... | collective-permute-start | bytes 49160 | tf_op jit(solution)/shard_map/ppermute | solution.py:23
  40.6 3.8 %collective-permute-start.7 = (f32[8,512]{1,0:T(8,128)S(1)}, f32[8,512]{1,0:T(8,128)S(1)}, u32[]{:S(2)}, u32[]{:S(2)}) collective-permute-start(f32[8,512]{1,0:T(8,128)S(1)} %add.25), channel_id=1, source_target_pairs={{0,2},{1,3},{2,0},{3,1},{4,6},{5,7},{6,4},{7,5},{8,10},{9,11},{10,... | collective-permute-start | bytes 49160 | tf_op jit(solution)/shard_map/ppermute | solution.py:23
  44.4 3.7 %collective-permute-start.8 = (f32[8,512]{1,0:T(8,128)S(1)}, f32[8,512]{1,0:T(8,128)S(1)}, u32[]{:S(2)}, u32[]{:S(2)}) collective-permute-start(f32[8,512]{1,0:T(8,128)S(1)} %add.26), channel_id=1, source_target_pairs={{0,4},{1,5},{2,6},{3,7},{4,0},{5,1},{6,2},{7,3},{8,12},{9,13},{10,... | collective-permute-start | bytes 49160 | tf_op jit(solution)/shard_map/ppermute | solution.py:23

commit v3 on v2

--- a/solution.py
+++ b/solution.py
@@ -21,12 +21,6 @@
 def crossed(value, bit):
     size = lax.axis_size("expert")
     return lax.ppermute(value, "expert", [(i, i ^ bit) for i in range(size)])
-
-
-def pick_half(ref, bit, mine):
-    half = ref.shape[1] // 2
-    side = lax.rem(lax.axis_index("expert") // bit, 2)
-    return ref[:, pl.ds(pl.multiple_of((side if mine else 1 - side) * half, half), half)]
 
 
 def project_kernel(
@@ -70,8 +64,11 @@
     leave.start()
     for fetch in fetches[3:]:
         fetch.wait()
-    keep_ref[...] = pick_half(queries_ref, experts // 2, True)
-    send_ref[...] = pick_half(queries_ref, experts // 2, False)
+    core = lax.rem(here, 2)
+    for chip in range(experts // 2):
+        for ref, which in ((keep_ref, core), (send_ref, 1 - core)):
+            lanes = pl.ds(pl.multiple_of((2 * chip + which) * tok_dev, tok_dev), tok_dev)
+            ref[chip] = queries_ref[:, lanes]
     routes = routes_ref[...]
     onehot = lax.broadcasted_iota(jnp.int32, (experts, tok_dev), 0) == routes
     earlier = lax.broadcasted_iota(jnp.int32, (tok_dev, tok_dev), 0) < lax.broadcasted_iota(
@@ -85,11 +82,12 @@
     leave.wait()
 
 
-def split_kernel(bit, kept_ref, got_ref, keep_ref, send_ref):
-    rows = kept_ref.shape[0]
-    for first, ref in ((0, kept_ref), (rows, got_ref)):
-        keep_ref[first : first + rows] = pick_half(ref, bit, True)
-        send_ref[first : first + rows] = pick_half(ref, bit, False)
+def gather_kernel(keep_ref, got_ref, *out_refs):
+    chip = lax.axis_index("expert") // 2
+    head = keep_ref.shape[1]
+    for k, out_ref in enumerate(out_refs):
+        out_ref[:head] = keep_ref[lax.bitwise_xor(chip, k)]
+        out_ref[head:] = got_ref[lax.bitwise_xor(chip, k)]
 
 
 def block_kernel(group, kv_ref, keys_ref, values_ref):
@@ -111,32 +109,18 @@
 
 
 def attend_kernel(
-    scale,
-    enc_dev,
-    head,
-    keys_ref,
-    values_ref,
-    lengths_ref,
-    residual_ref,
-    gain_ref,
-    target_ref,
-    kept_ref,
-    got_ref,
-    hidden_ref,
-    out_ref,
-    q_ref,
+    scale, enc_dev, head, keys_ref, values_ref, lengths_ref, residual_ref, gain_ref, target_ref, *refs
 ):
     parts, rows, cols = keys_ref.shape
     group, heads = cols // head, parts * cols // head
+    *query_refs, hidden_ref, out_ref, q_ref = refs
     pipes, tok_dev = rows // (group * enc_dev), q_ref.shape[1]
     f32, bf16 = jnp.float32, jnp.bfloat16
     here = lax.axis_index("expert")
-    levels = heads.bit_length() - 1
-    for r in range(heads):
-        flips = sum(1 << (levels - 1 - i) for i in range(levels) if r >> i & 1)
-        which = pl.multiple_of(lax.bitwise_xor(here, flips) * head, head)
-        ref, first = (kept_ref, r) if r < heads // 2 else (got_ref, r - heads // 2)
-        q_ref[pl.ds(which, head)] = ref[first * head : (first + 1) * head]
+    for k, ref in zip((0, *range(len(query_refs) - 1, 0, -1)), query_refs, strict=True):
+        for i in range(2):
+            which = pl.multiple_of(lax.bitwise_xor(here, 2 * k + i) * head, head)
+            q_ref[pl.ds(which, head)] = ref[i * head : (i + 1) * head]
     shape = (pipes, group, enc_dev, tok_dev)
     position = lax.broadcasted_iota(jnp.int32, shape, 0) * enc_dev + lax.broadcasted_iota(
         jnp.int32, shape, 2
@@ -237,7 +221,7 @@
     here, own_pipe = lax.axis_index("expert"), lax.axis_index("pipe")
     params = pltpu.CompilerParams(vmem_limit_bytes=(8 << 20) if model <= 1024 else (40 << 20))
     queries_turned = queries.T
-    half = (head, experts * tok_dev // 2)
+    half = (experts // 2, head, tok_dev)
     spread_kv, keep, send, own_lengths, gain, target, near_residual = pl.pallas_call(
         functools.partial(project_kernel, cap),
         out_shape=[
@@ -280,19 +264,16 @@
     kv = lax.all_to_all(
         spread_kv, EVERYONE, split_axis=0, concat_axis=0, tiled=True
     ).reshape(pipes, experts, enc_dev, 2 * head)
-    bit = experts // 2
-    got = crossed(send, bit)
-    while bit > 1:
-        bit //= 2
-        keep, send = pl.pallas_call(
-            functools.partial(split_kernel, bit),
-            out_shape=[jax.ShapeDtypeStruct((2 * keep.shape[0], keep.shape[1] // 2), bf16)] * 2,
-            in_specs=[VMEM] * 2,
-            out_specs=[VMEM] * 2,
-            compiler_params=params,
-            cost_estimate=pl.CostEstimate(flops=0, bytes_accessed=0, transcendentals=0),
-        )(keep, got)
-        got = crossed(send, bit)
+    chips = experts // 2
+    query_blocks = pl.pallas_call(
+        gather_kernel,
+        out_shape=[jax.ShapeDtypeStruct((2 * head, tok_dev), bf16)] * chips,
+        in_specs=[VMEM] * 2,
+        out_specs=[VMEM] * chips,
+        compiler_params=params,
+        cost_estimate=pl.CostEstimate(flops=1 << 34, bytes_accessed=1 << 26, transcendentals=0),
+    )(keep, crossed(send, 1))
+    query_blocks = [query_blocks[0]] + [crossed(query_blocks[k], 2 * k) for k in range(1, chips)]
     group = max(g for g in range(2, experts + 1, 2) if experts % g == 0 and g * head <= 512)
     blocks = (experts // group, pipes * group * enc_dev, group * head)
     key_blocks, value_blocks = pl.pallas_call(
@@ -309,11 +290,11 @@
             jax.ShapeDtypeStruct((tok_dev, model), f32),
             jax.ShapeDtypeStruct((pipes, experts * cap, model), bf16),
         ),
-        in_specs=[VMEM] * 8,
+        in_specs=[VMEM] * (6 + chips),
         out_specs=[VMEM] * 2,
         scratch_shapes=[pltpu.VMEM((model, tok_dev), bf16)],
         compiler_params=params,
-    )(key_blocks, value_blocks, own_lengths, near_residual, gain, target, keep, got)
+    )(key_blocks, value_blocks, own_lengths, near_residual, gain, target, query_blocks[0], *query_blocks[:0:-1])
     outgoing = outgoing.reshape(pipes * experts, cap, model)
     kv, outgoing = lax.optimization_barrier((kv, outgoing))
     total, *others = pl.pallas_call(

time: 50.3 us -> 50.2 us (level)
  waiting for transfers between devices: 15.3 us -> 13.7 us
  starting transfers between devices: 26.2 us -> 27.7 us
    ppermute x6 -> x7, waiting for transfers between devices: 7.74 us -> 5 us  [crossed(): return lax.ppermute(value, 'expert', [(i, i ^ bit) for i in range(size)])]
    all_to_all x1, starting transfers between devices: 4.89 us -> 6.96 us  [per_device(): lax.all_to_all(spread_kv, EVERYONE, split_axis=0, concat_axis=0, tiled=True)]
    all_to_all x1, waiting for transfers between devices: 2.68 us -> 3.81 us  [per_device(): lax.all_to_all(spread_kv, EVERYONE, split_axis=0, concat_axis=0, tiled=True)]
    ppermute x6 -> x7, starting transfers between devices: 8.7 us -> 7.84 us  [crossed(): return lax.ppermute(value, 'expert', [(i, i ^ bit) for i in range(size)])]
  transfers between devices with their start and end apart: 12 -> 13, of which waited for: 9 -> 8; matrix products, arithmetic and copies ran while one was open for 2% -> 2% of each run, Pallas kernels for 1% -> 1%
where the time goes in v3:
time: 50.2 us; the launch traced here: 49.8 us
  starting transfers between devices  27.7 us (55%)
  waiting for transfers between devices  13.7 us (27%)
  Pallas kernels  4.73 us (9%)
  matrix products  1.56 us (3%)
  between operations  0.79 us (2%)
  local copies, waits for them, and re-layouts  0.68 us (1%)
  other arithmetic  0.62 us (1%)
    ppermute x7, starting transfers between devices, crossed(): return lax.ppermute(value, 'expert', [(i, i ^ bit) for i in range(size)])  7.84 us
    all_to_all x1, starting transfers between devices, per_device(): lax.all_to_all(spread_kv, EVERYONE, split_axis=0, concat_axis=0, tiled=True)  6.96 us
    ppermute x3, starting transfers between devices, shifted(): lax.ppermute(value, axis, [(i, (i + step) % size) for i in range(size)])  5.66 us
    ppermute x7, waiting for transfers between devices, crossed(): return lax.ppermute(value, 'expert', [(i, i ^ bit) for i in range(size)])  5 us
    all_to_all x1, starting transfers between devices, per_device(): lax.all_to_all(outgoing, EVERYONE, split_axis=0, concat_axis=0, tiled=True)  4.28 us
    all_to_all x1, waiting for transfers between devices, per_device(): lax.all_to_all(spread_kv, EVERYONE, split_axis=0, concat_axis=0, tiled=True)  3.81 us
    ppermute x3, waiting for transfers between devices, shifted(): lax.ppermute(value, axis, [(i, (i + step) % size) for i in range(size)])  3.59 us
    all_to_all x1, starting transfers between devices, per_device(): lax.all_to_all(part.reshape(pipes * experts, cap, model), EVERYONE, split...  3.01 us
  transfers between devices with their start and end apart: 13, of which 8 were waited for; matrix products, arithmetic and copies ran while one was open for 2% of the time, Pallas kernels for 1%

profile of v3, /device:TPU:0, one launch (start us, length us, event | category | flops | bytes accessed | tf_op | source)
XLA Modules:
  0.0 49.8 jit_solution(7071902429335270633)
XLA Ops:
  0.6 0.0 copy-start
  0.6 1.9 %shard_map.122 = (bf16[32,8,128]{2,1,0:T(8,128)(2,1)}, bf16[4,64,128]{2,1,0:T(8,128)(2,1)S(1)}, bf16[4,64,128]{2,1,0:T(8,128)(2,1)S(1)}, s32[128]{0:T(128)S(1)},...) custom-call(bf16[8,512]{1,0:T(8,128)(2,1)} %enc_hbm.1, bf16[64,512]{1,0:T(8,128)(2,1)} %bitcast.30, ...), custom_call_target="tpu_custom_call" | custom-call | tf_op jit(solution)/shard_map/pallas_call | solution.py:225
  2.5 0.5 %collective-permute-start = (bf16[4,64,128]{2,1,0:T(8,128)(2,1)S(1)}, bf16[4,64,128]{2,1,0:T(8,128)(2,1)S(1)}, u32[]{:S(2)}, u32[]{:S(2)}) collective-permute-start(bf16[4,64,128]{2,1,0:T(8,128)(2,1)S(1)} %get-tuple-element.31), channel_id=1, source_target_pairs={{0,1},{1,0},{2,3},{3,2},{4,5},{5,4},{6,7},{7,6},{8,9},{9,8},{10,11... | collective-permute-start | bytes 196616 | tf_op jit(solution)/shard_map/ppermute | solution.py:23
  3.0 7.0 %all-to-all-start = ((bf16[32,8,128]{2,1,0:T(8,128)(2,1)}), bf16[32,8,128]{2,1,0:T(8,128)(2,1)S(1)}, u32[]{:S(2)}, u32[]{:S(2)}) async-start(bf16[32,8,128]{2,1,0:T(8,128)(2,1)} %get-tuple-element.23), calls=%async_computation | async-start | bytes 131072 | tf_op jit(solution)/shard_map/all_to_all | solution.py:264
  10.0 0.0 collective-permute-done.got_ref
  10.0 2.7 %collective-permute-start.1 = (bf16[128,128]{1,0:T(8,128)(2,1)S(1)}, bf16[128,128]{1,0:T(8,128)(2,1)S(1)}, u32[]{:S(2)}, u32[]{:S(2)}) collective-permute-start(bf16[128,128]{1,0:T(8,128)(2,1)S(1)} %get-tuple-element.33), channel_id=1, source_target_pairs={{0,6},{1,7},{2,4},{3,5},{4,2},{5,3},{6,0},{7,1},{8,14},{9,15},{10,... | collective-permute-start | bytes 98312 | tf_op jit(solution)/shard_map/ppermute | solution.py:23
  12.8 0.6 %collective-permute-start.2 = (bf16[128,128]{1,0:T(8,128)(2,1)S(1)}, bf16[128,128]{1,0:T(8,128)(2,1)S(1)}, u32[]{:S(2)}, u32[]{:S(2)}) collective-permute-start(bf16[128,128]{1,0:T(8,128)(2,1)S(1)} %get-tuple-element.34), channel_id=1, source_target_pairs={{0,4},{1,5},{2,6},{3,7},{4,0},{5,1},{6,2},{7,3},{8,12},{9,13},{10,... | collective-permute-start | bytes 98312 | tf_op jit(solution)/shard_map/ppermute | solution.py:23
  13.3 0.3 collective-permute-start.3
  13.6 3.8 %all-to-all-done = bf16[32,8,128]{2,1,0:T(8,128)(2,1)S(1)} async-done(((bf16[32,8,128]{2,1,0:T(8,128)(2,1)}), bf16[32,8,128]{2,1,0:T(8,128)(2,1)S(1)}, u32[]{:S(2)}, u32[]{:S(2)}) %all-to-all-start) | async-done | bytes 65568 | tf_op jit(solution)/shard_map/all_to_all | solution.py:264
  17.4 0.1 shard_map.123
  17.6 0.0 collective-permute-done.1.refs_1_
  17.6 0.0 collective-permute-done.2.refs_2_
  17.6 0.0 collective-permute-done.3.refs_3_
  17.6 0.0 copy-start.3
  17.6 1.4 %shard_map.125 = (f32[128,512]{1,0:T(8,128)S(1)}, bf16[4,64,512]{2,1,0:T(8,128)(2,1)}) custom-call(bf16[1,256,512]{2,1,0:T(8,128)(2,1)S(1)} %get-tuple-element.24.keys_ref, bf16[1,256,512]{2,1,0:T(8,128)(2,1)S(1)} %get-tuple-element.25.values_ref, s32[128]{0:T(128)S(1)} %get-tuple-element.26.lengths_ref, ...), custom_call_target="tpu_custom_call" | custom-call | tf_op jit(solution)/shard_map/pallas_call | solution.py:287
  19.0 0.0 copy-start.1
  19.0 0.0 copy-start.2
  19.0 0.0 copy-start.4
  19.0 4.3 %all-to-all-start.1 = ((bf16[32,8,512]{2,1,0:T(8,128)(2,1)}), bf16[32,8,512]{2,1,0:T(8,128)(2,1)S(1)}, u32[]{:S(2)}, u32[]{:S(2)}) async-start(bf16[32,8,512]{2,1,0:T(8,128)(2,1)} %bitcast.5), calls=%async_computation.1 | async-start | bytes 524288 | tf_op jit(solution)/shard_map/all_to_all | solution.py:312
  23.3 0.0 copy-done.3
  23.3 0.0 copy-done.1
  23.3 0.0 copy-done.2
  23.4 0.4 shard_map.127
  23.8 1.8 %collective-permute-start.4 = (f32[8,128]{1,0:T(8,128)S(1)}, f32[8,128]{1,0:T(8,128)S(1)}, u32[]{:S(2)}, u32[]{:S(2)}) collective-permute-start(f32[8,128]{1,0:T(8,128)S(1)} %get-tuple-element.41), channel_id=1, source_target_pairs={{0,8},{8,16},{16,24},{24,0},{1,9},{9,17},{17,25},{25,1},{2,10},{10... | collective-permute-start | bytes 12296 | tf_op jit(solution)/shard_map/ppermute | solution.py:18
  25.6 2.4 %collective-permute-start.5 = (f32[8,128]{1,0:T(8,128)S(1)}, f32[8,128]{1,0:T(8,128)S(1)}, u32[]{:S(2)}, u32[]{:S(2)}) collective-permute-start(f32[8,128]{1,0:T(8,128)S(1)} %get-tuple-element.42), channel_id=1, source_target_pairs={{0,16},{8,24},{16,0},{24,8},{1,17},{9,25},{17,1},{25,9},{2,18},{10... | collective-permute-start | bytes 12296 | tf_op jit(solution)/shard_map/ppermute | solution.py:18
  28.0 1.4 %collective-permute-start.6 = (f32[8,128]{1,0:T(8,128)S(1)}, f32[8,128]{1,0:T(8,128)S(1)}, u32[]{:S(2)}, u32[]{:S(2)}) collective-permute-start(f32[8,128]{1,0:T(8,128)S(1)} %get-tuple-element.43), channel_id=1, source_target_pairs={{0,24},{8,0},{16,8},{24,16},{1,25},{9,1},{17,9},{25,17},{2,26},{10... | collective-permute-start | bytes 12296 | tf_op jit(solution)/shard_map/ppermute | solution.py:18
  29.4 3.0 %collective-permute-done.4 = f32[8,128]{1,0:T(8,128)S(1)} collective-permute-done((f32[8,128]{1,0:T(8,128)S(1)}, f32[8,128]{1,0:T(8,128)S(1)}, u32[]{:S(2)}, u32[]{:S(2)}) %collective-permute-start.4) | collective-permute-done | bytes 4128 | tf_op jit(solution)/shard_map/ppermute | solution.py:18
  32.4 0.6 %collective-permute-done.5 = f32[8,128]{1,0:T(8,128)S(1)} collective-permute-done((f32[8,128]{1,0:T(8,128)S(1)}, f32[8,128]{1,0:T(8,128)S(1)}, u32[]{:S(2)}, u32[]{:S(2)}) %collective-permute-start.5) | collective-permute-done | bytes 4128 | tf_op jit(solution)/shard_map/ppermute | solution.py:18
  33.0 0.0 collective-permute-done.6
  33.0 1.0 %all-to-all-done.1 = bf16[32,8,512]{2,1,0:T(8,128)(2,1)S(1)} async-done(((bf16[32,8,512]{2,1,0:T(8,128)(2,1)}), bf16[32,8,512]{2,1,0:T(8,128)(2,1)S(1)}, u32[]{:S(2)}, u32[]{:S(2)}) %all-to-all-start.1) | async-done | bytes 262176 | tf_op jit(solution)/shard_map/all_to_all | solution.py:312
  34.0 0.0 copy-done
  34.1 0.0 copy-done.4
  34.1 1.3 %fusion.1 = bf16[32,8,512]{2,1,0:T(8,128)(2,1)} fusion(bf16[1,320,512]{2,1,0:T(8,128)(2,1)S(1)} %copy-done, bf16[1,512,320]{1,2,0:T(8,128)(2,1)S(1)} %copy-done.4, bf16[32,8,512]{2,1,0:T(8,128)(2,1)S(1)} %all-to-all-done.1), kind=kOutput, calls=%fused_computation.3 | convolution fusion | flops 168067072 | bytes 1179648 | tf_op jit(solution)/shard_map/dot_general | solution.py:319
  35.3 3.0 %all-to-all-start.2 = ((bf16[32,8,512]{2,1,0:T(8,128)(2,1)}), bf16[32,8,512]{2,1,0:T(8,128)(2,1)S(1)}, u32[]{:S(2)}, u32[]{:S(2)}) async-start(bf16[32,8,512]{2,1,0:T(8,128)(2,1)} %fusion.1), calls=%async_computation.2 | async-start | bytes 524288 | tf_op jit(solution)/shard_map/all_to_all | solution.py:325
  38.3 0.0 copy-done.5
  38.3 0.0 copy-start.6
  38.3 0.2 fusion.8
  38.5 0.6 %copy-done.6 = bf16[512,64]{0,1:T(8,128)(2,1)S(1)} copy-done((bf16[512,64]{0,1:T(8,128)(2,1)S(1)}, bf16[512,64]{0,1:T(8,128)(2,1)}, u32[]{:S(2)}) %copy-start.6) | copy-done | bytes 65560
  39.2 0.1 convolution_add_fusion
  39.3 0.3 collective-permute-start.7
  39.6 0.9 %collective-permute-done.7 = f32[8,512]{1,0:T(8,128)S(1)} collective-permute-done((f32[8,512]{1,0:T(8,128)S(1)}, f32[8,512]{1,0:T(8,128)S(1)}, u32[]{:S(2)}, u32[]{:S(2)}) %collective-permute-start.7) | collective-permute-done | bytes 16416 | tf_op jit(solution)/shard_map/ppermute | solution.py:23
  40.5 1.8 %collective-permute-start.8 = (f32[8,512]{1,0:T(8,128)S(1)}, f32[8,512]{1,0:T(8,128)S(1)}, u32[]{:S(2)}, u32[]{:S(2)}) collective-permute-start(f32[8,512]{1,0:T(8,128)S(1)} %add.25), channel_id=1, source_target_pairs={{0,2},{1,3},{2,0},{3,1},{4,6},{5,7},{6,4},{7,5},{8,10},{9,11},{10,... | collective-permute-start | bytes 49160 | tf_op jit(solution)/shard_map/ppermute | solution.py:23
  42.3 2.1 %collective-permute-done.8 = f32[8,512]{1,0:T(8,128)S(1)} collective-permute-done((f32[8,512]{1,0:T(8,128)S(1)}, f32[8,512]{1,0:T(8,128)S(1)}, u32[]{:S(2)}, u32[]{:S(2)}) %collective-permute-start.8) | collective-permute-done | bytes 16416 | tf_op jit(solution)/shard_map/ppermute | solution.py:23
  44.3 1.7 %collective-permute-start.9 = (f32[8,512]{1,0:T(8,128)S(1)}, f32[8,512]{1,0:T(8,128)S(1)}, u32[]{:S(2)}, u32[]{:S(2)}) collective-permute-start(f32[8,512]{1,0:T(8,128)S(1)} %add.26), channel_id=1, source_target_pairs={{0,4},{1,5},{2,6},{3,7},{4,0},{5,1},{6,2},{7,3},{8,12},{9,13},{10,... | collective-permute-start | bytes 49160 | tf_op jit(solution)/shard_map/ppermute | solution.py:23
  46.1 2.0 %collective-permute-done.9 = f32[8,512]{1,0:T(8,128)S(1)} collective-permute-done((f32[8,512]{1,0:T(8,128)S(1)}, f32[8,512]{1,0:T(8,128)S(1)}, u32[]{:S(2)}, u32[]{:S(2)}) %collective-permute-start.9) | collective-permute-done | bytes 16416 | tf_op jit(solution)/shard_map/ppermute | solution.py:23
  48.1 0.6 %add_convert_fusion = bf16[8,512]{1,0:T(8,128)(2,1)} fusion(f32[8,512]{1,0:T(8,128)S(1)} %add.26, f32[8,512]{1,0:T(8,128)S(1)} %collective-permute-done.9), kind=kLoop, calls=%fused_computation.9 | loop fusion | flops 8192 | bytes 40960 | tf_op jit(solution)/shard_map/convert_element_type | solution.py:341
  48.7 0.2 all-to-all-done.2
  48.9 0.9 %shard_map.126 = bf16[128,512]{1,0:T(8,128)(2,1)} custom-call(bf16[4,64,512]{2,1,0:T(8,128)(2,1)S(1)} %bitcast.23, s32[1,128]{1,0:T(1,128)S(1)} %get-tuple-element.29.target_ref, f32[128,512]{1,0:T(8,128)S(1)} %get-tuple-element.38.hidden_ref), custom_call_target="tpu_custom_call" | custom-call | tf_op jit(solution)/shard_map/pallas_call | solution.py:332
  (5 shorter events, 0.0 us)
Async XLA Ops:
  0.6 33.4 %copy-start = (bf16[1,320,512]{2,1,0:T(8,128)(2,1)S(1)}, bf16[1,320,512]{2,1,0:T(8,128)(2,1)}, u32[]{:S(2)}) copy-start(bf16[1,320,512]{2,1,0:T(8,128)(2,1)} %param.21) | copy-start | bytes 983044
  2.5 7.5 %collective-permute-start = (bf16[4,64,128]{2,1,0:T(8,128)(2,1)S(1)}, bf16[4,64,128]{2,1,0:T(8,128)(2,1)S(1)}, u32[]{:S(2)}, u32[]{:S(2)}) collective-permute-start(bf16[4,64,128]{2,1,0:T(8,128)(2,1)S(1)} %get-tuple-element.31), channel_id=1, source_target_pairs={{0,1},{1,0},{2,3},{3,2},{4,5},{5,4},{6,7},{7,6},{8,9},{9,8},{10,11... | collective-permute-start | bytes 196616 | tf_op jit(solution)/shard_map/ppermute | solution.py:23
  3.0 14.4 %all-to-all-start = ((bf16[32,8,128]{2,1,0:T(8,128)(2,1)}), bf16[32,8,128]{2,1,0:T(8,128)(2,1)S(1)}, u32[]{:S(2)}, u32[]{:S(2)}) async-start(bf16[32,8,128]{2,1,0:T(8,128)(2,1)} %get-tuple-element.23), calls=%async_computation | async-start | bytes 131072 | tf_op jit(solution)/shard_map/all_to_all | solution.py:264
  10.0 7.5 %collective-permute-start.1 = (bf16[128,128]{1,0:T(8,128)(2,1)S(1)}, bf16[128,128]{1,0:T(8,128)(2,1)S(1)}, u32[]{:S(2)}, u32[]{:S(2)}) collective-permute-start(bf16[128,128]{1,0:T(8,128)(2,1)S(1)} %get-tuple-element.33), channel_id=1, source_target_pairs={{0,6},{1,7},{2,4},{3,5},{4,2},{5,3},{6,0},{7,1},{8,14},{9,15},{10,... | collective-permute-start | bytes 98312 | tf_op jit(solution)/shard_map/ppermute | solution.py:23
  12.8 4.8 %collective-permute-start.2 = (bf16[128,128]{1,0:T(8,128)(2,1)S(1)}, bf16[128,128]{1,0:T(8,128)(2,1)S(1)}, u32[]{:S(2)}, u32[]{:S(2)}) collective-permute-start(bf16[128,128]{1,0:T(8,128)(2,1)S(1)} %get-tuple-element.34), channel_id=1, source_target_pairs={{0,4},{1,5},{2,6},{3,7},{4,0},{5,1},{6,2},{7,3},{8,12},{9,13},{10,... | collective-permute-start | bytes 98312 | tf_op jit(solution)/shard_map/ppermute | solution.py:23
  13.3 4.2 %collective-permute-start.3 = (bf16[128,128]{1,0:T(8,128)(2,1)S(1)}, bf16[128,128]{1,0:T(8,128)(2,1)S(1)}, u32[]{:S(2)}, u32[]{:S(2)}) collective-permute-start(bf16[128,128]{1,0:T(8,128)(2,1)S(1)} %get-tuple-element.35), channel_id=1, source_target_pairs={{0,2},{1,3},{2,0},{3,1},{4,6},{5,7},{6,4},{7,5},{8,10},{9,11},{10,... | collective-permute-start | bytes 98312 | tf_op jit(solution)/shard_map/ppermute | solution.py:23
  17.6 5.7 %copy-start.3 = (s32[1024]{0:T(1024)S(1)}, s32[1024]{0:T(1024)}, u32[]{:S(2)}) copy-start(s32[1024]{0:T(1024)} %lengths_ref.1) | copy-start | bytes 12292
  19.0 4.3 %copy-start.1 = (bf16[1024,64]{0,1:T(8,128)(2,1)S(1)}, bf16[1024,64]{0,1:T(8,128)(2,1)}, u32[]{:S(2)}) copy-start(bf16[1024,64]{0,1:T(8,128)(2,1)} %param.14) | copy-start | bytes 393220
  19.0 4.3 %copy-start.2 = (bf16[1024,64]{0,1:T(8,128)(2,1)S(1)}, bf16[1024,64]{0,1:T(8,128)(2,1)}, u32[]{:S(2)}) copy-start(bf16[1024,64]{0,1:T(8,128)(2,1)} %param.16) | copy-start | bytes 393220
  19.0 15.0 %copy-start.4 = (bf16[1,512,320]{1,2,0:T(8,128)(2,1)S(1)}, bf16[1,512,320]{1,2,0:T(8,128)(2,1)}, u32[]{:S(2)}) copy-start(bf16[1,512,320]{1,2,0:T(8,128)(2,1)} %param.20) | copy-start | bytes 983044
  19.0 15.0 %all-to-all-start.1 = ((bf16[32,8,512]{2,1,0:T(8,128)(2,1)}), bf16[32,8,512]{2,1,0:T(8,128)(2,1)S(1)}, u32[]{:S(2)}, u32[]{:S(2)}) async-start(bf16[32,8,512]{2,1,0:T(8,128)(2,1)} %bitcast.5), calls=%async_computation.1 | async-start | bytes 524288 | tf_op jit(solution)/shard_map/all_to_all | solution.py:312
  23.8 8.7 %collective-permute-start.4 = (f32[8,128]{1,0:T(8,128)S(1)}, f32[8,128]{1,0:T(8,128)S(1)}, u32[]{:S(2)}, u32[]{:S(2)}) collective-permute-start(f32[8,128]{1,0:T(8,128)S(1)} %get-tuple-element.41), channel_id=1, source_target_pairs={{0,8},{8,16},{16,24},{24,0},{1,9},{9,17},{17,25},{25,1},{2,10},{10... | collective-permute-start | bytes 12296 | tf_op jit(solution)/shard_map/ppermute | solution.py:18
  25.6 7.4 %collective-permute-start.5 = (f32[8,128]{1,0:T(8,128)S(1)}, f32[8,128]{1,0:T(8,128)S(1)}, u32[]{:S(2)}, u32[]{:S(2)}) collective-permute-start(f32[8,128]{1,0:T(8,128)S(1)} %get-tuple-element.42), channel_id=1, source_target_pairs={{0,16},{8,24},{16,0},{24,8},{1,17},{9,25},{17,1},{25,9},{2,18},{10... | collective-permute-start | bytes 12296 | tf_op jit(solution)/shard_map/ppermute | solution.py:18
  28.0 5.0 %collective-permute-start.6 = (f32[8,128]{1,0:T(8,128)S(1)}, f32[8,128]{1,0:T(8,128)S(1)}, u32[]{:S(2)}, u32[]{:S(2)}) collective-permute-start(f32[8,128]{1,0:T(8,128)S(1)} %get-tuple-element.43), channel_id=1, source_target_pairs={{0,24},{8,0},{16,8},{24,16},{1,25},{9,1},{17,9},{25,17},{2,26},{10... | collective-permute-start | bytes 12296 | tf_op jit(solution)/shard_map/ppermute | solution.py:18
  35.3 3.0 %copy-start.5 = (bf16[512,64]{0,1:T(8,128)(2,1)S(1)}, bf16[512,64]{0,1:T(8,128)(2,1)}, u32[]{:S(2)}) copy-start(bf16[512,64]{0,1:T(8,128)(2,1)} %param.13) | copy-start | bytes 196612
  35.3 13.6 %all-to-all-start.2 = ((bf16[32,8,512]{2,1,0:T(8,128)(2,1)}), bf16[32,8,512]{2,1,0:T(8,128)(2,1)S(1)}, u32[]{:S(2)}, u32[]{:S(2)}) async-start(bf16[32,8,512]{2,1,0:T(8,128)(2,1)} %fusion.1), calls=%async_computation.2 | async-start | bytes 524288 | tf_op jit(solution)/shard_map/all_to_all | solution.py:325
  38.3 0.8 %copy-start.6 = (bf16[512,64]{0,1:T(8,128)(2,1)S(1)}, bf16[512,64]{0,1:T(8,128)(2,1)}, u32[]{:S(2)}) copy-start(bf16[512,64]{0,1:T(8,128)(2,1)} %param.12) | copy-start | bytes 196612
  39.3 1.2 %collective-permute-start.7 = (f32[8,512]{1,0:T(8,128)S(1)}, f32[8,512]{1,0:T(8,128)S(1)}, u32[]{:S(2)}, u32[]{:S(2)}) collective-permute-start(f32[8,512]{1,0:T(8,128)S(1)} %convolution_add_fusion), channel_id=1, source_target_pairs={{0,1},{1,0},{2,3},{3,2},{4,5},{5,4},{6,7},{7,6},{8,9},{9,8},{10,11... | collective-permute-start | bytes 49160 | tf_op jit(solution)/shard_map/ppermute | solution.py:23
  40.5 3.8 %collective-permute-start.8 = (f32[8,512]{1,0:T(8,128)S(1)}, f32[8,512]{1,0:T(8,128)S(1)}, u32[]{:S(2)}, u32[]{:S(2)}) collective-permute-start(f32[8,512]{1,0:T(8,128)S(1)} %add.25), channel_id=1, source_target_pairs={{0,2},{1,3},{2,0},{3,1},{4,6},{5,7},{6,4},{7,5},{8,10},{9,11},{10,... | collective-permute-start | bytes 49160 | tf_op jit(solution)/shard_map/ppermute | solution.py:23
  44.3 3.7 %collective-permute-start.9 = (f32[8,512]{1,0:T(8,128)S(1)}, f32[8,512]{1,0:T(8,128)S(1)}, u32[]{:S(2)}, u32[]{:S(2)}) collective-permute-start(f32[8,512]{1,0:T(8,128)S(1)} %add.26), channel_id=1, source_target_pairs={{0,4},{1,5},{2,6},{3,7},{4,0},{5,1},{6,2},{7,3},{8,12},{9,13},{10,... | collective-permute-start | bytes 49160 | tf_op jit(solution)/shard_map/ppermute | solution.py:23

commit v4 on v3

--- a/solution.py
+++ b/solution.py
@@ -185,6 +185,40 @@
         out_ref[...] = sums_ref[lax.rem(own + s, pipes)]
 
 
+def gradient_kernel(keys_in_ref, values_in_ref, *refs):
+    *sum_refs, out_ref = refs
+    f32, bf16 = jnp.float32, jnp.bfloat16
+    total = sum_refs[0][...]
+    for ref in sum_refs[1:]:
+        total = total + ref[...]
+    total, head = total.astype(bf16), keys_in_ref.shape[0]
+    out_ref[...] = jnp.dot(total[:, :head], keys_in_ref[...], preferred_element_type=f32) + jnp.dot(
+        total[:, head:], values_in_ref[...], preferred_element_type=f32
+    )
+
+
+def expert_kernel(rows_ref, first_ref, second_ref, out_hbm, out_ref, left):
+    chunks = left.shape[0]
+    size = rows_ref.shape[0] // chunks
+    f32, bf16 = jnp.float32, jnp.bfloat16
+    active = jnp.maximum(
+        lax.dot_general(
+            rows_ref[...], first_ref[...], (((1,), (1,)), ((), ())), preferred_element_type=f32
+        ),
+        0.0,
+    ).astype(bf16)
+    leaves = []
+    for i in range(chunks):
+        chunk = slice(i * size, (i + 1) * size)
+        out_ref[chunk] = jnp.dot(
+            active[chunk], second_ref[...], preferred_element_type=f32
+        ).astype(bf16)
+        leaves.append(pltpu.make_async_copy(out_ref.at[chunk], out_hbm.at[chunk], left.at[i]))
+        leaves[-1].start()
+    for leave in leaves:
+        leave.wait()
+
+
 def combine_kernel(returned_ref, target_ref, hidden_ref, out_ref):
     slots, tok_dev = returned_ref.shape[1], hidden_ref.shape[0]
     f32, bf16 = jnp.float32, jnp.bfloat16
@@ -306,22 +340,28 @@
         compiler_params=params,
         cost_estimate=pl.CostEstimate(flops=0, bytes_accessed=0, transcendentals=0),
     )(kv, queries_turned, context_grad.T, lengths)
-    for s, other in enumerate(others):
-        total = total + shifted(other, "pipe", s + 1)
-    total = total.astype(bf16)
+    sums = [total] + [shifted(other, "pipe", s + 1) for s, other in enumerate(others)]
     arrived = lax.all_to_all(outgoing, EVERYONE, split_axis=0, concat_axis=0, tiled=True)
-    active = jnp.maximum(
-        jnp.dot(
-            arrived.reshape(pipes * experts * cap, model), w_in[0], preferred_element_type=f32
+    arrived, *sums = lax.optimization_barrier((arrived, *sums))
+    rows = pipes * experts * cap
+    part = pl.pallas_call(
+        expert_kernel,
+        out_shape=jax.ShapeDtypeStruct((rows, model), bf16),
+        in_specs=[VMEM] * 3,
+        out_specs=HBM,
+        scratch_shapes=[pltpu.VMEM((rows, model), bf16), pltpu.SemaphoreType.DMA((2,))],
+        compiler_params=params,
+        cost_estimate=pl.CostEstimate(
+            flops=4 * rows * model * w_in.shape[2], bytes_accessed=1 << 20, transcendentals=0
         ),
-        0.0,
-    ).astype(bf16)
-    part = jnp.dot(active, w_out[0], preferred_element_type=f32).astype(bf16)
-    enc_part = lax.dot_general(
-        total[:, :head], key_weight, (((1,), (1,)), ((), ())), preferred_element_type=f32
-    ) + lax.dot_general(
-        total[:, head:], value_weight, (((1,), (1,)), ((), ())), preferred_element_type=f32
-    )
+    )(arrived.reshape(rows, model), w_in[0].T, w_out[0])
+    enc_part = pl.pallas_call(
+        gradient_kernel,
+        out_shape=jax.ShapeDtypeStruct((enc_dev, model), f32),
+        in_specs=[VMEM] * (2 + pipes),
+        out_specs=VMEM,
+        compiler_params=params,
+    )(key_weight.T, value_weight.T, *sums)
     returned = lax.all_to_all(
         part.reshape(pipes * experts, cap, model),
         EVERYONE,

time: 50.2 us -> 50.1 us (level)
  matrix products: 1.56 us -> 0 us
  Pallas kernels: 4.73 us -> 6.1 us
  waiting for transfers between devices: 13.7 us -> 14.6 us
  local copies, waits for them, and re-layouts: 0.68 us -> 0.03 us
    dot_general x3 -> x0, matrix products: 1.56 us -> none  [the longest x1 1.26 us: per_device(): part = jnp.dot(active, w_out[0], preferred_element_type=f32).astype(bf16)]
    pallas_call x0 -> x2, Pallas kernels: none -> 1.41 us  [the longest x1 1.22 us: per_device(): pl.pallas_call(expert_kernel, out_shape=jax.ShapeDtypeStruct((rows, model...]
    unnamed x14, local copies, waits for them, and re-layouts: 0.68 us -> 0.03 us
    ppermute x7, waiting for transfers between devices: 5 us -> 5.61 us  [crossed(): return lax.ppermute(value, 'expert', [(i, i ^ bit) for i in range(size)])]
  transfers between devices with their start and end apart: 13 -> 13, of which waited for: 8 -> 8; matrix products, arithmetic and copies ran while one was open for 2% -> 1% of each run, Pallas kernels for 1% -> 2%
where the time goes in v4:
time: 50.1 us; the launch traced here: 49.7 us
  starting transfers between devices  27.6 us (55%)
  waiting for transfers between devices  14.6 us (29%)
  Pallas kernels  6.1 us (12%)
  between operations  0.8 us (2%)
  other arithmetic  0.61 us (1%)
    ppermute x7, starting transfers between devices, crossed(): return lax.ppermute(value, 'expert', [(i, i ^ bit) for i in range(size)])  7.7 us
    all_to_all x1, starting transfers between devices, per_device(): lax.all_to_all(spread_kv, EVERYONE, split_axis=0, concat_axis=0, tiled=True)  6.96 us
    ppermute x3, starting transfers between devices, shifted(): lax.ppermute(value, axis, [(i, (i + step) % size) for i in range(size)])  5.66 us
    ppermute x7, waiting for transfers between devices, crossed(): return lax.ppermute(value, 'expert', [(i, i ^ bit) for i in range(size)])  5.61 us
    all_to_all x1, starting transfers between devices, per_device(): lax.all_to_all(outgoing, EVERYONE, split_axis=0, concat_axis=0, tiled=True)  4.28 us
    all_to_all x1, waiting for transfers between devices, per_device(): lax.all_to_all(spread_kv, EVERYONE, split_axis=0, concat_axis=0, tiled=True)  3.81 us
    ppermute x3, waiting for transfers between devices, shifted(): lax.ppermute(value, axis, [(i, (i + step) % size) for i in range(size)])  3.59 us
    all_to_all x1, starting transfers between devices, per_device(): lax.all_to_all(part.reshape(pipes * experts, cap, model), EVERYONE, split...  2.99 us
  transfers between devices with their start and end apart: 13, of which 8 were waited for; matrix products, arithmetic and copies ran while one was open for 1% of the time, Pallas kernels for 2%

profile of v4, /device:TPU:0, one launch (start us, length us, event | category | flops | bytes accessed | tf_op | source)
XLA Modules:
  0.0 49.7 jit_solution(16087530031627050386)
XLA Ops:
  0.6 1.8 %shard_map.122 = (bf16[32,8,128]{2,1,0:T(8,128)(2,1)}, bf16[4,64,128]{2,1,0:T(8,128)(2,1)S(1)}, bf16[4,64,128]{2,1,0:T(8,128)(2,1)S(1)}, s32[128]{0:T(128)S(1)},...) custom-call(bf16[8,512]{1,0:T(8,128)(2,1)} %enc_hbm.1, bf16[64,512]{1,0:T(8,128)(2,1)} %bitcast.20, ...), custom_call_target="tpu_custom_call" | custom-call | tf_op jit(solution)/shard_map/pallas_call | solution.py:259
  2.5 0.5 %collective-permute-start = (bf16[4,64,128]{2,1,0:T(8,128)(2,1)S(1)}, bf16[4,64,128]{2,1,0:T(8,128)(2,1)S(1)}, u32[]{:S(2)}, u32[]{:S(2)}) collective-permute-start(bf16[4,64,128]{2,1,0:T(8,128)(2,1)S(1)} %get-tuple-element.36), channel_id=1, source_target_pairs={{0,1},{1,0},{2,3},{3,2},{4,5},{5,4},{6,7},{7,6},{8,9},{9,8},{10,11... | collective-permute-start | bytes 196616 | tf_op jit(solution)/shard_map/ppermute | solution.py:23
  3.0 7.0 %all-to-all-start = ((bf16[32,8,128]{2,1,0:T(8,128)(2,1)}), bf16[32,8,128]{2,1,0:T(8,128)(2,1)S(1)}, u32[]{:S(2)}, u32[]{:S(2)}) async-start(bf16[32,8,128]{2,1,0:T(8,128)(2,1)} %get-tuple-element.28), calls=%async_computation | async-start | bytes 131072 | tf_op jit(solution)/shard_map/all_to_all | solution.py:298
  9.9 0.0 collective-permute-done.got_ref
  10.0 2.7 %collective-permute-start.1 = (bf16[128,128]{1,0:T(8,128)(2,1)S(1)}, bf16[128,128]{1,0:T(8,128)(2,1)S(1)}, u32[]{:S(2)}, u32[]{:S(2)}) collective-permute-start(bf16[128,128]{1,0:T(8,128)(2,1)S(1)} %get-tuple-element.38), channel_id=1, source_target_pairs={{0,6},{1,7},{2,4},{3,5},{4,2},{5,3},{6,0},{7,1},{8,14},{9,15},{10,... | collective-permute-start | bytes 98312 | tf_op jit(solution)/shard_map/ppermute | solution.py:23
  12.7 0.6 %collective-permute-start.2 = (bf16[128,128]{1,0:T(8,128)(2,1)S(1)}, bf16[128,128]{1,0:T(8,128)(2,1)S(1)}, u32[]{:S(2)}, u32[]{:S(2)}) collective-permute-start(bf16[128,128]{1,0:T(8,128)(2,1)S(1)} %get-tuple-element.39), channel_id=1, source_target_pairs={{0,4},{1,5},{2,6},{3,7},{4,0},{5,1},{6,2},{7,3},{8,12},{9,13},{10,... | collective-permute-start | bytes 98312 | tf_op jit(solution)/shard_map/ppermute | solution.py:23
  13.3 0.3 collective-permute-start.3
  13.5 3.8 %all-to-all-done = bf16[32,8,128]{2,1,0:T(8,128)(2,1)S(1)} async-done(((bf16[32,8,128]{2,1,0:T(8,128)(2,1)}), bf16[32,8,128]{2,1,0:T(8,128)(2,1)S(1)}, u32[]{:S(2)}, u32[]{:S(2)}) %all-to-all-start) | async-done | bytes 65568 | tf_op jit(solution)/shard_map/all_to_all | solution.py:298
  17.4 0.0 copy-start.5
  17.4 0.1 shard_map.123
  17.5 0.0 collective-permute-done.1.refs_1_
  17.5 0.0 collective-permute-done.2.refs_2_
  17.5 0.0 collective-permute-done.3.refs_3_
  17.5 0.0 copy-start.6
  17.5 1.4 %shard_map.125 = (f32[128,512]{1,0:T(8,128)S(1)}, bf16[4,64,512]{2,1,0:T(8,128)(2,1)}) custom-call(bf16[1,256,512]{2,1,0:T(8,128)(2,1)S(1)} %get-tuple-element.29.keys_ref, bf16[1,256,512]{2,1,0:T(8,128)(2,1)S(1)} %get-tuple-element.30.values_ref, s32[128]{0:T(128)S(1)} %get-tuple-element.31.lengths_ref, ...), custom_call_target="tpu_custom_call" | custom-call | tf_op jit(solution)/shard_map/pallas_call | solution.py:321
  19.0 0.0 copy-start
  19.0 0.0 copy-start.1
  19.0 0.0 copy-start.2
  19.0 4.3 %all-to-all-start.1 = ((bf16[32,8,512]{2,1,0:T(8,128)(2,1)}), bf16[32,8,512]{2,1,0:T(8,128)(2,1)S(1)}, u32[]{:S(2)}, u32[]{:S(2)}) async-start(bf16[32,8,512]{2,1,0:T(8,128)(2,1)} %bitcast.5), calls=%async_computation.1 | async-start | bytes 524288 | tf_op jit(solution)/shard_map/all_to_all | solution.py:344
  23.3 0.0 copy-done.5
  23.3 0.0 copy-done.6
  23.3 0.0 copy-done
  23.3 0.4 shard_map.126
  23.7 1.8 %collective-permute-start.4 = (f32[8,128]{1,0:T(8,128)S(1)}, f32[8,128]{1,0:T(8,128)S(1)}, u32[]{:S(2)}, u32[]{:S(2)}) collective-permute-start(f32[8,128]{1,0:T(8,128)S(1)} %get-tuple-element.45), channel_id=1, source_target_pairs={{0,8},{8,16},{16,24},{24,0},{1,9},{9,17},{17,25},{25,1},{2,10},{10... | collective-permute-start | bytes 12296 | tf_op jit(solution)/shard_map/ppermute | solution.py:18
  25.5 2.4 %collective-permute-start.5 = (f32[8,128]{1,0:T(8,128)S(1)}, f32[8,128]{1,0:T(8,128)S(1)}, u32[]{:S(2)}, u32[]{:S(2)}) collective-permute-start(f32[8,128]{1,0:T(8,128)S(1)} %get-tuple-element.46), channel_id=1, source_target_pairs={{0,16},{8,24},{16,0},{24,8},{1,17},{9,25},{17,1},{25,9},{2,18},{10... | collective-permute-start | bytes 12296 | tf_op jit(solution)/shard_map/ppermute | solution.py:18
  27.9 1.4 %collective-permute-start.6 = (f32[8,128]{1,0:T(8,128)S(1)}, f32[8,128]{1,0:T(8,128)S(1)}, u32[]{:S(2)}, u32[]{:S(2)}) collective-permute-start(f32[8,128]{1,0:T(8,128)S(1)} %get-tuple-element.47), channel_id=1, source_target_pairs={{0,24},{8,0},{16,8},{24,16},{1,25},{9,1},{17,9},{25,17},{2,26},{10... | collective-permute-start | bytes 12296 | tf_op jit(solution)/shard_map/ppermute | solution.py:18
  29.4 3.0 %collective-permute-done.4.refs_1_ = f32[8,128]{1,0:T(8,128)S(1)} collective-permute-done((f32[8,128]{1,0:T(8,128)S(1)}, f32[8,128]{1,0:T(8,128)S(1)}, u32[]{:S(2)}, u32[]{:S(2)}) %collective-permute-start.4) | collective-permute-done | bytes 4128 | tf_op jit(solution)/shard_map/ppermute | solution.py:18
  32.4 0.6 %collective-permute-done.5.refs_2_ = f32[8,128]{1,0:T(8,128)S(1)} collective-permute-done((f32[8,128]{1,0:T(8,128)S(1)}, f32[8,128]{1,0:T(8,128)S(1)}, u32[]{:S(2)}, u32[]{:S(2)}) %collective-permute-start.5) | collective-permute-done | bytes 4128 | tf_op jit(solution)/shard_map/ppermute | solution.py:18
  33.0 0.0 collective-permute-done.6.refs_3_
  33.0 1.0 %all-to-all-done.1 = bf16[32,8,512]{2,1,0:T(8,128)(2,1)S(1)} async-done(((bf16[32,8,512]{2,1,0:T(8,128)(2,1)}), bf16[32,8,512]{2,1,0:T(8,128)(2,1)S(1)}, u32[]{:S(2)}, u32[]{:S(2)}) %all-to-all-start.1) | async-done | bytes 262176 | tf_op jit(solution)/shard_map/all_to_all | solution.py:344
  34.0 0.0 copy-done.1
  34.0 0.0 copy-done.2
  34.0 1.2 %shard_map.127 = bf16[256,512]{1,0:T(8,128)(2,1)} custom-call(bf16[256,512]{1,0:T(8,128)(2,1)S(1)} %bitcast.15, bf16[320,512]{1,0:T(8,128)(2,1)S(1)} %bitcast.18, bf16[320,512]{1,0:T(8,128)(2,1)S(1)} %bitcast.19), custom_call_target="tpu_custom_call" | custom-call | flops 167772160 | bytes 1048576 | tf_op jit(solution)/shard_map/pallas_call | solution.py:347
  35.2 0.0 copy-start.3
  35.2 0.0 copy-start.4
  35.2 3.0 %all-to-all-start.2 = ((bf16[32,8,512]{2,1,0:T(8,128)(2,1)}), bf16[32,8,512]{2,1,0:T(8,128)(2,1)S(1)}, u32[]{:S(2)}, u32[]{:S(2)}) async-start(bf16[32,8,512]{2,1,0:T(8,128)(2,1)} %bitcast.11), calls=%async_computation.2 | async-start | bytes 524288 | tf_op jit(solution)/shard_map/all_to_all | solution.py:365
  38.2 0.0 copy-done.3
  38.2 0.0 copy-done.4
  38.3 0.2 shard_map.129
  38.4 0.3 collective-permute-start.7
  38.7 0.9 %collective-permute-done.7 = f32[8,512]{1,0:T(8,128)S(1)} collective-permute-done((f32[8,512]{1,0:T(8,128)S(1)}, f32[8,512]{1,0:T(8,128)S(1)}, u32[]{:S(2)}, u32[]{:S(2)}) %collective-permute-start.7) | collective-permute-done | bytes 16416 | tf_op jit(solution)/shard_map/ppermute | solution.py:23
  39.6 1.8 %collective-permute-start.8 = (f32[8,512]{1,0:T(8,128)S(1)}, f32[8,512]{1,0:T(8,128)S(1)}, u32[]{:S(2)}, u32[]{:S(2)}) collective-permute-start(f32[8,512]{1,0:T(8,128)S(1)} %add.9), channel_id=1, source_target_pairs={{0,2},{1,3},{2,0},{3,1},{4,6},{5,7},{6,4},{7,5},{8,10},{9,11},{10,... | collective-permute-start | bytes 49160 | tf_op jit(solution)/shard_map/ppermute | solution.py:23
  41.4 2.3 %collective-permute-done.8 = f32[8,512]{1,0:T(8,128)S(1)} collective-permute-done((f32[8,512]{1,0:T(8,128)S(1)}, f32[8,512]{1,0:T(8,128)S(1)}, u32[]{:S(2)}, u32[]{:S(2)}) %collective-permute-start.8) | collective-permute-done | bytes 16416 | tf_op jit(solution)/shard_map/ppermute | solution.py:23
  43.7 1.6 %collective-permute-start.9 = (f32[8,512]{1,0:T(8,128)S(1)}, f32[8,512]{1,0:T(8,128)S(1)}, u32[]{:S(2)}, u32[]{:S(2)}) collective-permute-start(f32[8,512]{1,0:T(8,128)S(1)} %add.10), channel_id=1, source_target_pairs={{0,4},{1,5},{2,6},{3,7},{4,0},{5,1},{6,2},{7,3},{8,12},{9,13},{10,... | collective-permute-start | bytes 49160 | tf_op jit(solution)/shard_map/ppermute | solution.py:23
  45.3 2.4 %collective-permute-done.9 = f32[8,512]{1,0:T(8,128)S(1)} collective-permute-done((f32[8,512]{1,0:T(8,128)S(1)}, f32[8,512]{1,0:T(8,128)S(1)}, u32[]{:S(2)}, u32[]{:S(2)}) %collective-permute-start.9) | collective-permute-done | bytes 16416 | tf_op jit(solution)/shard_map/ppermute | solution.py:23
  47.7 0.6 %add_convert_fusion = bf16[8,512]{1,0:T(8,128)(2,1)} fusion(f32[8,512]{1,0:T(8,128)S(1)} %add.10, f32[8,512]{1,0:T(8,128)S(1)} %collective-permute-done.9), kind=kLoop, calls=%fused_computation | loop fusion | flops 8192 | bytes 40960 | tf_op jit(solution)/shard_map/convert_element_type | solution.py:381
  48.3 0.5 %all-to-all-done.2 = bf16[32,8,512]{2,1,0:T(8,128)(2,1)S(1)} async-done(((bf16[32,8,512]{2,1,0:T(8,128)(2,1)}), bf16[32,8,512]{2,1,0:T(8,128)(2,1)S(1)}, u32[]{:S(2)}, u32[]{:S(2)}) %all-to-all-start.2) | async-done | bytes 262176 | tf_op jit(solution)/shard_map/all_to_all | solution.py:365
  48.8 0.9 %shard_map.128 = bf16[128,512]{1,0:T(8,128)(2,1)} custom-call(bf16[4,64,512]{2,1,0:T(8,128)(2,1)S(1)} %bitcast.14, s32[1,128]{1,0:T(1,128)S(1)} %get-tuple-element.34.target_ref, f32[128,512]{1,0:T(8,128)S(1)} %get-tuple-element.49.hidden_ref), custom_call_target="tpu_custom_call" | custom-call | tf_op jit(solution)/shard_map/pallas_call | solution.py:372
  (3 shorter events, 0.0 us)
Async XLA Ops:
  2.5 7.5 %collective-permute-start = (bf16[4,64,128]{2,1,0:T(8,128)(2,1)S(1)}, bf16[4,64,128]{2,1,0:T(8,128)(2,1)S(1)}, u32[]{:S(2)}, u32[]{:S(2)}) collective-permute-start(bf16[4,64,128]{2,1,0:T(8,128)(2,1)S(1)} %get-tuple-element.36), channel_id=1, source_target_pairs={{0,1},{1,0},{2,3},{3,2},{4,5},{5,4},{6,7},{7,6},{8,9},{9,8},{10,11... | collective-permute-start | bytes 196616 | tf_op jit(solution)/shard_map/ppermute | solution.py:23
  3.0 14.4 %all-to-all-start = ((bf16[32,8,128]{2,1,0:T(8,128)(2,1)}), bf16[32,8,128]{2,1,0:T(8,128)(2,1)S(1)}, u32[]{:S(2)}, u32[]{:S(2)}) async-start(bf16[32,8,128]{2,1,0:T(8,128)(2,1)} %get-tuple-element.28), calls=%async_computation | async-start | bytes 131072 | tf_op jit(solution)/shard_map/all_to_all | solution.py:298
  10.0 7.5 %collective-permute-start.1 = (bf16[128,128]{1,0:T(8,128)(2,1)S(1)}, bf16[128,128]{1,0:T(8,128)(2,1)S(1)}, u32[]{:S(2)}, u32[]{:S(2)}) collective-permute-start(bf16[128,128]{1,0:T(8,128)(2,1)S(1)} %get-tuple-element.38), channel_id=1, source_target_pairs={{0,6},{1,7},{2,4},{3,5},{4,2},{5,3},{6,0},{7,1},{8,14},{9,15},{10,... | collective-permute-start | bytes 98312 | tf_op jit(solution)/shard_map/ppermute | solution.py:23
  12.7 4.8 %collective-permute-start.2 = (bf16[128,128]{1,0:T(8,128)(2,1)S(1)}, bf16[128,128]{1,0:T(8,128)(2,1)S(1)}, u32[]{:S(2)}, u32[]{:S(2)}) collective-permute-start(bf16[128,128]{1,0:T(8,128)(2,1)S(1)} %get-tuple-element.39), channel_id=1, source_target_pairs={{0,4},{1,5},{2,6},{3,7},{4,0},{5,1},{6,2},{7,3},{8,12},{9,13},{10,... | collective-permute-start | bytes 98312 | tf_op jit(solution)/shard_map/ppermute | solution.py:23
  13.3 4.2 %collective-permute-start.3 = (bf16[128,128]{1,0:T(8,128)(2,1)S(1)}, bf16[128,128]{1,0:T(8,128)(2,1)S(1)}, u32[]{:S(2)}, u32[]{:S(2)}) collective-permute-start(bf16[128,128]{1,0:T(8,128)(2,1)S(1)} %get-tuple-element.40), channel_id=1, source_target_pairs={{0,2},{1,3},{2,0},{3,1},{4,6},{5,7},{6,4},{7,5},{8,10},{9,11},{10,... | collective-permute-start | bytes 98312 | tf_op jit(solution)/shard_map/ppermute | solution.py:23
  17.4 5.9 %copy-start.5 = (bf16[1024,64]{0,1:T(8,128)(2,1)S(1)}, bf16[1024,64]{0,1:T(8,128)(2,1)}, u32[]{:S(2)}) copy-start(bf16[1024,64]{0,1:T(8,128)(2,1)} %param.16) | copy-start | bytes 393220
  17.5 5.7 %copy-start.6 = (s32[1024]{0:T(1024)S(1)}, s32[1024]{0:T(1024)}, u32[]{:S(2)}) copy-start(s32[1024]{0:T(1024)} %lengths_ref.1) | copy-start | bytes 12292
  19.0 4.3 %copy-start = (bf16[1024,64]{0,1:T(8,128)(2,1)S(1)}, bf16[1024,64]{0,1:T(8,128)(2,1)}, u32[]{:S(2)}) copy-start(bf16[1024,64]{0,1:T(8,128)(2,1)} %param.14) | copy-start | bytes 393220
  19.0 15.0 %copy-start.1 = (bf16[1,512,320]{1,2,0:T(8,128)(2,1)S(1)}, bf16[1,512,320]{1,2,0:T(8,128)(2,1)}, u32[]{:S(2)}) copy-start(bf16[1,512,320]{1,2,0:T(8,128)(2,1)} %param.20) | copy-start | bytes 983044
  19.0 15.0 %copy-start.2 = (bf16[1,320,512]{2,1,0:T(8,128)(2,1)S(1)}, bf16[1,320,512]{2,1,0:T(8,128)(2,1)}, u32[]{:S(2)}) copy-start(bf16[1,320,512]{2,1,0:T(8,128)(2,1)} %param.21) | copy-start | bytes 983044
  19.0 15.0 %all-to-all-start.1 = ((bf16[32,8,512]{2,1,0:T(8,128)(2,1)}), bf16[32,8,512]{2,1,0:T(8,128)(2,1)S(1)}, u32[]{:S(2)}, u32[]{:S(2)}) async-start(bf16[32,8,512]{2,1,0:T(8,128)(2,1)} %bitcast.5), calls=%async_computation.1 | async-start | bytes 524288 | tf_op jit(solution)/shard_map/all_to_all | solution.py:344
  23.7 8.7 %collective-permute-start.4 = (f32[8,128]{1,0:T(8,128)S(1)}, f32[8,128]{1,0:T(8,128)S(1)}, u32[]{:S(2)}, u32[]{:S(2)}) collective-permute-start(f32[8,128]{1,0:T(8,128)S(1)} %get-tuple-element.45), channel_id=1, source_target_pairs={{0,8},{8,16},{16,24},{24,0},{1,9},{9,17},{17,25},{25,1},{2,10},{10... | collective-permute-start | bytes 12296 | tf_op jit(solution)/shard_map/ppermute | solution.py:18
  25.5 7.4 %collective-permute-start.5 = (f32[8,128]{1,0:T(8,128)S(1)}, f32[8,128]{1,0:T(8,128)S(1)}, u32[]{:S(2)}, u32[]{:S(2)}) collective-permute-start(f32[8,128]{1,0:T(8,128)S(1)} %get-tuple-element.46), channel_id=1, source_target_pairs={{0,16},{8,24},{16,0},{24,8},{1,17},{9,25},{17,1},{25,9},{2,18},{10... | collective-permute-start | bytes 12296 | tf_op jit(solution)/shard_map/ppermute | solution.py:18
  27.9 5.0 %collective-permute-start.6 = (f32[8,128]{1,0:T(8,128)S(1)}, f32[8,128]{1,0:T(8,128)S(1)}, u32[]{:S(2)}, u32[]{:S(2)}) collective-permute-start(f32[8,128]{1,0:T(8,128)S(1)} %get-tuple-element.47), channel_id=1, source_target_pairs={{0,24},{8,0},{16,8},{24,16},{1,25},{9,1},{17,9},{25,17},{2,26},{10... | collective-permute-start | bytes 12296 | tf_op jit(solution)/shard_map/ppermute | solution.py:18
  35.2 3.0 %copy-start.3 = (bf16[512,64]{0,1:T(8,128)(2,1)S(1)}, bf16[512,64]{0,1:T(8,128)(2,1)}, u32[]{:S(2)}) copy-start(bf16[512,64]{0,1:T(8,128)(2,1)} %param.12) | copy-start | bytes 196612
  35.2 3.0 %copy-start.4 = (bf16[512,64]{0,1:T(8,128)(2,1)S(1)}, bf16[512,64]{0,1:T(8,128)(2,1)}, u32[]{:S(2)}) copy-start(bf16[512,64]{0,1:T(8,128)(2,1)} %param.13) | copy-start | bytes 196612
  35.2 13.6 %all-to-all-start.2 = ((bf16[32,8,512]{2,1,0:T(8,128)(2,1)}), bf16[32,8,512]{2,1,0:T(8,128)(2,1)S(1)}, u32[]{:S(2)}, u32[]{:S(2)}) async-start(bf16[32,8,512]{2,1,0:T(8,128)(2,1)} %bitcast.11), calls=%async_computation.2 | async-start | bytes 524288 | tf_op jit(solution)/shard_map/all_to_all | solution.py:365
  38.4 1.2 %collective-permute-start.7 = (f32[8,512]{1,0:T(8,128)S(1)}, f32[8,512]{1,0:T(8,128)S(1)}, u32[]{:S(2)}, u32[]{:S(2)}) collective-permute-start(f32[8,512]{1,0:T(8,128)S(1)} %shard_map.129), channel_id=1, source_target_pairs={{0,1},{1,0},{2,3},{3,2},{4,5},{5,4},{6,7},{7,6},{8,9},{9,8},{10,11... | collective-permute-start | bytes 49160 | tf_op jit(solution)/shard_map/ppermute | solution.py:23
  39.6 4.1 %collective-permute-start.8 = (f32[8,512]{1,0:T(8,128)S(1)}, f32[8,512]{1,0:T(8,128)S(1)}, u32[]{:S(2)}, u32[]{:S(2)}) collective-permute-start(f32[8,512]{1,0:T(8,128)S(1)} %add.9), channel_id=1, source_target_pairs={{0,2},{1,3},{2,0},{3,1},{4,6},{5,7},{6,4},{7,5},{8,10},{9,11},{10,... | collective-permute-start | bytes 49160 | tf_op jit(solution)/shard_map/ppermute | solution.py:23
  43.7 4.0 %collective-permute-start.9 = (f32[8,512]{1,0:T(8,128)S(1)}, f32[8,512]{1,0:T(8,128)S(1)}, u32[]{:S(2)}, u32[]{:S(2)}) collective-permute-start(f32[8,512]{1,0:T(8,128)S(1)} %add.10), channel_id=1, source_target_pairs={{0,4},{1,5},{2,6},{3,7},{4,0},{5,1},{6,2},{7,3},{8,12},{9,13},{10,... | collective-permute-start | bytes 49160 | tf_op jit(solution)/shard_map/ppermute | solution.py:23

commit v5 on v4

--- a/solution.py
+++ b/solution.py
@@ -69,25 +69,28 @@
         for ref, which in ((keep_ref, core), (send_ref, 1 - core)):
             lanes = pl.ds(pl.multiple_of((2 * chip + which) * tok_dev, tok_dev), tok_dev)
             ref[chip] = queries_ref[:, lanes]
-    routes = routes_ref[...]
-    onehot = lax.broadcasted_iota(jnp.int32, (experts, tok_dev), 0) == routes
-    earlier = lax.broadcasted_iota(jnp.int32, (tok_dev, tok_dev), 0) < lax.broadcasted_iota(
-        jnp.int32, (tok_dev, tok_dev), 1
-    )
-    before = jnp.dot(
-        onehot.astype(f32).astype(bf16), earlier.astype(f32).astype(bf16), preferred_element_type=f32
-    )
-    slot_rank = jnp.sum(jnp.where(onehot, before, 0.0), axis=0, keepdims=True).astype(jnp.int32)
-    target_ref[...] = jnp.where(slot_rank < cap, routes * cap + slot_rank, -1)
+    target_ref[...] = routes_ref[...]
     leave.wait()
 
 
-def gather_kernel(keep_ref, got_ref, *out_refs):
+def gather_kernel(cap, keep_ref, got_ref, routes_ref, target_ref, *out_refs):
+    f32, bf16 = jnp.float32, jnp.bfloat16
+    experts, tok_dev = lax.axis_size("expert"), routes_ref.shape[1]
     chip = lax.axis_index("expert") // 2
     head = keep_ref.shape[1]
     for k, out_ref in enumerate(out_refs):
         out_ref[:head] = keep_ref[lax.bitwise_xor(chip, k)]
         out_ref[head:] = got_ref[lax.bitwise_xor(chip, k)]
+    routes = routes_ref[...]
+    onehot = lax.broadcasted_iota(jnp.int32, (experts, tok_dev), 0) == routes
+    earlier = lax.broadcasted_iota(jnp.int32, (tok_dev, tok_dev), 0) < lax.broadcasted_iota(
+        jnp.int32, (tok_dev, tok_dev), 1
+    )
+    before = jnp.dot(
+        onehot.astype(f32).astype(bf16), earlier.astype(f32).astype(bf16), preferred_element_type=f32
+    )
+    slot_rank = jnp.sum(jnp.where(onehot, before, 0.0), axis=0, keepdims=True).astype(jnp.int32)
+    target_ref[...] = jnp.where(slot_rank < cap, routes * cap + slot_rank, -1)
 
 
 def block_kernel(group, kv_ref, keys_ref, values_ref):
@@ -299,14 +302,15 @@
         spread_kv, EVERYONE, split_axis=0, concat_axis=0, tiled=True
     ).reshape(pipes, experts, enc_dev, 2 * head)
     chips = experts // 2
-    query_blocks = pl.pallas_call(
-        gather_kernel,
-        out_shape=[jax.ShapeDtypeStruct((2 * head, tok_dev), bf16)] * chips,
-        in_specs=[VMEM] * 2,
-        out_specs=[VMEM] * chips,
+    target, *query_blocks = pl.pallas_call(
+        functools.partial(gather_kernel, cap),
+        out_shape=[jax.ShapeDtypeStruct((1, tok_dev), jnp.int32)]
+        + [jax.ShapeDtypeStruct((2 * head, tok_dev), bf16)] * chips,
+        in_specs=[VMEM] * 3,
+        out_specs=[VMEM] * (1 + chips),
         compiler_params=params,
         cost_estimate=pl.CostEstimate(flops=1 << 34, bytes_accessed=1 << 26, transcendentals=0),
-    )(keep, crossed(send, 1))
+    )(keep, crossed(send, 1), target)
     query_blocks = [query_blocks[0]] + [crossed(query_blocks[k], 2 * k) for k in range(1, chips)]
     group = max(g for g in range(2, experts + 1, 2) if experts % g == 0 and g * head <= 512)
     blocks = (experts // group, pipes * group * enc_dev, group * head)

time: 50.1 us -> 50.2 us (level)
  no operation moved by 1% of the time
where the time goes in v5:
time: 50.2 us; the launch traced here: 49.8 us
  starting transfers between devices  27.6 us (55%)
  waiting for transfers between devices  14.5 us (29%)
  Pallas kernels  6.22 us (12%)
  between operations  0.79 us (2%)
  other arithmetic  0.61 us (1%)
    ppermute x7, starting transfers between devices, crossed(): return lax.ppermute(value, 'expert', [(i, i ^ bit) for i in range(size)])  7.63 us
    all_to_all x1, starting transfers between devices, per_device(): lax.all_to_all(spread_kv, EVERYONE, split_axis=0, concat_axis=0, tiled=True)  6.96 us
    ppermute x3, starting transfers between devices, shifted(): lax.ppermute(value, axis, [(i, (i + step) % size) for i in range(size)])  5.66 us
    ppermute x7, waiting for transfers between devices, crossed(): return lax.ppermute(value, 'expert', [(i, i ^ bit) for i in range(size)])  5.61 us
    all_to_all x1, starting transfers between devices, per_device(): lax.all_to_all(outgoing, EVERYONE, split_axis=0, concat_axis=0, tiled=True)  4.33 us
    all_to_all x1, waiting for transfers between devices, per_device(): lax.all_to_all(spread_kv, EVERYONE, split_axis=0, concat_axis=0, tiled=True)  3.76 us
    ppermute x3, waiting for transfers between devices, shifted(): lax.ppermute(value, axis, [(i, (i + step) % size) for i in range(size)])  3.59 us
    all_to_all x1, starting transfers between devices, per_device(): lax.all_to_all(part.reshape(pipes * experts, cap, model), EVERYONE, split...  2.99 us
  transfers between devices with their start and end apart: 13, of which 8 were waited for; matrix products, arithmetic and copies ran while one was open for 1% of the time, Pallas kernels for 2%

profile of v5, /device:TPU:0, one launch (start us, length us, event | category | flops | bytes accessed | tf_op | source)
XLA Modules:
  0.0 49.8 jit_solution(9637063989737804658)
XLA Ops:
  0.6 1.8 %shard_map.122 = (bf16[32,8,128]{2,1,0:T(8,128)(2,1)}, bf16[4,64,128]{2,1,0:T(8,128)(2,1)S(1)}, bf16[4,64,128]{2,1,0:T(8,128)(2,1)S(1)}, s32[128]{0:T(128)S(1)},...) custom-call(bf16[8,512]{1,0:T(8,128)(2,1)} %enc_hbm.1, bf16[64,512]{1,0:T(8,128)(2,1)} %bitcast.20, ...), custom_call_target="tpu_custom_call" | custom-call | tf_op jit(solution)/shard_map/pallas_call | solution.py:262
  2.5 0.5 %collective-permute-start = (bf16[4,64,128]{2,1,0:T(8,128)(2,1)S(1)}, bf16[4,64,128]{2,1,0:T(8,128)(2,1)S(1)}, u32[]{:S(2)}, u32[]{:S(2)}) collective-permute-start(bf16[4,64,128]{2,1,0:T(8,128)(2,1)S(1)} %get-tuple-element.36), channel_id=1, source_target_pairs={{0,1},{1,0},{2,3},{3,2},{4,5},{5,4},{6,7},{7,6},{8,9},{9,8},{10,11... | collective-permute-start | bytes 196616 | tf_op jit(solution)/shard_map/ppermute | solution.py:23
  3.0 7.0 %all-to-all-start = ((bf16[32,8,128]{2,1,0:T(8,128)(2,1)}), bf16[32,8,128]{2,1,0:T(8,128)(2,1)S(1)}, u32[]{:S(2)}, u32[]{:S(2)}) async-start(bf16[32,8,128]{2,1,0:T(8,128)(2,1)} %get-tuple-element.29), calls=%async_computation | async-start | bytes 131072 | tf_op jit(solution)/shard_map/all_to_all | solution.py:301
  9.9 0.0 collective-permute-done.got_ref
  10.0 0.1 shard_map.124
  10.1 2.7 %collective-permute-start.1 = (bf16[128,128]{1,0:T(8,128)(2,1)S(1)}, bf16[128,128]{1,0:T(8,128)(2,1)S(1)}, u32[]{:S(2)}, u32[]{:S(2)}) collective-permute-start(bf16[128,128]{1,0:T(8,128)(2,1)S(1)} %get-tuple-element.40), channel_id=1, source_target_pairs={{0,6},{1,7},{2,4},{3,5},{4,2},{5,3},{6,0},{7,1},{8,14},{9,15},{10,... | collective-permute-start | bytes 98312 | tf_op jit(solution)/shard_map/ppermute | solution.py:23
  12.8 0.6 %collective-permute-start.2 = (bf16[128,128]{1,0:T(8,128)(2,1)S(1)}, bf16[128,128]{1,0:T(8,128)(2,1)S(1)}, u32[]{:S(2)}, u32[]{:S(2)}) collective-permute-start(bf16[128,128]{1,0:T(8,128)(2,1)S(1)} %get-tuple-element.41), channel_id=1, source_target_pairs={{0,4},{1,5},{2,6},{3,7},{4,0},{5,1},{6,2},{7,3},{8,12},{9,13},{10,... | collective-permute-start | bytes 98312 | tf_op jit(solution)/shard_map/ppermute | solution.py:23
  13.3 0.3 collective-permute-start.3
  13.6 3.8 %all-to-all-done = bf16[32,8,128]{2,1,0:T(8,128)(2,1)S(1)} async-done(((bf16[32,8,128]{2,1,0:T(8,128)(2,1)}), bf16[32,8,128]{2,1,0:T(8,128)(2,1)S(1)}, u32[]{:S(2)}, u32[]{:S(2)}) %all-to-all-start) | async-done | bytes 65568 | tf_op jit(solution)/shard_map/all_to_all | solution.py:301
  17.4 0.0 copy-start.5
  17.4 0.1 shard_map.123
  17.5 0.0 collective-permute-done.1.refs_1_
  17.5 0.0 collective-permute-done.2.refs_2_
  17.5 0.0 collective-permute-done.3.refs_3_
  17.5 0.0 copy-start.6
  17.5 1.4 %shard_map.125 = (f32[128,512]{1,0:T(8,128)S(1)}, bf16[4,64,512]{2,1,0:T(8,128)(2,1)}) custom-call(bf16[1,256,512]{2,1,0:T(8,128)(2,1)S(1)} %get-tuple-element.30.keys_ref, bf16[1,256,512]{2,1,0:T(8,128)(2,1)S(1)} %get-tuple-element.31.values_ref, s32[128]{0:T(128)S(1)} %get-tuple-element.32.lengths_ref, ...), custom_call_target="tpu_custom_call" | custom-call | tf_op jit(solution)/shard_map/pallas_call | solution.py:325
  19.0 0.0 copy-start
  19.0 0.0 copy-start.1
  19.0 4.3 %all-to-all-start.1 = ((bf16[32,8,512]{2,1,0:T(8,128)(2,1)}), bf16[32,8,512]{2,1,0:T(8,128)(2,1)S(1)}, u32[]{:S(2)}, u32[]{:S(2)}) async-start(bf16[32,8,512]{2,1,0:T(8,128)(2,1)} %bitcast.5), calls=%async_computation.1 | async-start | bytes 524288 | tf_op jit(solution)/shard_map/all_to_all | solution.py:348
  23.3 0.0 copy-done.5
  23.3 0.0 copy-done.6
  23.3 0.0 copy-done
  23.3 0.4 shard_map.126
  23.8 1.8 %collective-permute-start.4 = (f32[8,128]{1,0:T(8,128)S(1)}, f32[8,128]{1,0:T(8,128)S(1)}, u32[]{:S(2)}, u32[]{:S(2)}) collective-permute-start(f32[8,128]{1,0:T(8,128)S(1)} %get-tuple-element.47), channel_id=1, source_target_pairs={{0,8},{8,16},{16,24},{24,0},{1,9},{9,17},{17,25},{25,1},{2,10},{10... | collective-permute-start | bytes 12296 | tf_op jit(solution)/shard_map/ppermute | solution.py:18
  25.6 2.4 %collective-permute-start.5 = (f32[8,128]{1,0:T(8,128)S(1)}, f32[8,128]{1,0:T(8,128)S(1)}, u32[]{:S(2)}, u32[]{:S(2)}) collective-permute-start(f32[8,128]{1,0:T(8,128)S(1)} %get-tuple-element.48), channel_id=1, source_target_pairs={{0,16},{8,24},{16,0},{24,8},{1,17},{9,25},{17,1},{25,9},{2,18},{10... | collective-permute-start | bytes 12296 | tf_op jit(solution)/shard_map/ppermute | solution.py:18
  28.0 1.4 %collective-permute-start.6 = (f32[8,128]{1,0:T(8,128)S(1)}, f32[8,128]{1,0:T(8,128)S(1)}, u32[]{:S(2)}, u32[]{:S(2)}) collective-permute-start(f32[8,128]{1,0:T(8,128)S(1)} %get-tuple-element.49), channel_id=1, source_target_pairs={{0,24},{8,0},{16,8},{24,16},{1,25},{9,1},{17,9},{25,17},{2,26},{10... | collective-permute-start | bytes 12296 | tf_op jit(solution)/shard_map/ppermute | solution.py:18
  29.4 3.0 %collective-permute-done.4.refs_1_ = f32[8,128]{1,0:T(8,128)S(1)} collective-permute-done((f32[8,128]{1,0:T(8,128)S(1)}, f32[8,128]{1,0:T(8,128)S(1)}, u32[]{:S(2)}, u32[]{:S(2)}) %collective-permute-start.4) | collective-permute-done | bytes 4128 | tf_op jit(solution)/shard_map/ppermute | solution.py:18
  32.4 0.6 %collective-permute-done.5.refs_2_ = f32[8,128]{1,0:T(8,128)S(1)} collective-permute-done((f32[8,128]{1,0:T(8,128)S(1)}, f32[8,128]{1,0:T(8,128)S(1)}, u32[]{:S(2)}, u32[]{:S(2)}) %collective-permute-start.5) | collective-permute-done | bytes 4128 | tf_op jit(solution)/shard_map/ppermute | solution.py:18
  33.0 0.0 collective-permute-done.6.refs_3_
  33.0 1.0 %all-to-all-done.1 = bf16[32,8,512]{2,1,0:T(8,128)(2,1)S(1)} async-done(((bf16[32,8,512]{2,1,0:T(8,128)(2,1)}), bf16[32,8,512]{2,1,0:T(8,128)(2,1)S(1)}, u32[]{:S(2)}, u32[]{:S(2)}) %all-to-all-start.1) | async-done | bytes 262176 | tf_op jit(solution)/shard_map/all_to_all | solution.py:348
  34.0 0.0 copy-done.1
  34.0 0.0 copy-done.2
  34.0 1.2 %shard_map.127 = bf16[256,512]{1,0:T(8,128)(2,1)} custom-call(bf16[256,512]{1,0:T(8,128)(2,1)S(1)} %bitcast.15, bf16[320,512]{1,0:T(8,128)(2,1)S(1)} %bitcast.18, bf16[320,512]{1,0:T(8,128)(2,1)S(1)} %bitcast.19), custom_call_target="tpu_custom_call" | custom-call | flops 167772160 | bytes 1048576 | tf_op jit(solution)/shard_map/pallas_call | solution.py:351
  35.3 0.0 copy-start.3
  35.3 0.0 copy-start.4
  35.3 3.0 %all-to-all-start.2 = ((bf16[32,8,512]{2,1,0:T(8,128)(2,1)}), bf16[32,8,512]{2,1,0:T(8,128)(2,1)S(1)}, u32[]{:S(2)}, u32[]{:S(2)}) async-start(bf16[32,8,512]{2,1,0:T(8,128)(2,1)} %bitcast.11), calls=%async_computation.2 | async-start | bytes 524288 | tf_op jit(solution)/shard_map/all_to_all | solution.py:369
  38.3 0.0 copy-done.3
  38.3 0.0 copy-done.4
  38.3 0.2 shard_map.129
  38.5 0.3 collective-permute-start.7
  38.8 0.9 %collective-permute-done.7 = f32[8,512]{1,0:T(8,128)S(1)} collective-permute-done((f32[8,512]{1,0:T(8,128)S(1)}, f32[8,512]{1,0:T(8,128)S(1)}, u32[]{:S(2)}, u32[]{:S(2)}) %collective-permute-start.7) | collective-permute-done | bytes 16416 | tf_op jit(solution)/shard_map/ppermute | solution.py:23
  39.7 1.8 %collective-permute-start.8 = (f32[8,512]{1,0:T(8,128)S(1)}, f32[8,512]{1,0:T(8,128)S(1)}, u32[]{:S(2)}, u32[]{:S(2)}) collective-permute-start(f32[8,512]{1,0:T(8,128)S(1)} %add.9), channel_id=1, source_target_pairs={{0,2},{1,3},{2,0},{3,1},{4,6},{5,7},{6,4},{7,5},{8,10},{9,11},{10,... | collective-permute-start | bytes 49160 | tf_op jit(solution)/shard_map/ppermute | solution.py:23
  41.5 2.3 %collective-permute-done.8 = f32[8,512]{1,0:T(8,128)S(1)} collective-permute-done((f32[8,512]{1,0:T(8,128)S(1)}, f32[8,512]{1,0:T(8,128)S(1)}, u32[]{:S(2)}, u32[]{:S(2)}) %collective-permute-start.8) | collective-permute-done | bytes 16416 | tf_op jit(solution)/shard_map/ppermute | solution.py:23
  43.8 1.6 %collective-permute-start.9 = (f32[8,512]{1,0:T(8,128)S(1)}, f32[8,512]{1,0:T(8,128)S(1)}, u32[]{:S(2)}, u32[]{:S(2)}) collective-permute-start(f32[8,512]{1,0:T(8,128)S(1)} %add.10), channel_id=1, source_target_pairs={{0,4},{1,5},{2,6},{3,7},{4,0},{5,1},{6,2},{7,3},{8,12},{9,13},{10,... | collective-permute-start | bytes 49160 | tf_op jit(solution)/shard_map/ppermute | solution.py:23
  45.4 2.4 %collective-permute-done.9 = f32[8,512]{1,0:T(8,128)S(1)} collective-permute-done((f32[8,512]{1,0:T(8,128)S(1)}, f32[8,512]{1,0:T(8,128)S(1)}, u32[]{:S(2)}, u32[]{:S(2)}) %collective-permute-start.9) | collective-permute-done | bytes 16416 | tf_op jit(solution)/shard_map/ppermute | solution.py:23
  47.7 0.6 %add_convert_fusion = bf16[8,512]{1,0:T(8,128)(2,1)} fusion(f32[8,512]{1,0:T(8,128)S(1)} %add.10, f32[8,512]{1,0:T(8,128)S(1)} %collective-permute-done.9), kind=kLoop, calls=%fused_computation | loop fusion | flops 8192 | bytes 40960 | tf_op jit(solution)/shard_map/convert_element_type | solution.py:385
  48.3 0.5 %all-to-all-done.2 = bf16[32,8,512]{2,1,0:T(8,128)(2,1)S(1)} async-done(((bf16[32,8,512]{2,1,0:T(8,128)(2,1)}), bf16[32,8,512]{2,1,0:T(8,128)(2,1)S(1)}, u32[]{:S(2)}, u32[]{:S(2)}) %all-to-all-start.2) | async-done | bytes 262176 | tf_op jit(solution)/shard_map/all_to_all | solution.py:369
  48.9 0.9 %shard_map.128 = bf16[128,512]{1,0:T(8,128)(2,1)} custom-call(bf16[4,64,512]{2,1,0:T(8,128)(2,1)S(1)} %bitcast.14, s32[1,128]{1,0:T(1,128)S(1)} %get-tuple-element.38.target_ref, f32[128,512]{1,0:T(8,128)S(1)} %get-tuple-element.51.hidden_ref), custom_call_target="tpu_custom_call" | custom-call | tf_op jit(solution)/shard_map/pallas_call | solution.py:376
  (3 shorter events, 0.0 us)
Async XLA Ops:
  2.5 7.5 %collective-permute-start = (bf16[4,64,128]{2,1,0:T(8,128)(2,1)S(1)}, bf16[4,64,128]{2,1,0:T(8,128)(2,1)S(1)}, u32[]{:S(2)}, u32[]{:S(2)}) collective-permute-start(bf16[4,64,128]{2,1,0:T(8,128)(2,1)S(1)} %get-tuple-element.36), channel_id=1, source_target_pairs={{0,1},{1,0},{2,3},{3,2},{4,5},{5,4},{6,7},{7,6},{8,9},{9,8},{10,11... | collective-permute-start | bytes 196616 | tf_op jit(solution)/shard_map/ppermute | solution.py:23
  3.0 14.4 %all-to-all-start = ((bf16[32,8,128]{2,1,0:T(8,128)(2,1)}), bf16[32,8,128]{2,1,0:T(8,128)(2,1)S(1)}, u32[]{:S(2)}, u32[]{:S(2)}) async-start(bf16[32,8,128]{2,1,0:T(8,128)(2,1)} %get-tuple-element.29), calls=%async_computation | async-start | bytes 131072 | tf_op jit(solution)/shard_map/all_to_all | solution.py:301
  10.1 7.4 %collective-permute-start.1 = (bf16[128,128]{1,0:T(8,128)(2,1)S(1)}, bf16[128,128]{1,0:T(8,128)(2,1)S(1)}, u32[]{:S(2)}, u32[]{:S(2)}) collective-permute-start(bf16[128,128]{1,0:T(8,128)(2,1)S(1)} %get-tuple-element.40), channel_id=1, source_target_pairs={{0,6},{1,7},{2,4},{3,5},{4,2},{5,3},{6,0},{7,1},{8,14},{9,15},{10,... | collective-permute-start | bytes 98312 | tf_op jit(solution)/shard_map/ppermute | solution.py:23
  12.8 4.7 %collective-permute-start.2 = (bf16[128,128]{1,0:T(8,128)(2,1)S(1)}, bf16[128,128]{1,0:T(8,128)(2,1)S(1)}, u32[]{:S(2)}, u32[]{:S(2)}) collective-permute-start(bf16[128,128]{1,0:T(8,128)(2,1)S(1)} %get-tuple-element.41), channel_id=1, source_target_pairs={{0,4},{1,5},{2,6},{3,7},{4,0},{5,1},{6,2},{7,3},{8,12},{9,13},{10,... | collective-permute-start | bytes 98312 | tf_op jit(solution)/shard_map/ppermute | solution.py:23
  13.3 4.2 %collective-permute-start.3 = (bf16[128,128]{1,0:T(8,128)(2,1)S(1)}, bf16[128,128]{1,0:T(8,128)(2,1)S(1)}, u32[]{:S(2)}, u32[]{:S(2)}) collective-permute-start(bf16[128,128]{1,0:T(8,128)(2,1)S(1)} %get-tuple-element.42), channel_id=1, source_target_pairs={{0,2},{1,3},{2,0},{3,1},{4,6},{5,7},{6,4},{7,5},{8,10},{9,11},{10,... | collective-permute-start | bytes 98312 | tf_op jit(solution)/shard_map/ppermute | solution.py:23
  17.4 6.0 %copy-start.5 = (bf16[1024,64]{0,1:T(8,128)(2,1)S(1)}, bf16[1024,64]{0,1:T(8,128)(2,1)}, u32[]{:S(2)}) copy-start(bf16[1024,64]{0,1:T(8,128)(2,1)} %param.16) | copy-start | bytes 393220
  17.5 5.8 %copy-start.6 = (s32[1024]{0:T(1024)S(1)}, s32[1024]{0:T(1024)}, u32[]{:S(2)}) copy-start(s32[1024]{0:T(1024)} %lengths_ref.1) | copy-start | bytes 12292
  19.0 4.4 %copy-start = (bf16[1024,64]{0,1:T(8,128)(2,1)S(1)}, bf16[1024,64]{0,1:T(8,128)(2,1)}, u32[]{:S(2)}) copy-start(bf16[1024,64]{0,1:T(8,128)(2,1)} %param.14) | copy-start | bytes 393220
  19.0 15.1 %copy-start.1 = (bf16[1,512,320]{1,2,0:T(8,128)(2,1)S(1)}, bf16[1,512,320]{1,2,0:T(8,128)(2,1)}, u32[]{:S(2)}) copy-start(bf16[1,512,320]{1,2,0:T(8,128)(2,1)} %param.20) | copy-start | bytes 983044
  19.0 15.1 %copy-start.2 = (bf16[1,320,512]{2,1,0:T(8,128)(2,1)S(1)}, bf16[1,320,512]{2,1,0:T(8,128)(2,1)}, u32[]{:S(2)}) copy-start(bf16[1,320,512]{2,1,0:T(8,128)(2,1)} %param.21) | copy-start | bytes 983044
  19.0 15.1 %all-to-all-start.1 = ((bf16[32,8,512]{2,1,0:T(8,128)(2,1)}), bf16[32,8,512]{2,1,0:T(8,128)(2,1)S(1)}, u32[]{:S(2)}, u32[]{:S(2)}) async-start(bf16[32,8,512]{2,1,0:T(8,128)(2,1)} %bitcast.5), calls=%async_computation.1 | async-start | bytes 524288 | tf_op jit(solution)/shard_map/all_to_all | solution.py:348
  23.8 8.7 %collective-permute-start.4 = (f32[8,128]{1,0:T(8,128)S(1)}, f32[8,128]{1,0:T(8,128)S(1)}, u32[]{:S(2)}, u32[]{:S(2)}) collective-permute-start(f32[8,128]{1,0:T(8,128)S(1)} %get-tuple-element.47), channel_id=1, source_target_pairs={{0,8},{8,16},{16,24},{24,0},{1,9},{9,17},{17,25},{25,1},{2,10},{10... | collective-permute-start | bytes 12296 | tf_op jit(solution)/shard_map/ppermute | solution.py:18
  25.6 7.4 %collective-permute-start.5 = (f32[8,128]{1,0:T(8,128)S(1)}, f32[8,128]{1,0:T(8,128)S(1)}, u32[]{:S(2)}, u32[]{:S(2)}) collective-permute-start(f32[8,128]{1,0:T(8,128)S(1)} %get-tuple-element.48), channel_id=1, source_target_pairs={{0,16},{8,24},{16,0},{24,8},{1,17},{9,25},{17,1},{25,9},{2,18},{10... | collective-permute-start | bytes 12296 | tf_op jit(solution)/shard_map/ppermute | solution.py:18
  28.0 5.0 %collective-permute-start.6 = (f32[8,128]{1,0:T(8,128)S(1)}, f32[8,128]{1,0:T(8,128)S(1)}, u32[]{:S(2)}, u32[]{:S(2)}) collective-permute-start(f32[8,128]{1,0:T(8,128)S(1)} %get-tuple-element.49), channel_id=1, source_target_pairs={{0,24},{8,0},{16,8},{24,16},{1,25},{9,1},{17,9},{25,17},{2,26},{10... | collective-permute-start | bytes 12296 | tf_op jit(solution)/shard_map/ppermute | solution.py:18
  35.3 3.0 %copy-start.3 = (bf16[512,64]{0,1:T(8,128)(2,1)S(1)}, bf16[512,64]{0,1:T(8,128)(2,1)}, u32[]{:S(2)}) copy-start(bf16[512,64]{0,1:T(8,128)(2,1)} %param.12) | copy-start | bytes 196612
  35.3 3.0 %copy-start.4 = (bf16[512,64]{0,1:T(8,128)(2,1)S(1)}, bf16[512,64]{0,1:T(8,128)(2,1)}, u32[]{:S(2)}) copy-start(bf16[512,64]{0,1:T(8,128)(2,1)} %param.13) | copy-start | bytes 196612
  35.3 13.6 %all-to-all-start.2 = ((bf16[32,8,512]{2,1,0:T(8,128)(2,1)}), bf16[32,8,512]{2,1,0:T(8,128)(2,1)S(1)}, u32[]{:S(2)}, u32[]{:S(2)}) async-start(bf16[32,8,512]{2,1,0:T(8,128)(2,1)} %bitcast.11), calls=%async_computation.2 | async-start | bytes 524288 | tf_op jit(solution)/shard_map/all_to_all | solution.py:369
  38.5 1.2 %collective-permute-start.7 = (f32[8,512]{1,0:T(8,128)S(1)}, f32[8,512]{1,0:T(8,128)S(1)}, u32[]{:S(2)}, u32[]{:S(2)}) collective-permute-start(f32[8,512]{1,0:T(8,128)S(1)} %shard_map.129), channel_id=1, source_target_pairs={{0,1},{1,0},{2,3},{3,2},{4,5},{5,4},{6,7},{7,6},{8,9},{9,8},{10,11... | collective-permute-start | bytes 49160 | tf_op jit(solution)/shard_map/ppermute | solution.py:23
  39.7 4.1 %collective-permute-start.8 = (f32[8,512]{1,0:T(8,128)S(1)}, f32[8,512]{1,0:T(8,128)S(1)}, u32[]{:S(2)}, u32[]{:S(2)}) collective-permute-start(f32[8,512]{1,0:T(8,128)S(1)} %add.9), channel_id=1, source_target_pairs={{0,2},{1,3},{2,0},{3,1},{4,6},{5,7},{6,4},{7,5},{8,10},{9,11},{10,... | collective-permute-start | bytes 49160 | tf_op jit(solution)/shard_map/ppermute | solution.py:23
  43.8 4.0 %collective-permute-start.9 = (f32[8,512]{1,0:T(8,128)S(1)}, f32[8,512]{1,0:T(8,128)S(1)}, u32[]{:S(2)}, u32[]{:S(2)}) collective-permute-start(f32[8,512]{1,0:T(8,128)S(1)} %add.10), channel_id=1, source_target_pairs={{0,4},{1,5},{2,6},{3,7},{4,0},{5,1},{6,2},{7,3},{8,12},{9,13},{10,... | collective-permute-start | bytes 49160 | tf_op jit(solution)/shard_map/ppermute | solution.py:23

commit v6 on v4

--- a/solution.py
+++ b/solution.py
@@ -117,7 +117,7 @@
     pipes, tok_dev = rows // (group * enc_dev), q_ref.shape[1]
     f32, bf16 = jnp.float32, jnp.bfloat16
     here = lax.axis_index("expert")
-    for k, ref in zip((0, *range(len(query_refs) - 1, 0, -1)), query_refs, strict=True):
+    for k, ref in zip((0, len(query_refs) - 1, *range(1, len(query_refs) - 1)), query_refs, strict=True):
         for i in range(2):
             which = pl.multiple_of(lax.bitwise_xor(here, 2 * k + i) * head, head)
             q_ref[pl.ds(which, head)] = ref[i * head : (i + 1) * head]
@@ -328,7 +328,7 @@
         out_specs=[VMEM] * 2,
         scratch_shapes=[pltpu.VMEM((model, tok_dev), bf16)],
         compiler_params=params,
-    )(key_blocks, value_blocks, own_lengths, near_residual, gain, target, query_blocks[0], *query_blocks[:0:-1])
+    )(key_blocks, value_blocks, own_lengths, near_residual, gain, target, query_blocks[0], query_blocks[-1], *query_blocks[1:-1])
     outgoing = outgoing.reshape(pipes * experts, cap, model)
     kv, outgoing = lax.optimization_barrier((kv, outgoing))
     total, *others = pl.pallas_call(

time: 50.1 us -> 50.1 us (level)
  no operation moved by 1% of the time
where the time goes in v6:
time: 50.1 us; the launch traced here: 49.7 us
  starting transfers between devices  27.6 us (55%)
  waiting for transfers between devices  14.6 us (29%)
  Pallas kernels  6.1 us (12%)
  between operations  0.8 us (2%)
  other arithmetic  0.61 us (1%)
    ppermute x7, starting transfers between devices, crossed(): return lax.ppermute(value, 'expert', [(i, i ^ bit) for i in range(size)])  7.7 us
    all_to_all x1, starting transfers between devices, per_device(): lax.all_to_all(spread_kv, EVERYONE, split_axis=0, concat_axis=0, tiled=True)  6.96 us
    ppermute x3, starting transfers between devices, shifted(): lax.ppermute(value, axis, [(i, (i + step) % size) for i in range(size)])  5.66 us
    ppermute x7, waiting for transfers between devices, crossed(): return lax.ppermute(value, 'expert', [(i, i ^ bit) for i in range(size)])  5.61 us
    all_to_all x1, starting transfers between devices, per_device(): lax.all_to_all(outgoing, EVERYONE, split_axis=0, concat_axis=0, tiled=True)  4.28 us
    all_to_all x1, waiting for transfers between devices, per_device(): lax.all_to_all(spread_kv, EVERYONE, split_axis=0, concat_axis=0, tiled=True)  3.81 us
    ppermute x3, waiting for transfers between devices, shifted(): lax.ppermute(value, axis, [(i, (i + step) % size) for i in range(size)])  3.6 us
    all_to_all x1, starting transfers between devices, per_device(): lax.all_to_all(part.reshape(pipes * experts, cap, model), EVERYONE, split...  2.99 us
  transfers between devices with their start and end apart: 13, of which 8 were waited for; matrix products, arithmetic and copies ran while one was open for 1% of the time, Pallas kernels for 2%

profile of v6, /device:TPU:0, one launch (start us, length us, event | category | flops | bytes accessed | tf_op | source)
XLA Modules:
  0.0 49.7 jit_solution(13870258129066416064)
XLA Ops:
  0.6 1.8 %shard_map.122 = (bf16[32,8,128]{2,1,0:T(8,128)(2,1)}, bf16[4,64,128]{2,1,0:T(8,128)(2,1)S(1)}, bf16[4,64,128]{2,1,0:T(8,128)(2,1)S(1)}, s32[128]{0:T(128)S(1)},...) custom-call(bf16[8,512]{1,0:T(8,128)(2,1)} %enc_hbm.1, bf16[64,512]{1,0:T(8,128)(2,1)} %bitcast.20, ...), custom_call_target="tpu_custom_call" | custom-call | tf_op jit(solution)/shard_map/pallas_call | solution.py:259
  2.5 0.5 %collective-permute-start = (bf16[4,64,128]{2,1,0:T(8,128)(2,1)S(1)}, bf16[4,64,128]{2,1,0:T(8,128)(2,1)S(1)}, u32[]{:S(2)}, u32[]{:S(2)}) collective-permute-start(bf16[4,64,128]{2,1,0:T(8,128)(2,1)S(1)} %get-tuple-element.36), channel_id=1, source_target_pairs={{0,1},{1,0},{2,3},{3,2},{4,5},{5,4},{6,7},{7,6},{8,9},{9,8},{10,11... | collective-permute-start | bytes 196616 | tf_op jit(solution)/shard_map/ppermute | solution.py:23
  3.0 7.0 %all-to-all-start = ((bf16[32,8,128]{2,1,0:T(8,128)(2,1)}), bf16[32,8,128]{2,1,0:T(8,128)(2,1)S(1)}, u32[]{:S(2)}, u32[]{:S(2)}) async-start(bf16[32,8,128]{2,1,0:T(8,128)(2,1)} %get-tuple-element.28), calls=%async_computation | async-start | bytes 131072 | tf_op jit(solution)/shard_map/all_to_all | solution.py:298
  9.9 0.0 collective-permute-done.got_ref
  10.0 2.7 %collective-permute-start.1 = (bf16[128,128]{1,0:T(8,128)(2,1)S(1)}, bf16[128,128]{1,0:T(8,128)(2,1)S(1)}, u32[]{:S(2)}, u32[]{:S(2)}) collective-permute-start(bf16[128,128]{1,0:T(8,128)(2,1)S(1)} %get-tuple-element.38), channel_id=1, source_target_pairs={{0,6},{1,7},{2,4},{3,5},{4,2},{5,3},{6,0},{7,1},{8,14},{9,15},{10,... | collective-permute-start | bytes 98312 | tf_op jit(solution)/shard_map/ppermute | solution.py:23
  12.7 0.6 %collective-permute-start.2 = (bf16[128,128]{1,0:T(8,128)(2,1)S(1)}, bf16[128,128]{1,0:T(8,128)(2,1)S(1)}, u32[]{:S(2)}, u32[]{:S(2)}) collective-permute-start(bf16[128,128]{1,0:T(8,128)(2,1)S(1)} %get-tuple-element.39), channel_id=1, source_target_pairs={{0,2},{1,3},{2,0},{3,1},{4,6},{5,7},{6,4},{7,5},{8,10},{9,11},{10,... | collective-permute-start | bytes 98312 | tf_op jit(solution)/shard_map/ppermute | solution.py:23
  13.3 0.3 collective-permute-start.3
  13.5 3.8 %all-to-all-done = bf16[32,8,128]{2,1,0:T(8,128)(2,1)S(1)} async-done(((bf16[32,8,128]{2,1,0:T(8,128)(2,1)}), bf16[32,8,128]{2,1,0:T(8,128)(2,1)S(1)}, u32[]{:S(2)}, u32[]{:S(2)}) %all-to-all-start) | async-done | bytes 65568 | tf_op jit(solution)/shard_map/all_to_all | solution.py:298
  17.4 0.0 copy-start.5
  17.4 0.1 shard_map.123
  17.5 0.0 collective-permute-done.1.refs_1_
  17.5 0.0 collective-permute-done.2.refs_2_
  17.5 0.0 collective-permute-done.3.refs_3_
  17.5 0.0 copy-start.6
  17.5 1.4 %shard_map.125 = (f32[128,512]{1,0:T(8,128)S(1)}, bf16[4,64,512]{2,1,0:T(8,128)(2,1)}) custom-call(bf16[1,256,512]{2,1,0:T(8,128)(2,1)S(1)} %get-tuple-element.29.keys_ref, bf16[1,256,512]{2,1,0:T(8,128)(2,1)S(1)} %get-tuple-element.30.values_ref, s32[128]{0:T(128)S(1)} %get-tuple-element.31.lengths_ref, ...), custom_call_target="tpu_custom_call" | custom-call | tf_op jit(solution)/shard_map/pallas_call | solution.py:321
  19.0 0.0 copy-start
  19.0 0.0 copy-start.1
  19.0 0.0 copy-start.2
  19.0 4.3 %all-to-all-start.1 = ((bf16[32,8,512]{2,1,0:T(8,128)(2,1)}), bf16[32,8,512]{2,1,0:T(8,128)(2,1)S(1)}, u32[]{:S(2)}, u32[]{:S(2)}) async-start(bf16[32,8,512]{2,1,0:T(8,128)(2,1)} %bitcast.5), calls=%async_computation.1 | async-start | bytes 524288 | tf_op jit(solution)/shard_map/all_to_all | solution.py:344
  23.3 0.0 copy-done.5
  23.3 0.0 copy-done.6
  23.3 0.0 copy-done
  23.3 0.4 shard_map.126
  23.7 1.8 %collective-permute-start.4 = (f32[8,128]{1,0:T(8,128)S(1)}, f32[8,128]{1,0:T(8,128)S(1)}, u32[]{:S(2)}, u32[]{:S(2)}) collective-permute-start(f32[8,128]{1,0:T(8,128)S(1)} %get-tuple-element.45), channel_id=1, source_target_pairs={{0,8},{8,16},{16,24},{24,0},{1,9},{9,17},{17,25},{25,1},{2,10},{10... | collective-permute-start | bytes 12296 | tf_op jit(solution)/shard_map/ppermute | solution.py:18
  25.5 2.4 %collective-permute-start.5 = (f32[8,128]{1,0:T(8,128)S(1)}, f32[8,128]{1,0:T(8,128)S(1)}, u32[]{:S(2)}, u32[]{:S(2)}) collective-permute-start(f32[8,128]{1,0:T(8,128)S(1)} %get-tuple-element.46), channel_id=1, source_target_pairs={{0,16},{8,24},{16,0},{24,8},{1,17},{9,25},{17,1},{25,9},{2,18},{10... | collective-permute-start | bytes 12296 | tf_op jit(solution)/shard_map/ppermute | solution.py:18
  27.9 1.4 %collective-permute-start.6 = (f32[8,128]{1,0:T(8,128)S(1)}, f32[8,128]{1,0:T(8,128)S(1)}, u32[]{:S(2)}, u32[]{:S(2)}) collective-permute-start(f32[8,128]{1,0:T(8,128)S(1)} %get-tuple-element.47), channel_id=1, source_target_pairs={{0,24},{8,0},{16,8},{24,16},{1,25},{9,1},{17,9},{25,17},{2,26},{10... | collective-permute-start | bytes 12296 | tf_op jit(solution)/shard_map/ppermute | solution.py:18
  29.4 3.0 %collective-permute-done.4.refs_1_ = f32[8,128]{1,0:T(8,128)S(1)} collective-permute-done((f32[8,128]{1,0:T(8,128)S(1)}, f32[8,128]{1,0:T(8,128)S(1)}, u32[]{:S(2)}, u32[]{:S(2)}) %collective-permute-start.4) | collective-permute-done | bytes 4128 | tf_op jit(solution)/shard_map/ppermute | solution.py:18
  32.4 0.6 %collective-permute-done.5.refs_2_ = f32[8,128]{1,0:T(8,128)S(1)} collective-permute-done((f32[8,128]{1,0:T(8,128)S(1)}, f32[8,128]{1,0:T(8,128)S(1)}, u32[]{:S(2)}, u32[]{:S(2)}) %collective-permute-start.5) | collective-permute-done | bytes 4128 | tf_op jit(solution)/shard_map/ppermute | solution.py:18
  33.0 0.0 collective-permute-done.6.refs_3_
  33.0 1.0 %all-to-all-done.1 = bf16[32,8,512]{2,1,0:T(8,128)(2,1)S(1)} async-done(((bf16[32,8,512]{2,1,0:T(8,128)(2,1)}), bf16[32,8,512]{2,1,0:T(8,128)(2,1)S(1)}, u32[]{:S(2)}, u32[]{:S(2)}) %all-to-all-start.1) | async-done | bytes 262176 | tf_op jit(solution)/shard_map/all_to_all | solution.py:344
  34.0 0.0 copy-done.1
  34.0 0.0 copy-done.2
  34.0 1.2 %shard_map.127 = bf16[256,512]{1,0:T(8,128)(2,1)} custom-call(bf16[256,512]{1,0:T(8,128)(2,1)S(1)} %bitcast.15, bf16[320,512]{1,0:T(8,128)(2,1)S(1)} %bitcast.18, bf16[320,512]{1,0:T(8,128)(2,1)S(1)} %bitcast.19), custom_call_target="tpu_custom_call" | custom-call | flops 167772160 | bytes 1048576 | tf_op jit(solution)/shard_map/pallas_call | solution.py:347
  35.2 0.0 copy-start.3
  35.2 0.0 copy-start.4
  35.2 3.0 %all-to-all-start.2 = ((bf16[32,8,512]{2,1,0:T(8,128)(2,1)}), bf16[32,8,512]{2,1,0:T(8,128)(2,1)S(1)}, u32[]{:S(2)}, u32[]{:S(2)}) async-start(bf16[32,8,512]{2,1,0:T(8,128)(2,1)} %bitcast.11), calls=%async_computation.2 | async-start | bytes 524288 | tf_op jit(solution)/shard_map/all_to_all | solution.py:365
  38.2 0.0 copy-done.3
  38.2 0.0 copy-done.4
  38.3 0.2 shard_map.129
  38.5 0.3 collective-permute-start.7
  38.7 0.9 %collective-permute-done.7 = f32[8,512]{1,0:T(8,128)S(1)} collective-permute-done((f32[8,512]{1,0:T(8,128)S(1)}, f32[8,512]{1,0:T(8,128)S(1)}, u32[]{:S(2)}, u32[]{:S(2)}) %collective-permute-start.7) | collective-permute-done | bytes 16416 | tf_op jit(solution)/shard_map/ppermute | solution.py:23
  39.6 1.8 %collective-permute-start.8 = (f32[8,512]{1,0:T(8,128)S(1)}, f32[8,512]{1,0:T(8,128)S(1)}, u32[]{:S(2)}, u32[]{:S(2)}) collective-permute-start(f32[8,512]{1,0:T(8,128)S(1)} %add.9), channel_id=1, source_target_pairs={{0,2},{1,3},{2,0},{3,1},{4,6},{5,7},{6,4},{7,5},{8,10},{9,11},{10,... | collective-permute-start | bytes 49160 | tf_op jit(solution)/shard_map/ppermute | solution.py:23
  41.4 2.3 %collective-permute-done.8 = f32[8,512]{1,0:T(8,128)S(1)} collective-permute-done((f32[8,512]{1,0:T(8,128)S(1)}, f32[8,512]{1,0:T(8,128)S(1)}, u32[]{:S(2)}, u32[]{:S(2)}) %collective-permute-start.8) | collective-permute-done | bytes 16416 | tf_op jit(solution)/shard_map/ppermute | solution.py:23
  43.7 1.6 %collective-permute-start.9 = (f32[8,512]{1,0:T(8,128)S(1)}, f32[8,512]{1,0:T(8,128)S(1)}, u32[]{:S(2)}, u32[]{:S(2)}) collective-permute-start(f32[8,512]{1,0:T(8,128)S(1)} %add.10), channel_id=1, source_target_pairs={{0,4},{1,5},{2,6},{3,7},{4,0},{5,1},{6,2},{7,3},{8,12},{9,13},{10,... | collective-permute-start | bytes 49160 | tf_op jit(solution)/shard_map/ppermute | solution.py:23
  45.3 2.4 %collective-permute-done.9 = f32[8,512]{1,0:T(8,128)S(1)} collective-permute-done((f32[8,512]{1,0:T(8,128)S(1)}, f32[8,512]{1,0:T(8,128)S(1)}, u32[]{:S(2)}, u32[]{:S(2)}) %collective-permute-start.9) | collective-permute-done | bytes 16416 | tf_op jit(solution)/shard_map/ppermute | solution.py:23
  47.7 0.6 %add_convert_fusion = bf16[8,512]{1,0:T(8,128)(2,1)} fusion(f32[8,512]{1,0:T(8,128)S(1)} %add.10, f32[8,512]{1,0:T(8,128)S(1)} %collective-permute-done.9), kind=kLoop, calls=%fused_computation | loop fusion | flops 8192 | bytes 40960 | tf_op jit(solution)/shard_map/convert_element_type | solution.py:381
  48.3 0.5 %all-to-all-done.2 = bf16[32,8,512]{2,1,0:T(8,128)(2,1)S(1)} async-done(((bf16[32,8,512]{2,1,0:T(8,128)(2,1)}), bf16[32,8,512]{2,1,0:T(8,128)(2,1)S(1)}, u32[]{:S(2)}, u32[]{:S(2)}) %all-to-all-start.2) | async-done | bytes 262176 | tf_op jit(solution)/shard_map/all_to_all | solution.py:365
  48.8 0.9 %shard_map.128 = bf16[128,512]{1,0:T(8,128)(2,1)} custom-call(bf16[4,64,512]{2,1,0:T(8,128)(2,1)S(1)} %bitcast.14, s32[1,128]{1,0:T(1,128)S(1)} %get-tuple-element.34.target_ref, f32[128,512]{1,0:T(8,128)S(1)} %get-tuple-element.49.hidden_ref), custom_call_target="tpu_custom_call" | custom-call | tf_op jit(solution)/shard_map/pallas_call | solution.py:372
  (3 shorter events, 0.0 us)
Async XLA Ops:
  2.5 7.5 %collective-permute-start = (bf16[4,64,128]{2,1,0:T(8,128)(2,1)S(1)}, bf16[4,64,128]{2,1,0:T(8,128)(2,1)S(1)}, u32[]{:S(2)}, u32[]{:S(2)}) collective-permute-start(bf16[4,64,128]{2,1,0:T(8,128)(2,1)S(1)} %get-tuple-element.36), channel_id=1, source_target_pairs={{0,1},{1,0},{2,3},{3,2},{4,5},{5,4},{6,7},{7,6},{8,9},{9,8},{10,11... | collective-permute-start | bytes 196616 | tf_op jit(solution)/shard_map/ppermute | solution.py:23
  3.0 14.4 %all-to-all-start = ((bf16[32,8,128]{2,1,0:T(8,128)(2,1)}), bf16[32,8,128]{2,1,0:T(8,128)(2,1)S(1)}, u32[]{:S(2)}, u32[]{:S(2)}) async-start(bf16[32,8,128]{2,1,0:T(8,128)(2,1)} %get-tuple-element.28), calls=%async_computation | async-start | bytes 131072 | tf_op jit(solution)/shard_map/all_to_all | solution.py:298
  10.0 7.5 %collective-permute-start.1 = (bf16[128,128]{1,0:T(8,128)(2,1)S(1)}, bf16[128,128]{1,0:T(8,128)(2,1)S(1)}, u32[]{:S(2)}, u32[]{:S(2)}) collective-permute-start(bf16[128,128]{1,0:T(8,128)(2,1)S(1)} %get-tuple-element.38), channel_id=1, source_target_pairs={{0,6},{1,7},{2,4},{3,5},{4,2},{5,3},{6,0},{7,1},{8,14},{9,15},{10,... | collective-permute-start | bytes 98312 | tf_op jit(solution)/shard_map/ppermute | solution.py:23
  12.7 4.8 %collective-permute-start.2 = (bf16[128,128]{1,0:T(8,128)(2,1)S(1)}, bf16[128,128]{1,0:T(8,128)(2,1)S(1)}, u32[]{:S(2)}, u32[]{:S(2)}) collective-permute-start(bf16[128,128]{1,0:T(8,128)(2,1)S(1)} %get-tuple-element.39), channel_id=1, source_target_pairs={{0,2},{1,3},{2,0},{3,1},{4,6},{5,7},{6,4},{7,5},{8,10},{9,11},{10,... | collective-permute-start | bytes 98312 | tf_op jit(solution)/shard_map/ppermute | solution.py:23
  13.3 4.2 %collective-permute-start.3 = (bf16[128,128]{1,0:T(8,128)(2,1)S(1)}, bf16[128,128]{1,0:T(8,128)(2,1)S(1)}, u32[]{:S(2)}, u32[]{:S(2)}) collective-permute-start(bf16[128,128]{1,0:T(8,128)(2,1)S(1)} %get-tuple-element.40), channel_id=1, source_target_pairs={{0,4},{1,5},{2,6},{3,7},{4,0},{5,1},{6,2},{7,3},{8,12},{9,13},{10,... | collective-permute-start | bytes 98312 | tf_op jit(solution)/shard_map/ppermute | solution.py:23
  17.4 5.9 %copy-start.5 = (bf16[1024,64]{0,1:T(8,128)(2,1)S(1)}, bf16[1024,64]{0,1:T(8,128)(2,1)}, u32[]{:S(2)}) copy-start(bf16[1024,64]{0,1:T(8,128)(2,1)} %param.16) | copy-start | bytes 393220
  17.5 5.7 %copy-start.6 = (s32[1024]{0:T(1024)S(1)}, s32[1024]{0:T(1024)}, u32[]{:S(2)}) copy-start(s32[1024]{0:T(1024)} %lengths_ref.1) | copy-start | bytes 12292
  19.0 4.3 %copy-start = (bf16[1024,64]{0,1:T(8,128)(2,1)S(1)}, bf16[1024,64]{0,1:T(8,128)(2,1)}, u32[]{:S(2)}) copy-start(bf16[1024,64]{0,1:T(8,128)(2,1)} %param.14) | copy-start | bytes 393220
  19.0 15.0 %copy-start.1 = (bf16[1,512,320]{1,2,0:T(8,128)(2,1)S(1)}, bf16[1,512,320]{1,2,0:T(8,128)(2,1)}, u32[]{:S(2)}) copy-start(bf16[1,512,320]{1,2,0:T(8,128)(2,1)} %param.20) | copy-start | bytes 983044
  19.0 15.0 %copy-start.2 = (bf16[1,320,512]{2,1,0:T(8,128)(2,1)S(1)}, bf16[1,320,512]{2,1,0:T(8,128)(2,1)}, u32[]{:S(2)}) copy-start(bf16[1,320,512]{2,1,0:T(8,128)(2,1)} %param.21) | copy-start | bytes 983044
  19.0 15.0 %all-to-all-start.1 = ((bf16[32,8,512]{2,1,0:T(8,128)(2,1)}), bf16[32,8,512]{2,1,0:T(8,128)(2,1)S(1)}, u32[]{:S(2)}, u32[]{:S(2)}) async-start(bf16[32,8,512]{2,1,0:T(8,128)(2,1)} %bitcast.5), calls=%async_computation.1 | async-start | bytes 524288 | tf_op jit(solution)/shard_map/all_to_all | solution.py:344
  23.7 8.7 %collective-permute-start.4 = (f32[8,128]{1,0:T(8,128)S(1)}, f32[8,128]{1,0:T(8,128)S(1)}, u32[]{:S(2)}, u32[]{:S(2)}) collective-permute-start(f32[8,128]{1,0:T(8,128)S(1)} %get-tuple-element.45), channel_id=1, source_target_pairs={{0,8},{8,16},{16,24},{24,0},{1,9},{9,17},{17,25},{25,1},{2,10},{10... | collective-permute-start | bytes 12296 | tf_op jit(solution)/shard_map/ppermute | solution.py:18
  25.5 7.4 %collective-permute-start.5 = (f32[8,128]{1,0:T(8,128)S(1)}, f32[8,128]{1,0:T(8,128)S(1)}, u32[]{:S(2)}, u32[]{:S(2)}) collective-permute-start(f32[8,128]{1,0:T(8,128)S(1)} %get-tuple-element.46), channel_id=1, source_target_pairs={{0,16},{8,24},{16,0},{24,8},{1,17},{9,25},{17,1},{25,9},{2,18},{10... | collective-permute-start | bytes 12296 | tf_op jit(solution)/shard_map/ppermute | solution.py:18
  27.9 5.0 %collective-permute-start.6 = (f32[8,128]{1,0:T(8,128)S(1)}, f32[8,128]{1,0:T(8,128)S(1)}, u32[]{:S(2)}, u32[]{:S(2)}) collective-permute-start(f32[8,128]{1,0:T(8,128)S(1)} %get-tuple-element.47), channel_id=1, source_target_pairs={{0,24},{8,0},{16,8},{24,16},{1,25},{9,1},{17,9},{25,17},{2,26},{10... | collective-permute-start | bytes 12296 | tf_op jit(solution)/shard_map/ppermute | solution.py:18
  35.2 3.0 %copy-start.3 = (bf16[512,64]{0,1:T(8,128)(2,1)S(1)}, bf16[512,64]{0,1:T(8,128)(2,1)}, u32[]{:S(2)}) copy-start(bf16[512,64]{0,1:T(8,128)(2,1)} %param.12) | copy-start | bytes 196612
  35.2 3.0 %copy-start.4 = (bf16[512,64]{0,1:T(8,128)(2,1)S(1)}, bf16[512,64]{0,1:T(8,128)(2,1)}, u32[]{:S(2)}) copy-start(bf16[512,64]{0,1:T(8,128)(2,1)} %param.13) | copy-start | bytes 196612
  35.2 13.6 %all-to-all-start.2 = ((bf16[32,8,512]{2,1,0:T(8,128)(2,1)}), bf16[32,8,512]{2,1,0:T(8,128)(2,1)S(1)}, u32[]{:S(2)}, u32[]{:S(2)}) async-start(bf16[32,8,512]{2,1,0:T(8,128)(2,1)} %bitcast.11), calls=%async_computation.2 | async-start | bytes 524288 | tf_op jit(solution)/shard_map/all_to_all | solution.py:365
  38.5 1.2 %collective-permute-start.7 = (f32[8,512]{1,0:T(8,128)S(1)}, f32[8,512]{1,0:T(8,128)S(1)}, u32[]{:S(2)}, u32[]{:S(2)}) collective-permute-start(f32[8,512]{1,0:T(8,128)S(1)} %shard_map.129), channel_id=1, source_target_pairs={{0,1},{1,0},{2,3},{3,2},{4,5},{5,4},{6,7},{7,6},{8,9},{9,8},{10,11... | collective-permute-start | bytes 49160 | tf_op jit(solution)/shard_map/ppermute | solution.py:23
  39.6 4.1 %collective-permute-start.8 = (f32[8,512]{1,0:T(8,128)S(1)}, f32[8,512]{1,0:T(8,128)S(1)}, u32[]{:S(2)}, u32[]{:S(2)}) collective-permute-start(f32[8,512]{1,0:T(8,128)S(1)} %add.9), channel_id=1, source_target_pairs={{0,2},{1,3},{2,0},{3,1},{4,6},{5,7},{6,4},{7,5},{8,10},{9,11},{10,... | collective-permute-start | bytes 49160 | tf_op jit(solution)/shard_map/ppermute | solution.py:23
  43.7 4.0 %collective-permute-start.9 = (f32[8,512]{1,0:T(8,128)S(1)}, f32[8,512]{1,0:T(8,128)S(1)}, u32[]{:S(2)}, u32[]{:S(2)}) collective-permute-start(f32[8,512]{1,0:T(8,128)S(1)} %add.10), channel_id=1, source_target_pairs={{0,4},{1,5},{2,6},{3,7},{4,0},{5,1},{6,2},{7,3},{8,12},{9,13},{10,... | collective-permute-start | bytes 49160 | tf_op jit(solution)/shard_map/ppermute | solution.py:23
